TPU v7x, 32 devices: a whole 2x2x4 slice. The times are simulated.
32 devices in a mesh: space: 8 (over z, x), var: 4 (over y, core).
Axes of the slice: x: 2, y: 2, z: 4, core: 2. Of those that a mesh axis runs over, the one named last changes fastest.
Arguments:
- control: bfloat16 [8192, 1536], P('space', 'var'), may hold values from -6 to 6
- roots: bfloat16 [64, 5, 128, 128], P('space'), may hold values from -0.25 to 0.25
- neighbours: int32 [64, 5], P('space'), may hold values from 0 to 63, as said below
- sigma: float32 [96, 8192], P('var', 'space'), may hold values from 0.3 to 3
- obs_op: bfloat16 [96, 16], P('var'), may hold values from -0.625 to 0.625
- foot_cols: int32 [256, 16], P('space'), may hold values from 0 to 1023
- foot_wgt: float32 [256, 16], P('space'), may hold values from 0.05 to 0.2
- obs_value: float32 [256, 256], P('space'), may hold values from -6 to 6
- obs_rinv: float32 [256, 16], P('space'), may hold values from 0.5 to 4
- owner_counts: int32 [8, 8], P('space'), may hold values from 0 to 4, as said below
Outputs:
- gradient: bfloat16 [8192, 1536], P('space', 'var')
Inputs may be any that keep to these rules, and one draw needn't show every extreme that they name: `neighbours`: neighbour 0 of each block is the block itself; every neighbour lies within 8 blocks of it, and on every tile some block has a neighbour exactly 8 blocks away. `owner_counts`: in every draw one owner receives 4 footprints from every tile.
All inputs are finite; a program needn't handle non-finite values.
Results may differ from a plain program's by a relative error of at most 0.0034.
Values may be sent and summed in bfloat16 or wider, within the bound.
No kernel may reach another device: no remote copies, remote signals or barrier semaphores. Data moves between devices by JAX's collectives and lax.ppermute only.
A program may use at most 64 MiB of HBM per device.

v0:
```python
import jax
import jax.numpy as jnp
from jax import lax
from jax.sharding import PartitionSpec as P


def padded(block, sides, width):
    for axis, dim in sides:
        count = lax.axis_size(axis)
        forward = [(i, i + 1) for i in range(count - 1)]
        backward = [(target, source) for source, target in forward]
        low = lax.ppermute(
            lax.slice_in_dim(block, block.shape[dim] - width, None, axis=dim), axis, forward
        )
        high = lax.ppermute(lax.slice_in_dim(block, 0, width, axis=dim), axis, backward)
        block = jnp.concatenate([low, block, high], axis=dim)
    return block


def round_part(values):
    narrow = lax.optimization_barrier(values.astype(jnp.bfloat16))
    return narrow.astype(jnp.float32)


def shards(
    control,
    roots,
    neighbours,
    sigma,
    obs_op,
    foot_cols,
    foot_wgt,
    obs_value,
    obs_rinv,
    owner_counts,
):
    block_count = roots.shape[0]
    block_size = roots.shape[2]
    links = roots.shape[1]
    lane_width = control.shape[1]
    var_count = sigma.shape[0]
    members = lane_width // var_count
    band_count = obs_op.shape[1]
    band_width = band_count * members
    col_count = control.shape[0]
    slot_count = foot_cols.shape[0]
    identity_m = jnp.eye(members, dtype=jnp.bfloat16)
    op_wide = (obs_op[:, None, :, None] * identity_m[None, :, None, :]).reshape(
        lane_width, band_width
    )
    blocks = control.reshape(block_count, block_size, lane_width)
    extended = padded(blocks, (("space", 0),), block_count)
    tile_index = lax.axis_index("space")
    local_ids = neighbours - (tile_index - 1) * block_count
    summed = jnp.zeros((block_count, block_size, lane_width), jnp.float32)
    for link_index in range(links):
        picked = jnp.take(extended, local_ids[:, link_index], axis=0)
        summed = summed + jnp.einsum(
            "bij,bjn->bin", roots[:, link_index], picked, preferred_element_type=jnp.float32
        )
    sig_rep = jnp.repeat(sigma.T, members, axis=1)
    state_bf = (summed.reshape(col_count, lane_width) * sig_rep).astype(jnp.bfloat16)
    band_cols = jnp.dot(state_bf, op_wide, preferred_element_type=jnp.float32)
    picked_bands = jnp.take(band_cols, foot_cols, axis=0)
    partial_model = jnp.sum(foot_wgt[:, :, None] * picked_bands, axis=1)
    rinv_rep = jnp.repeat(obs_rinv, members, axis=1)
    modelled = lax.psum(partial_model, "var")
    arrived = lax.all_to_all(modelled, "space", split_axis=0, concat_axis=0, tiled=True)
    owner_misfit = rinv_rep * (arrived - obs_value)
    returned = lax.all_to_all(owner_misfit, "space", split_axis=0, concat_axis=0, tiled=True)
    capacity = slot_count // owner_counts.shape[1]
    slot_ids = jnp.arange(slot_count, dtype=jnp.int32)
    live_mask = slot_ids % capacity < jnp.repeat(owner_counts[0], capacity)
    misfit = jnp.where(live_mask[:, None], returned, 0.0)
    spread_terms = foot_wgt[:, :, None] * misfit[:, None, :]
    pulled = (
        jnp.zeros((col_count, band_width), jnp.float32)
        .at[foot_cols.reshape(-1)]
        .add(spread_terms.reshape(-1, band_width))
    )
    before = jnp.dot(
        pulled,
        op_wide.astype(jnp.float32).T,
        precision=lax.Precision.HIGHEST,
        preferred_element_type=jnp.float32,
    )
    adjoint_in = (
        (before * sig_rep).astype(jnp.bfloat16).reshape(block_count, block_size, lane_width)
    )
    roots_wide = padded(roots, (("space", 0),), block_count)
    lists_wide = padded(neighbours, (("space", 0),), block_count)
    inputs_wide = padded(adjoint_in, (("space", 0),), block_count)
    own_ids = lists_wide - tile_index * block_count
    sections = [
        jnp.zeros((block_count, block_size, lane_width), jnp.float32) for section in range(3)
    ]
    for link_index in range(links):
        terms = jnp.einsum(
            "bji,bjn->bin",
            roots_wide[:, link_index],
            inputs_wide,
            preferred_element_type=jnp.float32,
        )
        for section in range(3):
            lo_row = section * block_count
            targets = own_ids[lo_row : lo_row + block_count, link_index]
            inside = (targets >= 0) & (targets < block_count)
            chosen_terms = jnp.where(
                inside[:, None, None], terms[lo_row : lo_row + block_count], 0.0
            )
            sections[section] = (
                sections[section].at[jnp.clip(targets, 0, block_count - 1)].add(chosen_terms)
            )
    adjoint_sum = sections[1] + round_part(sections[0]) + round_part(sections[2])
    result = control.astype(jnp.float32) + adjoint_sum.reshape(col_count, lane_width)
    return result.astype(jnp.bfloat16)


def solution(mesh):
    return jax.shard_map(
        shards,
        mesh=mesh,
        in_specs=(
            P("space", "var"),
            P("space", None, None, None),
            P("space", None),
            P("var", "space"),
            P("var", None),
            P("space", None),
            P("space", None),
            P("space", None),
            P("space", None),
            P("space", None),
        ),
        out_specs=P("space", "var"),
        check_vma=False,
    )
```

profile of v0, /device:TPU:0, one launch (start us, length us, event | category | flops | bytes accessed | tf_op | source)
XLA Modules:
  0.0 227.0 jit_solution(17765449167630965813)
XLA Ops:
  0.0 5.9 %collective-permute-start.4 = (bf16[8,128,384]{2,1,0:T(8,128)(2,1)}, bf16[8,128,384]{2,1,0:T(8,128)(2,1)}, u32[]{:S(2)}, u32[]{:S(2)}) collective-permute-start(bf16[8,128,384]{2,1,0:T(8,128)(2,1)} %bitcast.141), channel_id=1, source_target_pairs={{0,4},{4,8},{8,12},{12,16},{16,20},{20,24},{24,28},{1,5},{5,9},{9,... | collective-permute-start | bytes 2359304 | tf_op jit(solution)/shard_map/ppermute | solution.py:12
  7.2 2.4 %copy.86 = bf16[8,5,128,128]{2,3,0,1:T(8,128)(2,1)} copy(bf16[8,5,128,128]{3,2,1,0:T(8,128)(2,1)} %param.13) | data formatting | bytes 2621440 | tf_op args[1]
  9.7 5.6 %collective-permute-start.2 = (bf16[8,5,128,128]{2,3,0,1:T(8,128)(2,1)}, bf16[8,5,128,128]{2,3,0,1:T(8,128)(2,1)}, u32[]{:S(2)}, u32[]{:S(2)}) collective-permute-start(bf16[8,5,128,128]{2,3,0,1:T(8,128)(2,1)} %copy.86), channel_id=1, source_target_pairs={{0,4},{4,8},{8,12},{12,16},{16,20},{20,24},{24,28},{1,5},{5,9},{9,... | collective-permute-start | bytes 3932168 | tf_op jit(solution)/shard_map/ppermute | solution.py:12
  16.7 4.5 %collective-permute-start = (s32[8,5]{0,1:T(8,128)S(1)}, s32[8,5]{0,1:T(8,128)S(1)}, u32[]{:S(2)}, u32[]{:S(2)}) collective-permute-start(s32[8,5]{0,1:T(8,128)S(1)} %copy.83), channel_id=1, source_target_pairs={{0,4},{4,8},{8,12},{12,16},{16,20},{20,24},{24,28},{1,5},{5,9},{9,... | collective-permute-start | bytes 488 | tf_op jit(solution)/shard_map/ppermute | solution.py:12
  27.0 41.2 %collective-permute-done.4 = bf16[8,128,384]{2,1,0:T(8,128)(2,1)} collective-permute-done((bf16[8,128,384]{2,1,0:T(8,128)(2,1)}, bf16[8,128,384]{2,1,0:T(8,128)(2,1)}, u32[]{:S(2)}, u32[]{:S(2)}) %collective-permute-start.4) | collective-permute-done | bytes 786464 | tf_op jit(solution)/shard_map/ppermute | solution.py:12
  86.1 10.9 %psum.7 = f32[8,4,256]{2,1,0:T(4,128)} all-reduce(f32[8,4,256]{2,1,0:T(4,128)S(1)} %all_to_all.16), channel_id=1, replica_groups=mesh['space'=8,'var'=4] {'var'}, use_global_device_ids=true, to_apply=%region_1.3 | all-reduce | flops 8192 | bytes 65536 | tf_op jit(solution)/shard_map/psum | solution.py:67
  97.0 8.3 %all-to-all-start = ((f32[8,4,256]{2,1,0:T(4,128)}), f32[8,4,256]{2,1,0:T(4,128)S(1)}, u32[]{:S(2)}, u32[]{:S(2)}) async-start(f32[8,4,256]{2,1,0:T(4,128)} %psum.7), calls=%async_computation | async-start | bytes 65536 | tf_op jit(solution)/shard_map/all_to_all | solution.py:68
  105.5 6.4 %all-to-all-done = f32[8,4,256]{2,1,0:T(4,128)S(1)} async-done(((f32[8,4,256]{2,1,0:T(4,128)}), f32[8,4,256]{2,1,0:T(4,128)S(1)}, u32[]{:S(2)}, u32[]{:S(2)}) %all-to-all-start) | async-done | bytes 32800 | tf_op jit(solution)/shard_map/all_to_all | solution.py:68
  112.6 3.3 %all-to-all-start.1 = ((f32[8,4,256]{2,1,0:T(4,128)}), f32[8,4,256]{2,1,0:T(4,128)S(1)}, u32[]{:S(2)}, u32[]{:S(2)}) async-start(f32[8,4,256]{2,1,0:T(4,128)} %all_to_all.19), calls=%async_computation.1 | async-start | bytes 65536 | tf_op jit(solution)/shard_map/all_to_all | solution.py:70
  116.5 6.1 %all-to-all-done.1 = f32[8,4,256]{2,1,0:T(4,128)S(1)} async-done(((f32[8,4,256]{2,1,0:T(4,128)}), f32[8,4,256]{2,1,0:T(4,128)S(1)}, u32[]{:S(2)}, u32[]{:S(2)}) %all-to-all-start.1) | async-done | bytes 32800 | tf_op jit(solution)/shard_map/all_to_all | solution.py:70
  122.8 4.3 %scatter_custom_fusion = f32[1024,256]{1,0:T(8,128)} fusion(s32[512]{0:T(512)S(1)} %bitcast.147, f32[512,256]{1,0:T(8,128)S(1)} %bitcast_multiply_fusion.1, f32[]{:T(128)} %constant.28.clone.1), kind=kCustom, calls=%fused_computation.73 | custom fusion | flops 131072 | bytes 1048580 | tf_op jit(solution)/shard_map/scatter-add | solution.py:79
  129.3 2.4 %collective-permute-start.6 = (bf16[8,128,384]{2,1,0:T(8,128)(2,1)S(1)}, bf16[8,128,384]{2,1,0:T(8,128)(2,1)S(1)}, u32[]{:S(2)}, u32[]{:S(2)}) collective-permute-start(bf16[8,128,384]{2,1,0:T(8,128)(2,1)S(1)} %bitcast.131), channel_id=1, source_target_pairs={{0,4},{4,8},{8,12},{12,16},{16,20},{20,24},{24,28},{1,5},{5,9},{9,... | collective-permute-start | bytes 2359304 | tf_op jit(solution)/shard_map/ppermute | solution.py:12
  135.7 27.3 %collective-permute-done.6 = bf16[8,128,384]{2,1,0:T(8,128)(2,1)S(1)} collective-permute-done((bf16[8,128,384]{2,1,0:T(8,128)(2,1)S(1)}, bf16[8,128,384]{2,1,0:T(8,128)(2,1)S(1)}, u32[]{:S(2)}, u32[]{:S(2)}) %collective-permute-start.6) | collective-permute-done | bytes 786464 | tf_op jit(solution)/shard_map/ppermute | solution.py:12
  166.4 2.9 %scatter_fusion = f32[8,128,384]{2,1,0:T(8,128)S(1)} fusion(f32[8,128,384]{2,1,0:T(8,128)S(1)} %broadcast.293.clone.1, s32[8]{0:T(128)S(1)} %get-tuple-element.55, f32[8,128,384]{2,1,0:T(8,128)} %get-tuple-element.25), kind=kCustom, calls=%fused_computation.7 | custom fusion | flops 393216 | bytes 4718624 | tf_op jit(solution)/shard_map/scatter-add | solution.py:112
  171.4 2.4 %slice_select_fusion.3 = (f32[8,128,384]{2,1,0:T(8,128)}, f32[8,128,384]{2,1,0:T(8,128)}, f32[8,128,384]{2,1,0:T(8,128)}) fusion(f32[24,128,384]{2,1,0:T(8,128)S(1)} %fusion.5, pred[8]{0:T(512)(128)(4,1)S(1)} %get-tuple-element.38, pred[8]{0:T(512)(128)(4,1)S(1)} %get-tuple-element.33, pred[8]{0:T(512)(128)(4,1)S(1)} %get-tuple-element.28), kind=kLoop, calls=%fused_computation.28 | loop fusion | flops 1179648 | bytes 9437208 | tf_op jit(solution)/shard_map/jit(_where)/select_n | solution.py:108
  173.8 2.9 %scatter_fusion.1 = f32[8,128,384]{2,1,0:T(8,128)S(1)} fusion(f32[8,128,384]{2,1,0:T(8,128)S(1)} %scatter_fusion, s32[8]{0:T(128)S(1)} %get-tuple-element.54, f32[8,128,384]{2,1,0:T(8,128)} %get-tuple-element.22), kind=kCustom, calls=%fused_computation.8 | custom fusion | flops 393216 | bytes 4718624 | tf_op jit(solution)/shard_map/scatter-add | solution.py:112
  178.8 2.4 %slice_select_fusion.2 = (f32[8,128,384]{2,1,0:T(8,128)}, f32[8,128,384]{2,1,0:T(8,128)}, f32[8,128,384]{2,1,0:T(8,128)}) fusion(f32[24,128,384]{2,1,0:T(8,128)S(1)} %fusion.4, pred[8]{0:T(512)(128)(4,1)S(1)} %get-tuple-element.39, pred[8]{0:T(512)(128)(4,1)S(1)} %get-tuple-element.34, pred[8]{0:T(512)(128)(4,1)S(1)} %get-tuple-element.29), kind=kLoop, calls=%fused_computation.27 | loop fusion | flops 1179648 | bytes 9437208 | tf_op jit(solution)/shard_map/jit(_where)/select_n | solution.py:108
  181.2 2.9 %scatter_fusion.2 = f32[8,128,384]{2,1,0:T(8,128)S(1)} fusion(f32[8,128,384]{2,1,0:T(8,128)S(1)} %scatter_fusion.1, s32[8]{0:T(128)S(1)} %get-tuple-element.53, f32[8,128,384]{2,1,0:T(8,128)} %get-tuple-element.19), kind=kCustom, calls=%fused_computation.9 | custom fusion | flops 393216 | bytes 4718624 | tf_op jit(solution)/shard_map/scatter-add | solution.py:112
  186.2 2.4 %slice_select_fusion.1 = (f32[8,128,384]{2,1,0:T(8,128)}, f32[8,128,384]{2,1,0:T(8,128)}, f32[8,128,384]{2,1,0:T(8,128)}) fusion(f32[24,128,384]{2,1,0:T(8,128)S(1)} %fusion.3, pred[8]{0:T(512)(128)(4,1)S(1)} %get-tuple-element.40, pred[8]{0:T(512)(128)(4,1)S(1)} %get-tuple-element.35, pred[8]{0:T(512)(128)(4,1)S(1)} %get-tuple-element.30), kind=kLoop, calls=%fused_computation.26 | loop fusion | flops 1179648 | bytes 9437208 | tf_op jit(solution)/shard_map/jit(_where)/select_n | solution.py:108
  188.7 2.9 %scatter_fusion.3 = f32[8,128,384]{2,1,0:T(8,128)S(1)} fusion(f32[8,128,384]{2,1,0:T(8,128)S(1)} %scatter_fusion.2, s32[8]{0:T(128)S(1)} %get-tuple-element.52, f32[8,128,384]{2,1,0:T(8,128)} %get-tuple-element.16), kind=kCustom, calls=%fused_computation.10 | custom fusion | flops 393216 | bytes 4718624 | tf_op jit(solution)/shard_map/scatter-add | solution.py:112
  201.7 3.1 %scatter_fusion.6 = f32[8,128,384]{2,1,0:T(8,128)S(1)} fusion(f32[8,128,384]{2,1,0:T(8,128)S(1)} %scatter_fusion.5, s32[8]{0:T(128)S(1)} %get-tuple-element.49, f32[8,128,384]{2,1,0:T(8,128)} %get-tuple-element.21), kind=kCustom, calls=%fused_computation.13 | custom fusion | flops 393216 | bytes 4718624 | tf_op jit(solution)/shard_map/scatter-add | solution.py:112
  206.5 2.9 %scatter_fusion.8 = f32[8,128,384]{2,1,0:T(8,128)S(1)} fusion(f32[8,128,384]{2,1,0:T(8,128)S(1)} %scatter_fusion.7, s32[8]{0:T(128)S(1)} %get-tuple-element.47, f32[8,128,384]{2,1,0:T(8,128)} %get-tuple-element.15), kind=kCustom, calls=%fused_computation.15 | custom fusion | flops 393216 | bytes 4718624 | tf_op jit(solution)/shard_map/scatter-add | solution.py:112
  215.4 2.9 %scatter_fusion.11 = f32[8,128,384]{2,1,0:T(8,128)S(1)} fusion(f32[8,128,384]{2,1,0:T(8,128)S(1)} %scatter_fusion.10, s32[8]{0:T(128)S(1)} %get-tuple-element.44, f32[8,128,384]{2,1,0:T(8,128)} %get-tuple-element.20), kind=kCustom, calls=%fused_computation.18 | custom fusion | flops 393216 | bytes 4718624 | tf_op jit(solution)/shard_map/scatter-add | solution.py:112
  220.0 2.9 %scatter_fusion.13 = f32[8,128,384]{2,1,0:T(8,128)S(1)} fusion(f32[8,128,384]{2,1,0:T(8,128)S(1)} %scatter_fusion.12, s32[8]{0:T(128)S(1)} %get-tuple-element.42, f32[8,128,384]{2,1,0:T(8,128)} %get-tuple-element.14), kind=kCustom, calls=%fused_computation.20 | custom fusion | flops 393216 | bytes 4718624 | tf_op jit(solution)/shard_map/scatter-add | solution.py:112
  (144 shorter events, 67.1 us)
Async XLA Ops:
  0.0 16.6 %copy-start.20 = (s32[8,5]{1,0:T(8,128)S(1)}, s32[8,5]{1,0:T(8,128)}, u32[]{:S(2)}) copy-start(s32[8,5]{1,0:T(8,128)} %param.14) | copy-start | bytes 484
  0.0 21.2 %copy-start.18 = (s32[32,16]{0,1:T(8,128)S(1)}, s32[32,16]{0,1:T(8,128)}, u32[]{:S(2)}) copy-start(s32[32,16]{0,1:T(8,128)} %param.17) | copy-start | bytes 6148
  0.0 21.6 %copy-start.23 = (bf16[24,16]{0,1:T(8,128)(2,1)S(1)}, bf16[24,16]{0,1:T(8,128)(2,1)}, u32[]{:S(2)}) copy-start(bf16[24,16]{0,1:T(8,128)(2,1)} %param.16) | copy-start | bytes 2308
  0.0 22.0 %copy-start.17 = (f32[24,1024]{1,0:T(8,128)S(1)}, f32[24,1024]{1,0:T(8,128)}, u32[]{:S(2)}) copy-start(f32[24,1024]{1,0:T(8,128)} %param.15) | copy-start | bytes 294916
  0.0 68.2 %collective-permute-start.4 = (bf16[8,128,384]{2,1,0:T(8,128)(2,1)}, bf16[8,128,384]{2,1,0:T(8,128)(2,1)}, u32[]{:S(2)}, u32[]{:S(2)}) collective-permute-start(bf16[8,128,384]{2,1,0:T(8,128)(2,1)} %bitcast.141), channel_id=1, source_target_pairs={{0,4},{4,8},{8,12},{12,16},{16,20},{20,24},{24,28},{1,5},{5,9},{9,... | collective-permute-start | bytes 2359304 | tf_op jit(solution)/shard_map/ppermute | solution.py:12
  5.9 63.5 %collective-permute-start.5 = (bf16[8,128,384]{2,1,0:T(8,128)(2,1)}, bf16[8,128,384]{2,1,0:T(8,128)(2,1)}, u32[]{:S(2)}, u32[]{:S(2)}) collective-permute-start(bf16[8,128,384]{2,1,0:T(8,128)(2,1)} %bitcast.142), channel_id=1, source_target_pairs={{4,0},{8,4},{12,8},{16,12},{20,16},{24,20},{28,24},{5,1},{9,5},{13... | collective-permute-start | bytes 2359304 | tf_op jit(solution)/shard_map/ppermute | solution.py:15
  9.7 123.6 %collective-permute-start.2 = (bf16[8,5,128,128]{2,3,0,1:T(8,128)(2,1)}, bf16[8,5,128,128]{2,3,0,1:T(8,128)(2,1)}, u32[]{:S(2)}, u32[]{:S(2)}) collective-permute-start(bf16[8,5,128,128]{2,3,0,1:T(8,128)(2,1)} %copy.86), channel_id=1, source_target_pairs={{0,4},{4,8},{8,12},{12,16},{16,20},{20,24},{24,28},{1,5},{5,9},{9,... | collective-permute-start | bytes 3932168 | tf_op jit(solution)/shard_map/ppermute | solution.py:12
  15.3 118.0 %collective-permute-start.3 = (bf16[8,5,128,128]{2,3,0,1:T(8,128)(2,1)}, bf16[8,5,128,128]{2,3,0,1:T(8,128)(2,1)}, u32[]{:S(2)}, u32[]{:S(2)}) collective-permute-start(bf16[8,5,128,128]{2,3,0,1:T(8,128)(2,1)} %copy.86), channel_id=1, source_target_pairs={{4,0},{8,4},{12,8},{16,12},{20,16},{24,20},{28,24},{5,1},{9,5},{13... | collective-permute-start | bytes 3932168 | tf_op jit(solution)/shard_map/ppermute | solution.py:15
  16.7 115.1 %collective-permute-start = (s32[8,5]{0,1:T(8,128)S(1)}, s32[8,5]{0,1:T(8,128)S(1)}, u32[]{:S(2)}, u32[]{:S(2)}) collective-permute-start(s32[8,5]{0,1:T(8,128)S(1)} %copy.83), channel_id=1, source_target_pairs={{0,4},{4,8},{8,12},{12,16},{16,20},{20,24},{24,28},{1,5},{5,9},{9,... | collective-permute-start | bytes 488 | tf_op jit(solution)/shard_map/ppermute | solution.py:12
  25.0 44.4 %copy-start.12 = (bf16[1024,384]{1,0:T(8,128)(2,1)S(1)}, bf16[1024,384]{1,0:T(8,128)(2,1)}, u32[]{:S(2)}) copy-start(bf16[1024,384]{1,0:T(8,128)(2,1)} %param.12) | copy-start | bytes 2359300
  68.2 64.9 %collective-permute-start.1 = (s32[8,5]{0,1:T(8,128)S(1)}, s32[8,5]{0,1:T(8,128)S(1)}, u32[]{:S(2)}, u32[]{:S(2)}) collective-permute-start(s32[8,5]{0,1:T(8,128)S(1)} %copy.83), channel_id=1, source_target_pairs={{4,0},{8,4},{12,8},{16,12},{20,16},{24,20},{28,24},{5,1},{9,5},{13... | collective-permute-start | bytes 488 | tf_op jit(solution)/shard_map/ppermute | solution.py:15
  84.2 21.0 %copy-start.22 = (f32[32,16]{0,1:T(8,128)S(1)}, f32[32,16]{0,1:T(8,128)}, u32[]{:S(2)}) copy-start(f32[32,16]{0,1:T(8,128)} %param.20) | copy-start | bytes 6148
  84.2 21.1 %copy-start.24 = (s32[1,8]{1,0:T(1,128)S(1)}, s32[1,8]{1,0:T(1,128)}, u32[]{:S(2)}) copy-start(s32[1,8]{1,0:T(1,128)} %param.21) | copy-start | bytes 100
  84.2 27.7 %copy-start.19 = (f32[32,256]{1,0:T(8,128)S(1)}, f32[32,256]{1,0:T(8,128)}, u32[]{:S(2)}) copy-start(f32[32,256]{1,0:T(8,128)} %param.19) | copy-start | bytes 98308
  84.2 31.8 %copy-start.3 = (f32[1024,24,16]{0,2,1:T(8,128)S(1)}, f32[1024,24,16]{0,2,1:T(8,128)}, u32[]{:S(2)}) copy-start(f32[1024,24,16]{0,2,1:T(8,128)} %copy-done.2) | copy-start | bytes 4718596
  97.0 14.9 %all-to-all-start = ((f32[8,4,256]{2,1,0:T(4,128)}), f32[8,4,256]{2,1,0:T(4,128)S(1)}, u32[]{:S(2)}, u32[]{:S(2)}) async-start(f32[8,4,256]{2,1,0:T(4,128)} %psum.7), calls=%async_computation | async-start | bytes 65536 | tf_op jit(solution)/shard_map/all_to_all | solution.py:68
  112.6 10.0 %all-to-all-start.1 = ((f32[8,4,256]{2,1,0:T(4,128)}), f32[8,4,256]{2,1,0:T(4,128)S(1)}, u32[]{:S(2)}, u32[]{:S(2)}) async-start(f32[8,4,256]{2,1,0:T(4,128)} %all_to_all.19), calls=%async_computation.1 | async-start | bytes 65536 | tf_op jit(solution)/shard_map/all_to_all | solution.py:70
  129.3 33.7 %collective-permute-start.6 = (bf16[8,128,384]{2,1,0:T(8,128)(2,1)S(1)}, bf16[8,128,384]{2,1,0:T(8,128)(2,1)S(1)}, u32[]{:S(2)}, u32[]{:S(2)}) collective-permute-start(bf16[8,128,384]{2,1,0:T(8,128)(2,1)S(1)} %bitcast.131), channel_id=1, source_target_pairs={{0,4},{4,8},{8,12},{12,16},{16,20},{20,24},{24,28},{1,5},{5,9},{9,... | collective-permute-start | bytes 2359304 | tf_op jit(solution)/shard_map/ppermute | solution.py:12
  131.7 31.3 %collective-permute-start.7 = (bf16[8,128,384]{2,1,0:T(8,128)(2,1)S(1)}, bf16[8,128,384]{2,1,0:T(8,128)(2,1)S(1)}, u32[]{:S(2)}, u32[]{:S(2)}) collective-permute-start(bf16[8,128,384]{2,1,0:T(8,128)(2,1)S(1)} %bitcast.132), channel_id=1, source_target_pairs={{4,0},{8,4},{12,8},{16,12},{20,16},{24,20},{28,24},{5,1},{9,5},{13... | collective-permute-start | bytes 2359304 | tf_op jit(solution)/shard_map/ppermute | solution.py:15
  135.7 28.1 %copy-start.1 = (bf16[24,5,128,128]{2,3,0,1:T(8,128)(2,1)}, bf16[24,5,128,128]{2,3,0,1:T(8,128)(2,1)S(1)}, u32[]{:S(2)}) copy-start(bf16[24,5,128,128]{2,3,0,1:T(8,128)(2,1)S(1)} %pad_maximum_fusion) | copy-start | bytes 11796484
  201.7 3.1 %copy-start.8 = (f32[8,128,384]{2,1,0:T(8,128)S(1)}, f32[8,128,384]{2,1,0:T(8,128)}, u32[]{:S(2)}) copy-start(f32[8,128,384]{2,1,0:T(8,128)} %get-tuple-element.18) | copy-start | bytes 4718596
  206.5 2.9 %copy-start.9 = (f32[8,128,384]{2,1,0:T(8,128)S(1)}, f32[8,128,384]{2,1,0:T(8,128)}, u32[]{:S(2)}) copy-start(f32[8,128,384]{2,1,0:T(8,128)} %get-tuple-element.12) | copy-start | bytes 4718596
  215.4 2.9 %copy-start.5 = (f32[8,128,384]{2,1,0:T(8,128)S(1)}, f32[8,128,384]{2,1,0:T(8,128)}, u32[]{:S(2)}) copy-start(f32[8,128,384]{2,1,0:T(8,128)} %get-tuple-element.17) | copy-start | bytes 4718596
  220.0 2.9 %copy-start.7 = (f32[8,128,384]{2,1,0:T(8,128)S(1)}, f32[8,128,384]{2,1,0:T(8,128)}, u32[]{:S(2)}) copy-start(f32[8,128,384]{2,1,0:T(8,128)} %get-tuple-element.11) | copy-start | bytes 4718596
  (11 other events, 15.1 us)
where the time goes:
time: 229 us; the launch traced here: 227 us
  waiting for transfers between devices  81 us (35%)
  other arithmetic  59.8 us (26%)
  starting transfers between devices  35.2 us (15%)
  local copies, waits for them, and re-layouts  23.5 us (10%)
  matrix products  15.8 us (7%)
  blocking collectives  10.9 us (5%)
    ppermute x4, waiting for transfers between devices, padded(): lax.ppermute(lax.slice_in_dim(block, block.shape[dim] - width, None, axis...  68.5 us
    scatter-add x15, other arithmetic, shards(): sections[section].at[jnp.clip(targets, 0, block_count - 1)]  35 us
    ppermute x4, starting transfers between devices, padded(): lax.ppermute(lax.slice_in_dim(block, block.shape[dim] - width, None, axis...  18.5 us
    select_n x5, other arithmetic, shards(): jnp.where(inside[:, None, None], terms[lo_row:lo_row + block_count], 0.0)  11.8 us
    psum x1, blocking collectives, shards(): modelled = lax.psum(partial_model, 'var')  10.9 us
    dot_general x5, matrix products, shards(): jnp.einsum('bji,bjn->bin', roots_wide[:, link_index], inputs_wide, prefer...  9.39 us
    unnamed x56, local copies, waits for them, and re-layouts  9.35 us
    all_to_all x1, starting transfers between devices, shards(): lax.all_to_all(modelled, 'space', split_axis=0, concat_axis=0, tiled=True)  8.26 us
  transfers between devices with their start and end apart: 10, of which 4 were waited for; matrix products, arithmetic and copies ran while one was open for 14% of the time, Pallas kernels for 0%

commit v1 on v0

v1 whole, which is shorter than its diff:
```python
import functools

import jax
import jax.numpy as jnp
from jax import lax
from jax.experimental import pallas as pl
from jax.experimental.pallas import tpu as pltpu
from jax.sharding import PartitionSpec as P

F32 = jnp.float32
BF16 = jnp.bfloat16
LANES = 128
NT = (((1,), (1,)), ((), ()))


def repeat_steps(count, body):
    if count <= 2:
        for step in range(count):
            body(step)
    else:
        lax.fori_loop(0, count, lambda step, carry: (body(step), carry)[1], 0)


def at(step, size):
    if isinstance(step, int):
        return pl.ds(step * size, size)
    return pl.ds(pl.multiple_of(step * size, size), size)


def dot(a, b):
    return jnp.dot(a, b, preferred_element_type=F32)


def dot_nt(a, b):
    return lax.dot_general(a, b, NT, preferred_element_type=F32)


def split2(x):
    high = x.astype(BF16)
    return high, (x - high.astype(F32)).astype(BF16)


def iota(shape, axis):
    return lax.broadcasted_iota(jnp.int32, shape, axis)


def column(values):
    slots, width = values.shape
    wide = jnp.broadcast_to(values.astype(F32)[:, None, :], (slots, width, width))
    wide = wide.reshape(slots * width, width)
    hit = iota(wide.shape, 1) == lax.rem(iota(wide.shape, 0), width)
    return jnp.sum(jnp.where(hit, wide, 0.0), axis=1, keepdims=True)


def one_hot(cols, count):
    lane = iota((cols.shape[0], count), 1)
    return jnp.where(lane == cols.astype(jnp.int32), 1.0, 0.0).astype(BF16)


def scale_spread(dims, half):
    row = iota((LANES, dims.lanes), 0) - 2 * dims.vars * half
    lane = iota((LANES, dims.lanes), 1)
    first = lane - dims.members * row
    second = first + dims.members * dims.vars
    hit = ((first >= 0) & (first < dims.members)) | ((second >= 0) & (second < dims.members))
    return jnp.where(hit, 1.0, 0.0).astype(BF16)


def target_spread(dims, half):
    shape = (LANES, dims.others * dims.block)
    row = iota(shape, 0) - 4 * dims.vars - dims.others * half
    first = iota(shape, 1) - dims.block * row
    return jnp.where((first >= 0) & (first < dims.block), 1.0, 0.0).astype(BF16)


def fill_operator(dims, op_ref, targets, parts, shift):
    for q in range(dims.blocks):
        total = None
        for target, part in zip(targets, parts):
            term = jnp.where(target == float(q + shift), part, 0.0)
            total = term if total is None else total + term
        op_ref[:, q * dims.block : (q + 1) * dims.block] = total.astype(BF16)


def model_rows(dims, op_ref, plane, spread, control_ref, opw_ref):
    summed = dot(op_ref[...], control_ref[...])
    state = (summed * dot(plane, spread)).astype(BF16)
    bands = dot(state, opw_ref[...])
    return jnp.sum(bands.reshape(dims.chunk_slots, dims.points, bands.shape[1]), axis=1)


def select_kernel(dims, roots_ref, sigma_ref, cols_ref, wgt_ref, nb_ref, out_ref):
    tile = lax.axis_index("space")
    half = lax.rem(lax.axis_index("var"), 2)
    sigma = sigma_ref[...]
    rest = jnp.zeros((LANES - 2 * dims.vars, dims.columns), F32)
    sigma0 = split2(jnp.concatenate([sigma, sigma, rest], axis=0))
    pad = jnp.zeros((2 * dims.vars, dims.columns), F32)
    tail = jnp.zeros((LANES - 4 * dims.vars, dims.columns), F32)
    sigma1 = split2(jnp.concatenate([pad, sigma, sigma, tail], axis=0))
    nb = (nb_ref[...] - tile * dims.blocks).astype(F32)
    lane = iota((dims.blocks, LANES), 1)
    nbs = []
    for h in range(2):
        wide = jnp.zeros((dims.blocks, LANES), F32)
        for k in range(dims.others):
            wide = jnp.where(
                lane == 4 * dims.vars + dims.others * h + k, nb[:, k + 1 : k + 2], wide
            )
        nbs.append(wide.astype(BF16))

    def body(step):
        plane = jnp.zeros((dims.chunk, LANES), F32)
        for h, sigmas in ((0, sigma0), (1, sigma1)):
            slots = at(step + h * dims.half_chunks, dims.chunk_slots)
            cols = column(cols_ref[slots, :])
            hot = one_hot(cols, dims.columns)
            scale = dot_nt(hot, sigmas[0]) + dot_nt(hot, sigmas[1])
            hot_block = one_hot(jnp.floor(cols * (1.0 / dims.block)), dims.blocks)
            plane = plane + scale * column(wgt_ref[slots, :]) + dot(hot_block, nbs[h])
        lanes = iota((dims.chunk, LANES), 1)
        low = ((lanes >= dims.vars) & (lanes < 2 * dims.vars)) | (
            (lanes >= 3 * dims.vars) & (lanes < 4 * dims.vars)
        )
        high = plane.astype(BF16).astype(F32)
        rows = at(step, dims.chunk)
        wide = dims.others * dims.block
        out_ref[rows, wide : wide + LANES] = jnp.where(low, plane - high, high).astype(BF16)
        slots = at(step + half * dims.half_chunks, dims.chunk_slots)
        hot = one_hot(column(cols_ref[slots, :]), dims.columns)
        for k in range(dims.others):
            root = roots_ref[:, k + 1].reshape(dims.columns, dims.block)
            out_ref[rows, k * dims.block : (k + 1) * dims.block] = dot(hot, root).astype(BF16)

    repeat_steps(dims.half_chunks, body)


def own_kernel(
    dims, roots_ref, cols_ref, plane_ref, control_ref, opw_ref, model_ref, opt_ref, op_ref
):
    for h in range(2):
        spread = scale_spread(dims, h)
        targets_of = target_spread(dims, h)

        def body(step):
            plane = plane_ref[at(step, dims.chunk), :]
            slots = at(step + h * dims.half_chunks, dims.chunk_slots)
            cols = column(cols_ref[slots, :])
            hot = one_hot(cols, dims.columns)
            wide = dot(plane, targets_of)
            own = jnp.broadcast_to(
                jnp.floor(cols * (1.0 / dims.block)), (dims.chunk, dims.block)
            )
            targets, parts = [own], []
            for k in range(dims.others):
                targets.append(wide[:, k * dims.block : (k + 1) * dims.block])
            for k in range(dims.others + 1):
                root = roots_ref[:, k].reshape(dims.columns, dims.block)
                parts.append(dot(hot, root))
            fill_operator(dims, op_ref, targets, parts, 0)
            model_ref[slots, :] = model_rows(dims, op_ref, plane, spread, control_ref, opw_ref)
            opt_ref[:, at(step + h * dims.half_chunks, dims.chunk)] = op_ref[...].T

        repeat_steps(dims.half_chunks, body)


def side_parts(dims, plane_ref, message_ref, step, targets_of):
    rows = at(step, dims.chunk)
    wide = dims.others * dims.block
    plane = plane_ref[rows, wide : wide + LANES]
    target = dot(plane, targets_of)
    targets, parts = [], []
    for k in range(dims.others):
        lanes = slice(k * dims.block, (k + 1) * dims.block)
        targets.append(target[:, lanes])
        parts.append(message_ref[rows, lanes].astype(F32))
    return plane, targets, parts


def sides_kernel(dims, b0_ref, b1_ref, a0_ref, a1_ref, control_ref, opw_ref, below_ref, above_ref, op_ref):
    half = lax.rem(lax.axis_index("var"), 2)
    for which, refs in ((half, (b0_ref, a0_ref)), (1 - half, (b1_ref, a1_ref))):
        spread = scale_spread(dims, which)
        targets_of = target_spread(dims, which)
        for side, (ref, model_ref) in enumerate(zip(refs, (below_ref, above_ref))):
            plane_ref = (b0_ref, a0_ref)[side]
            shift = (dims.blocks, -dims.blocks)[side]

            def body(step):
                plane, targets, parts = side_parts(dims, plane_ref, ref, step, targets_of)
                fill_operator(dims, op_ref, targets, parts, shift)
                slots = at(step + which * dims.half_chunks, dims.chunk_slots)
                model_ref[slots, :] = model_rows(
                    dims, op_ref, plane, spread, control_ref, opw_ref
                )

            repeat_steps(dims.half_chunks, body)


def turn_kernel(dims, b0_ref, b1_ref, a0_ref, a1_ref, opt_ref, op_ref):
    half = lax.rem(lax.axis_index("var"), 2)
    for place, (which, refs) in enumerate(
        ((half, (b0_ref, a0_ref)), (1 - half, (b1_ref, a1_ref)))
    ):
        targets_of = target_spread(dims, which)
        for side, (ref, shift) in enumerate(zip(refs, (dims.blocks, -dims.blocks))):
            plane_ref = (b0_ref, a0_ref)[side]

            def body(step):
                _, targets, parts = side_parts(dims, plane_ref, ref, step, targets_of)
                fill_operator(dims, op_ref, targets, parts, shift)
                chunk = step + (2 * side + place) * dims.half_chunks
                opt_ref[:, at(chunk, dims.chunk)] = op_ref[...].T

            repeat_steps(dims.half_chunks, body)


def pull_rows(dims, w_ref, slots, scale):
    rows = w_ref[slots, :]
    wide = jnp.broadcast_to(
        rows[:, None, :], (dims.chunk_slots, dims.points, dims.lanes)
    ).reshape(dims.chunk, dims.lanes)
    return (wide * scale).astype(BF16)


def bands_to_vars(misfit, opw):
    high = misfit.astype(BF16)
    rest = misfit - high.astype(F32)
    middle = rest.astype(BF16)
    low = (rest - middle.astype(F32)).astype(BF16)
    return dot_nt(high, opw) + (dot_nt(middle, opw) + dot_nt(low, opw))


def own_adjoint_kernel(dims, misfit_ref, plane_ref, opt_ref, control_ref, opw_ref, out_ref, w_ref, adj_ref):
    w_ref[...] = bands_to_vars(misfit_ref[...], opw_ref[...])
    for h in range(2):
        spread = scale_spread(dims, h)

        def body(step):
            scale = dot(plane_ref[at(step, dims.chunk), :], spread)
            chunk = step + h * dims.half_chunks
            adj_ref[at(chunk, dims.chunk), :] = pull_rows(
                dims, w_ref, at(chunk, dims.chunk_slots), scale
            )

        repeat_steps(dims.half_chunks, body)
    for part in range(dims.columns // 256):
        rows = slice(part * 256, (part + 1) * 256)
        out_ref[rows, :] = control_ref[rows, :].astype(F32) + dot(opt_ref[rows, :], adj_ref[...])


def sides_adjoint_kernel(
    dims, mb_ref, ma_ref, below_ref, above_ref, opt_ref, own_ref, opw_ref, out_ref, w_ref, adj_ref
):
    half = lax.rem(lax.axis_index("var"), 2)
    spreads = [scale_spread(dims, half), scale_spread(dims, 1 - half)]
    for side, (misfit_ref, ref) in enumerate(((mb_ref, below_ref), (ma_ref, above_ref))):
        w_ref[...] = bands_to_vars(misfit_ref[...], opw_ref[...])
        for place, which in enumerate((half, 1 - half)):

            def body(step):
                scale = dot(ref[at(step, dims.chunk), :], spreads[place])
                chunk = step + (2 * side + place) * dims.half_chunks
                slots = at(step + which * dims.half_chunks, dims.chunk_slots)
                adj_ref[at(chunk, dims.chunk), :] = pull_rows(dims, w_ref, slots, scale)

            repeat_steps(dims.half_chunks, body)
    for part in range(dims.columns // 256):
        rows = slice(part * 256, (part + 1) * 256)
        total = own_ref[rows, :] + dot(opt_ref[rows, :], adj_ref[...])
        out_ref[rows, :] = total.astype(BF16)


class Dims:
    def __init__(self, control, roots, sigma, foot_cols):
        self.blocks, links, self.block = roots.shape[:3]
        self.others = links - 1
        self.columns, self.lanes = control.shape
        self.vars = sigma.shape[0]
        self.members = self.lanes // self.vars
        self.slots, self.points = foot_cols.shape
        self.rows = self.slots * self.points
        self.chunk = min(256, self.rows // 2)
        self.chunk_slots = self.chunk // self.points
        self.half_chunks = self.rows // 2 // self.chunk
        self.width = self.others * self.block + LANES


def call(kernel, name, out_shape, scratch, flops, in_specs=None):
    specs = {} if in_specs is None else {"in_specs": in_specs, "grid": (1,)}
    if in_specs is not None:
        specs["out_specs"] = jax.tree.map(
            lambda s: pl.BlockSpec(s.shape, lambda i, n=len(s.shape): (0,) * n), out_shape
        )
    return pl.pallas_call(
        kernel,
        out_shape=out_shape,
        scratch_shapes=scratch,
        compiler_params=pltpu.CompilerParams(vmem_limit_bytes=56 * 1024 * 1024),
        cost_estimate=pl.CostEstimate(flops=flops, bytes_accessed=4000000, transcendentals=0),
        name=name,
        **specs,
    )


def whole(array):
    return pl.BlockSpec(array.shape, lambda i, n=array.ndim: (0,) * n)


def shards(
    control,
    roots,
    neighbours,
    sigma,
    obs_op,
    foot_cols,
    foot_wgt,
    obs_value,
    obs_rinv,
    owner_counts,
):
    dims = Dims(control, roots, sigma, foot_cols)
    bands = obs_op.shape[1]
    members = dims.members
    tiles = lax.axis_size("space")
    ranks = lax.axis_size("var")
    forward = [(i, i + 1) for i in range(tiles - 1)]
    backward = [(i + 1, i) for i in range(tiles - 1)]
    up = lambda x: lax.ppermute(x, "space", forward)
    down = lambda x: lax.ppermute(x, "space", backward)
    swap = lambda x, bit: lax.ppermute(x, "var", [(i, i ^ bit) for i in range(ranks)])
    shape = jax.ShapeDtypeStruct
    half_rows = dims.rows // 2
    flat = bands * members

    message = call(
        functools.partial(select_kernel, dims),
        "select",
        shape((half_rows, dims.width), BF16),
        [],
        2000000000,
    )(roots, sigma, foot_cols, foot_wgt, neighbours)
    below0, above0 = up(message), down(message)
    below1, above1 = swap(below0, 1), swap(above0, 1)

    identity_m = jnp.eye(members, dtype=BF16)
    opw = (obs_op[:, None, :, None] * identity_m[None, :, None, :]).reshape(dims.lanes, flat)
    observed = lax.all_to_all(
        jnp.concatenate([obs_value, obs_rinv], axis=1), "space", 0, 0, tiled=True
    )
    capacity = dims.slots // owner_counts.shape[1]
    slot_ids = jnp.arange(dims.slots, dtype=jnp.int32)
    live = slot_ids % capacity < jnp.repeat(owner_counts[0], capacity)
    rinv = jnp.repeat(jnp.where(live[:, None], observed[:, flat:], 0.0), members, axis=1)
    value = observed[:, :flat]

    plane_spec = pl.BlockSpec((half_rows, LANES), lambda i: (0, dims.others * dims.block // LANES))
    own_model, own_opt = call(
        functools.partial(own_kernel, dims),
        "own_model",
        (shape((dims.slots, flat), F32), shape((dims.columns, dims.rows), BF16)),
        [pltpu.VMEM((dims.chunk, dims.columns), BF16)],
        4000000000,
        [whole(roots), whole(foot_cols), plane_spec, whole(control), whole(opw)],
    )(roots, foot_cols, message, control, opw)

    sides = (below0, below1, above0, above1)
    part_below, part_above = call(
        functools.partial(sides_kernel, dims),
        "sides_model",
        (shape((dims.slots, flat), F32),) * 2,
        [pltpu.VMEM((dims.chunk, dims.columns), BF16)],
        4000000000,
    )(*sides, control, opw)
    modelled = own_model + down(part_below) + up(part_above)
    bit = 1
    while bit < ranks:
        modelled = modelled + swap(modelled, bit)
        bit *= 2
    misfit = rinv * (modelled - value)
    misfit_below, misfit_above = up(misfit), down(misfit)

    sides_opt = call(
        functools.partial(turn_kernel, dims),
        "sides_turn",
        shape((dims.columns, 2 * dims.rows), BF16),
        [pltpu.VMEM((dims.chunk, dims.columns), BF16)],
        4000000000,
    )(*sides)
    own_total = call(
        functools.partial(own_adjoint_kernel, dims),
        "own_adjoint",
        shape((dims.columns, dims.lanes), F32),
        [pltpu.VMEM((dims.slots, dims.lanes), F32), pltpu.VMEM((dims.rows, dims.lanes), BF16)],
        2000000000,
        [whole(misfit), plane_spec, whole(own_opt), whole(control), whole(opw)],
    )(misfit, message, own_opt, control, opw)
    return call(
        functools.partial(sides_adjoint_kernel, dims),
        "sides_adjoint",
        shape((dims.columns, dims.lanes), BF16),
        [pltpu.VMEM((dims.slots, dims.lanes), F32), pltpu.VMEM((2 * dims.rows, dims.lanes), BF16)],
        4000000000,
        [whole(misfit), whole(misfit)] + [plane_spec] * 2 + [whole(sides_opt), whole(own_total), whole(opw)],
    )(misfit_below, misfit_above, below0, above0, sides_opt, own_total, opw)


def solution(mesh):
    return jax.shard_map(
        shards,
        mesh=mesh,
        in_specs=(
            P("space", "var"),
            P("space", None, None, None),
            P("space", None),
            P("var", "space"),
            P("var", None),
            P("space", None),
            P("space", None),
            P("space", None),
            P("space", None),
            P("space", None),
        ),
        out_specs=P("space", "var"),
        check_vma=False,
    )
```

time: 229 us -> 74.4 us (0.32)
  waiting for transfers between devices: 81 us -> 6.77 us
  other arithmetic: 59.8 us -> 0.29 us
  Pallas kernels: 0 us -> 29.5 us
  matrix products: 15.8 us -> 0 us
  local copies, waits for them, and re-layouts: 23.5 us -> 8.71 us
  blocking collectives: 10.9 us -> 0 us
  starting transfers between devices: 35.2 us -> 27.7 us
    ppermute x8 -> x10, waiting for transfers between devices: 68.5 us -> 6.76 us  [the longest x3 5.78 us: shards(): up = lambda x: lax.ppermute(x, 'space', forward)]
    scatter-add x16 -> x0, other arithmetic: 39.4 us -> none  [the longest x15 35 us: shards(): sections[section].at[jnp.clip(targets, 0, block_count - 1)]]
    pallas_call x0 -> x6, Pallas kernels: none -> 29.5 us  [the longest x1 6.18 us: shards(): call(functools.partial(own_kernel, dims), 'own_model', (shape((dims.slots...]
    dot_general x12 -> x0, matrix products: 15.8 us -> none  [the longest x5 9.39 us: shards(): jnp.einsum('bji,bjn->bin', roots_wide[:, link_index], inputs_wide, prefer...]
    all_to_all x2 -> x1, waiting for transfers between devices: 12.5 us -> 0.01 us  [shards(): lax.all_to_all(jnp.concatenate([obs_value, obs_rinv], axis=1), 'space', 0...]
    select_n x12 -> x1, other arithmetic: 12 us -> 0.07 us  [shards(): jnp.where(live[:, None], observed[:, flat:], 0.0)]
    psum x1 -> x0, blocking collectives: 10.9 us -> none  [shards(): modelled = lax.psum(partial_model, 'var')]
    gather x6 -> x0, local copies, waits for them, and re-layouts: 8.57 us -> none  [the longest x5 7 us: shards(): picked = jnp.take(extended, local_ids[:, link_index], axis=0)]
  transfers between devices with their start and end apart: 10 -> 11, of which waited for: 4 -> 3; matrix products, arithmetic and copies ran while one was open for 14% -> 4% of each run, Pallas kernels for 0% -> 29%
where the time goes in v1:
time: 74.4 us; the launch traced here: 73.1 us
  Pallas kernels  29.5 us (40%)
  starting transfers between devices  27.7 us (37%)
  local copies, waits for them, and re-layouts  8.71 us (12%)
  waiting for transfers between devices  6.77 us (9%)
    ppermute x3, starting transfers between devices, shards(): up = lambda x: lax.ppermute(x, 'space', forward)  16 us
    all_to_all x1, starting transfers between devices, shards(): lax.all_to_all(jnp.concatenate([obs_value, obs_rinv], axis=1), 'space', 0...  6.19 us
    pallas_call x1, Pallas kernels, shards(): call(functools.partial(own_kernel, dims), 'own_model', (shape((dims.slots...  6.18 us
    pallas_call x1, Pallas kernels, shards(): call(functools.partial(sides_kernel, dims), 'sides_model', (shape((dims.s...  6 us
    ppermute x3, waiting for transfers between devices, shards(): up = lambda x: lax.ppermute(x, 'space', forward)  5.78 us
    unnamed x28, local copies, waits for them, and re-layouts  5.57 us
    pallas_call x1, Pallas kernels, shards(): call(functools.partial(sides_adjoint_kernel, dims), 'sides_adjoint', shap...  4.93 us
    pallas_call x1, Pallas kernels, shards(): call(functools.partial(turn_kernel, dims), 'sides_turn', shape((dims.colu...  4.89 us
  transfers between devices with their start and end apart: 11, of which 3 were waited for; matrix products, arithmetic and copies ran while one was open for 4% of the time, Pallas kernels for 29%

profile of v1, /device:TPU:0, one launch (start us, length us, event | category | flops | bytes accessed | tf_op | source)
XLA Modules:
  0.0 73.1 jit_solution(17610248549442427940)
XLA Ops:
  0.0 1.4 %copy.21.cols_ref = s32[32,16]{1,0:T(8,128)} copy(s32[32,16]{0,1:T(8,128)} %param.15) | data formatting | bytes 4096 | tf_op args[5]
  1.4 1.4 %copy.19.wgt_ref = f32[32,16]{1,0:T(8,128)} copy(f32[32,16]{0,1:T(8,128)} %param.16) | data formatting | bytes 4096 | tf_op args[6]
  2.8 3.6 %select.3.plane_ref = bf16[256,640]{1,0:T(8,128)(2,1)} custom-call(bf16[8,5,128,128]{3,2,1,0:T(8,128)(2,1)} %roots_ref.3, f32[24,1024]{1,0:T(8,128)} %sigma_ref.1, s32[32,16]{1,0:T(8,128)} %copy.21.cols_ref, f32[32,16]{1,0:T(8,128)} %copy.19.wgt_ref, s32[8,5]{1,0:T(8,128)} %nb_ref.1), custom_call_target="tpu_custom_call" | custom-call | flops 2000000000 | bytes 4000000 | tf_op jit(solution)/shard_map/select/pallas_call | solution.py:336
  6.4 1.3 %collective-permute-start.2 = (bf16[256,640]{1,0:T(8,128)(2,1)}, bf16[256,640]{1,0:T(8,128)(2,1)S(1)}, u32[]{:S(2)}, u32[]{:S(2)}) collective-permute-start(bf16[256,640]{1,0:T(8,128)(2,1)} %select.3.plane_ref), channel_id=1, source_target_pairs={{4,0},{8,4},{12,8},{16,12},{20,16},{24,20},{28,24},{5,1},{9,5},{13... | collective-permute-start | bytes 983048 | tf_op jit(solution)/shard_map/ppermute | solution.py:330
  7.7 5.5 %collective-permute-start = (bf16[256,640]{1,0:T(8,128)(2,1)}, bf16[256,640]{1,0:T(8,128)(2,1)S(1)}, u32[]{:S(2)}, u32[]{:S(2)}) collective-permute-start(bf16[256,640]{1,0:T(8,128)(2,1)} %select.3.plane_ref), channel_id=1, source_target_pairs={{0,4},{4,8},{8,12},{12,16},{16,20},{20,24},{24,28},{1,5},{5,9},{9,... | collective-permute-start | bytes 983048 | tf_op jit(solution)/shard_map/ppermute | solution.py:329
  13.3 0.6 all_to_all.8
  13.9 6.2 %all-to-all-start = ((f32[8,4,272]{2,1,0:T(4,128)}), f32[8,4,272]{2,1,0:T(4,128)S(1)}, u32[]{:S(2)}, u32[]{:S(2)}) async-start(f32[8,4,272]{2,1,0:T(4,128)} %all_to_all.8), calls=%async_computation | async-start | bytes 98304 | tf_op jit(solution)/shard_map/all_to_all | solution.py:348
  20.5 2.2 %mul.23.opw_ref = bf16[384,256]{1,0:T(8,128)(2,1)} reshape(bf16[24,16,16,16]{3,2,1,0:T(8,128)(2,1)S(1)} %broadcast_multiply_fusion) | data formatting | bytes 393216 | tf_op jit(solution)/shard_map/mul | solution.py:347
  22.7 4.1 %collective-permute-done.b0_ref.below_ref = bf16[256,640]{1,0:T(8,128)(2,1)S(1)} collective-permute-done((bf16[256,640]{1,0:T(8,128)(2,1)}, bf16[256,640]{1,0:T(8,128)(2,1)S(1)}, u32[]{:S(2)}, u32[]{:S(2)}) %collective-permute-start) | collective-permute-done | bytes 327712 | tf_op jit(solution)/shard_map/ppermute | solution.py:329
  26.9 6.2 %own_model.1 = (f32[32,256]{1,0:T(8,128)}, bf16[1024,512]{1,0:T(8,128)(2,1)}) custom-call(bf16[8,5,128,128]{3,2,1,0:T(8,128)(2,1)} %roots_ref.3, s32[32,16]{1,0:T(8,128)} %copy.21.cols_ref, bf16[256,640]{1,0:T(8,128)(2,1)} %select.3.plane_ref, bf16[1024,384]{1,0:T(8,128)(2,1)} %control_ref.5, bf16[384,256]{1,0:T(8,128)(2,1)} %mul.23.opw_ref), custom_call_target="tpu_custom_call" | custom-call | flops 4000000000 | bytes 4000000 | tf_op jit(solution)/shard_map/own_model/pallas_call | solution.py:358
  33.1 0.7 copy-done.8
  33.8 0.7 copy-done.9
  34.5 6.0 %sides_model.1 = (f32[32,256]{1,0:T(8,128)}, f32[32,256]{1,0:T(8,128)}) custom-call(bf16[256,640]{1,0:T(8,128)(2,1)} %copy-done.7, bf16[256,640]{1,0:T(8,128)(2,1)} %copy-done.9, bf16[256,640]{1,0:T(8,128)(2,1)} %copy-done.6, bf16[256,640]{1,0:T(8,128)(2,1)} %copy-done.8, bf16[1024,384]{1,0:T(8,128)(2,1)} %control_ref.5, bf16[384,256]{1,0:T(8,128)(2,1)} %mul.23.opw_ref), custom_call_target="tpu_custom_call" | custom-call | flops 4000000000 | bytes 4000000 | tf_op jit(solution)/shard_map/sides_model/pallas_call | solution.py:368
  40.5 1.3 %collective-permute-start.4 = (f32[32,256]{1,0:T(8,128)}, f32[32,256]{1,0:T(8,128)S(1)}, u32[]{:S(2)}, u32[]{:S(2)}) collective-permute-start(f32[32,256]{1,0:T(8,128)} %get-tuple-element.10), channel_id=1, source_target_pairs={{4,0},{8,4},{12,8},{16,12},{20,16},{24,20},{28,24},{5,1},{9,5},{13... | collective-permute-start | bytes 98312 | tf_op jit(solution)/shard_map/ppermute | solution.py:330
  41.8 5.1 %collective-permute-start.5 = (f32[32,256]{1,0:T(8,128)}, f32[32,256]{1,0:T(8,128)S(1)}, u32[]{:S(2)}, u32[]{:S(2)}) collective-permute-start(f32[32,256]{1,0:T(8,128)} %get-tuple-element.11), channel_id=1, source_target_pairs={{0,4},{4,8},{8,12},{12,16},{16,20},{20,24},{24,28},{1,5},{5,9},{9,... | collective-permute-start | bytes 98312 | tf_op jit(solution)/shard_map/ppermute | solution.py:329
  47.0 1.7 %collective-permute-done.5 = f32[32,256]{1,0:T(8,128)S(1)} collective-permute-done((f32[32,256]{1,0:T(8,128)}, f32[32,256]{1,0:T(8,128)S(1)}, u32[]{:S(2)}, u32[]{:S(2)}) %collective-permute-start.5) | collective-permute-done | bytes 32800 | tf_op jit(solution)/shard_map/ppermute | solution.py:329
  49.0 1.0 %collective-permute-done.6 = f32[32,256]{1,0:T(8,128)S(1)} collective-permute-done((f32[32,256]{1,0:T(8,128)S(1)}, f32[32,256]{1,0:T(8,128)S(1)}, u32[]{:S(2)}, u32[]{:S(2)}) %collective-permute-start.6) | collective-permute-done | bytes 32800 | tf_op jit(solution)/shard_map/ppermute | solution.py:331
  49.9 1.5 %collective-permute-start.7 = (f32[32,256]{1,0:T(8,128)S(1)}, f32[32,256]{1,0:T(8,128)S(1)}, u32[]{:S(2)}, u32[]{:S(2)}) collective-permute-start(f32[32,256]{1,0:T(8,128)S(1)} %add.25), channel_id=1, source_target_pairs={{0,2},{1,3},{2,0},{3,1},{4,6},{5,7},{6,4},{7,5},{8,10},{9,11},{10,... | collective-permute-start | bytes 98312 | tf_op jit(solution)/shard_map/ppermute | solution.py:331
  51.4 4.9 %sides_turn.1.opt_ref = bf16[1024,1024]{1,0:T(8,128)(2,1)} custom-call(bf16[256,640]{1,0:T(8,128)(2,1)} %copy-done.7, bf16[256,640]{1,0:T(8,128)(2,1)} %copy-done.9, bf16[256,640]{1,0:T(8,128)(2,1)} %copy-done.6, bf16[256,640]{1,0:T(8,128)(2,1)} %copy-done.8), custom_call_target="tpu_custom_call" | custom-call | flops 4000000000 | bytes 4000000 | tf_op jit(solution)/shard_map/sides_turn/pallas_call | solution.py:383
  56.3 1.3 %collective-permute-start.9 = (f32[32,256]{1,0:T(8,128)S(1)}, f32[32,256]{1,0:T(8,128)S(1)}, u32[]{:S(2)}, u32[]{:S(2)}) collective-permute-start(f32[32,256]{1,0:T(8,128)S(1)} %fusion.misfit_ref), channel_id=1, source_target_pairs={{4,0},{8,4},{12,8},{16,12},{20,16},{24,20},{28,24},{5,1},{9,5},{13... | collective-permute-start | bytes 98312 | tf_op jit(solution)/shard_map/ppermute | solution.py:330
  57.6 5.4 %collective-permute-start.8 = (f32[32,256]{1,0:T(8,128)S(1)}, f32[32,256]{1,0:T(8,128)S(1)}, u32[]{:S(2)}, u32[]{:S(2)}) collective-permute-start(f32[32,256]{1,0:T(8,128)S(1)} %fusion.misfit_ref), channel_id=1, source_target_pairs={{0,4},{4,8},{8,12},{12,16},{16,20},{20,24},{24,28},{1,5},{5,9},{9,... | collective-permute-start | bytes 98312 | tf_op jit(solution)/shard_map/ppermute | solution.py:329
  63.1 3.9 %own_adjoint.1.own_ref = f32[1024,384]{1,0:T(8,128)} custom-call(f32[32,256]{1,0:T(8,128)} %copy-done.1, bf16[256,640]{1,0:T(8,128)(2,1)} %select.3.plane_ref, bf16[1024,512]{1,0:T(8,128)(2,1)} %get-tuple-element.12.opt_ref, bf16[1024,384]{1,0:T(8,128)(2,1)} %control_ref.5, bf16[384,256]{1,0:T(8,128)(2,1)} %mul.23.opw_ref), custom_call_target="tpu_custom_call" | custom-call | flops 2000000000 | bytes 4000000 | tf_op jit(solution)/shard_map/own_adjoint/pallas_call | solution.py:390
  67.6 0.6 copy-done.11
  68.2 4.9 %sides_adjoint.1 = bf16[1024,384]{1,0:T(8,128)(2,1)} custom-call(f32[32,256]{1,0:T(8,128)} %copy-done.11, f32[32,256]{1,0:T(8,128)} %copy-done.10, bf16[256,640]{1,0:T(8,128)(2,1)} %copy-done.7, bf16[256,640]{1,0:T(8,128)(2,1)} %copy-done.6, bf16[1024,1024]{1,0:T(8,128)(2,1)} %sides_turn.1.opt_ref, f32[1024,384]{1,0:T(8,128)} %own_adjoint.1.own_ref, ...), custom_call_target="tpu_custom_call" | custom-call | flops 4000000000 | bytes 4000000 | tf_op jit(solution)/shard_map/sides_adjoint/pallas_call | solution.py:398
  (48 shorter events, 1.5 us)
Async XLA Ops:
  2.7 10.4 %copy-start.3 = (f32[32,16]{0,1:T(8,128)S(1)}, f32[32,16]{0,1:T(8,128)}, u32[]{:S(2)}) copy-start(f32[32,16]{0,1:T(8,128)} %param.18) | copy-start | bytes 6148
  2.7 10.5 %copy-start = (f32[32,256]{1,0:T(8,128)S(1)}, f32[32,256]{1,0:T(8,128)}, u32[]{:S(2)}) copy-start(f32[32,256]{1,0:T(8,128)} %param.17) | copy-start | bytes 98308
  2.7 17.3 %copy-start.5 = (s32[1,8]{1,0:T(1,128)S(1)}, s32[1,8]{1,0:T(1,128)}, u32[]{:S(2)}) copy-start(s32[1,8]{1,0:T(1,128)} %param.19) | copy-start | bytes 100
  2.7 17.5 %copy-start.4 = (bf16[24,16]{0,1:T(8,128)(2,1)S(1)}, bf16[24,16]{0,1:T(8,128)(2,1)}, u32[]{:S(2)}) copy-start(bf16[24,16]{0,1:T(8,128)(2,1)} %param.14) | copy-start | bytes 2308
  6.4 16.4 %collective-permute-start.2 = (bf16[256,640]{1,0:T(8,128)(2,1)}, bf16[256,640]{1,0:T(8,128)(2,1)S(1)}, u32[]{:S(2)}, u32[]{:S(2)}) collective-permute-start(bf16[256,640]{1,0:T(8,128)(2,1)} %select.3.plane_ref), channel_id=1, source_target_pairs={{4,0},{8,4},{12,8},{16,12},{20,16},{24,20},{28,24},{5,1},{9,5},{13... | collective-permute-start | bytes 983048 | tf_op jit(solution)/shard_map/ppermute | solution.py:330
  7.7 19.2 %collective-permute-start = (bf16[256,640]{1,0:T(8,128)(2,1)}, bf16[256,640]{1,0:T(8,128)(2,1)S(1)}, u32[]{:S(2)}, u32[]{:S(2)}) collective-permute-start(bf16[256,640]{1,0:T(8,128)(2,1)} %select.3.plane_ref), channel_id=1, source_target_pairs={{0,4},{4,8},{8,12},{12,16},{16,20},{20,24},{24,28},{1,5},{5,9},{9,... | collective-permute-start | bytes 983048 | tf_op jit(solution)/shard_map/ppermute | solution.py:329
  13.9 33.0 %all-to-all-start = ((f32[8,4,272]{2,1,0:T(4,128)}), f32[8,4,272]{2,1,0:T(4,128)S(1)}, u32[]{:S(2)}, u32[]{:S(2)}) async-start(f32[8,4,272]{2,1,0:T(4,128)} %all_to_all.8), calls=%async_computation | async-start | bytes 98304 | tf_op jit(solution)/shard_map/all_to_all | solution.py:348
  22.7 10.3 %copy-start.6 = (bf16[256,640]{1,0:T(8,128)(2,1)}, bf16[256,640]{1,0:T(8,128)(2,1)S(1)}, u32[]{:S(2)}) copy-start(bf16[256,640]{1,0:T(8,128)(2,1)S(1)} %collective-permute-done.2.a0_ref.above_ref) | copy-start | bytes 983044
  22.7 10.3 %collective-permute-start.3 = (bf16[256,640]{1,0:T(8,128)(2,1)S(1)}, bf16[256,640]{1,0:T(8,128)(2,1)S(1)}, u32[]{:S(2)}, u32[]{:S(2)}) collective-permute-start(bf16[256,640]{1,0:T(8,128)(2,1)S(1)} %collective-permute-done.2.a0_ref.above_ref), channel_id=1, source_target_pairs={{0,1},{1,0},{2,3},{3,2},{4,5},{5,4},{6,7},{7,6},{8,9},{9,8},{10,11... | collective-permute-start | bytes 983048 | tf_op jit(solution)/shard_map/ppermute | solution.py:331
  26.9 6.2 %copy-start.7 = (bf16[256,640]{1,0:T(8,128)(2,1)}, bf16[256,640]{1,0:T(8,128)(2,1)S(1)}, u32[]{:S(2)}) copy-start(bf16[256,640]{1,0:T(8,128)(2,1)S(1)} %collective-permute-done.b0_ref.below_ref) | copy-start | bytes 983044
  26.9 6.2 %collective-permute-start.1 = (bf16[256,640]{1,0:T(8,128)(2,1)S(1)}, bf16[256,640]{1,0:T(8,128)(2,1)S(1)}, u32[]{:S(2)}, u32[]{:S(2)}) collective-permute-start(bf16[256,640]{1,0:T(8,128)(2,1)S(1)} %collective-permute-done.b0_ref.below_ref), channel_id=1, source_target_pairs={{0,1},{1,0},{2,3},{3,2},{4,5},{5,4},{6,7},{7,6},{8,9},{9,8},{10,11... | collective-permute-start | bytes 983048 | tf_op jit(solution)/shard_map/ppermute | solution.py:331
  33.0 15.6 %copy-start.2 = (f32[32,256]{1,0:T(8,128)S(1)}, f32[32,256]{1,0:T(8,128)}, u32[]{:S(2)}) copy-start(f32[32,256]{1,0:T(8,128)} %get-tuple-element.9) | copy-start | bytes 98308
  33.1 0.7 %copy-start.8 = (bf16[256,640]{1,0:T(8,128)(2,1)}, bf16[256,640]{1,0:T(8,128)(2,1)S(1)}, u32[]{:S(2)}) copy-start(bf16[256,640]{1,0:T(8,128)(2,1)S(1)} %collective-permute-done.3.a1_ref) | copy-start | bytes 983044
  33.8 0.7 copy-start.9
  40.5 6.4 %collective-permute-start.4 = (f32[32,256]{1,0:T(8,128)}, f32[32,256]{1,0:T(8,128)S(1)}, u32[]{:S(2)}, u32[]{:S(2)}) collective-permute-start(f32[32,256]{1,0:T(8,128)} %get-tuple-element.10), channel_id=1, source_target_pairs={{4,0},{8,4},{12,8},{16,12},{20,16},{24,20},{28,24},{5,1},{9,5},{13... | collective-permute-start | bytes 98312 | tf_op jit(solution)/shard_map/ppermute | solution.py:330
  41.8 6.8 %collective-permute-start.5 = (f32[32,256]{1,0:T(8,128)}, f32[32,256]{1,0:T(8,128)S(1)}, u32[]{:S(2)}, u32[]{:S(2)}) collective-permute-start(f32[32,256]{1,0:T(8,128)} %get-tuple-element.11), channel_id=1, source_target_pairs={{0,4},{4,8},{8,12},{12,16},{16,20},{20,24},{24,28},{1,5},{5,9},{9,... | collective-permute-start | bytes 98312 | tf_op jit(solution)/shard_map/ppermute | solution.py:329
  48.7 1.3 %collective-permute-start.6 = (f32[32,256]{1,0:T(8,128)S(1)}, f32[32,256]{1,0:T(8,128)S(1)}, u32[]{:S(2)}, u32[]{:S(2)}) collective-permute-start(f32[32,256]{1,0:T(8,128)S(1)} %add_add_fusion), channel_id=1, source_target_pairs={{0,1},{1,0},{2,3},{3,2},{4,5},{5,4},{6,7},{7,6},{8,9},{9,8},{10,11... | collective-permute-start | bytes 98312 | tf_op jit(solution)/shard_map/ppermute | solution.py:331
  49.9 6.4 %collective-permute-start.7 = (f32[32,256]{1,0:T(8,128)S(1)}, f32[32,256]{1,0:T(8,128)S(1)}, u32[]{:S(2)}, u32[]{:S(2)}) collective-permute-start(f32[32,256]{1,0:T(8,128)S(1)} %add.25), channel_id=1, source_target_pairs={{0,2},{1,3},{2,0},{3,1},{4,6},{5,7},{6,4},{7,5},{8,10},{9,11},{10,... | collective-permute-start | bytes 98312 | tf_op jit(solution)/shard_map/ppermute | solution.py:331
  56.3 6.8 %copy-start.1 = (f32[32,256]{1,0:T(8,128)}, f32[32,256]{1,0:T(8,128)S(1)}, u32[]{:S(2)}) copy-start(f32[32,256]{1,0:T(8,128)S(1)} %fusion.misfit_ref) | copy-start | bytes 98308
  56.3 10.6 %collective-permute-start.9 = (f32[32,256]{1,0:T(8,128)S(1)}, f32[32,256]{1,0:T(8,128)S(1)}, u32[]{:S(2)}, u32[]{:S(2)}) collective-permute-start(f32[32,256]{1,0:T(8,128)S(1)} %fusion.misfit_ref), channel_id=1, source_target_pairs={{4,0},{8,4},{12,8},{16,12},{20,16},{24,20},{28,24},{5,1},{9,5},{13... | collective-permute-start | bytes 98312 | tf_op jit(solution)/shard_map/ppermute | solution.py:330
  57.6 9.3 %collective-permute-start.8 = (f32[32,256]{1,0:T(8,128)S(1)}, f32[32,256]{1,0:T(8,128)S(1)}, u32[]{:S(2)}, u32[]{:S(2)}) collective-permute-start(f32[32,256]{1,0:T(8,128)S(1)} %fusion.misfit_ref), channel_id=1, source_target_pairs={{0,4},{4,8},{8,12},{12,16},{16,20},{20,24},{24,28},{1,5},{5,9},{9,... | collective-permute-start | bytes 98312 | tf_op jit(solution)/shard_map/ppermute | solution.py:329
  67.0 0.6 copy-start.10
  67.6 0.6 copy-start.11

commit v2 on v1

v2 whole, which is shorter than its diff:
```python
import functools

import jax
import jax.numpy as jnp
from jax import lax
from jax.experimental import pallas as pl
from jax.experimental.pallas import tpu as pltpu
from jax.sharding import PartitionSpec as P

F32 = jnp.float32
BF16 = jnp.bfloat16
LANES = 128
NT = (((1,), (1,)), ((), ()))


def repeat_steps(count, body):
    if count <= 2:
        for step in range(count):
            body(step)
    else:
        lax.fori_loop(0, count, lambda step, carry: (body(step), carry)[1], 0)


def at(step, size):
    if isinstance(step, int):
        return pl.ds(step * size, size)
    return pl.ds(pl.multiple_of(step * size, size), size)


def dot(a, b):
    return jnp.dot(a, b, preferred_element_type=F32)


def dot_nt(a, b):
    return lax.dot_general(a, b, NT, preferred_element_type=F32)


def iota(shape, axis):
    return lax.broadcasted_iota(jnp.int32, shape, axis)


def column(values):
    points, slots = values.shape
    wide = jnp.broadcast_to(values.astype(F32)[:, None, :], (points, slots, slots))
    wide = wide.reshape(points * slots, slots)
    hit = iota(wide.shape, 1) == lax.rem(iota(wide.shape, 0), slots)
    return jnp.sum(jnp.where(hit, wide, 0.0), axis=1, keepdims=True)


def one_hot(cols, count):
    lane = iota((cols.shape[0], count), 1)
    return jnp.where(lane == cols.astype(jnp.int32), 1.0, 0.0).astype(BF16)


def within(value, low, count):
    return (value >= low) & (value < low + count)


def as_bf16(mask):
    return jnp.where(mask, 1.0, 0.0).astype(BF16)


def scale_spread(dims, half):
    shape = (LANES, dims.lanes)
    first = iota(shape, 1) - dims.members * (iota(shape, 0) - dims.vars * half)
    second = first + dims.members * 2 * dims.vars
    return as_bf16(within(first, 0, dims.members) | within(second, 0, dims.members))


def target_spread(dims):
    shape = (LANES, dims.others * dims.block)
    return as_bf16(
        within(iota(shape, 1) - dims.block * (iota(shape, 0) - 4 * dims.vars), 0, dims.block)
    )


def fill_operator(dims, op_ref, targets, parts):
    for q in range(dims.blocks):
        total = None
        for target, part in zip(targets, parts):
            term = jnp.where(target == jnp.asarray(q, target.dtype), part, jnp.zeros((), part.dtype))
            total = term if total is None else total + term
        op_ref[:, q * dims.block : (q + 1) * dims.block] = total


def model_rows(dims, op_ref, plane, spread, control_ref, opw):
    summed = dot(op_ref[...], control_ref[...])
    state = (summed * dot(plane, spread)).astype(BF16)
    bands = dot(state, opw)
    return jnp.sum(bands.reshape(dims.chunk_points, dims.slots, bands.shape[1]), axis=0)


def select_kernel(dims, roots_ref, sigma_ref, sigma2_ref, cols_ref, wgt_ref, nb_ref, out_ref):
    tile = lax.axis_index("space")
    half = lax.rem(lax.axis_index("var"), 2)
    sigma, sigma2 = sigma_ref[...], sigma2_ref[...]
    sigma = jnp.concatenate(
        [jnp.where(half == 0, sigma, sigma2), jnp.where(half == 0, sigma2, sigma)], axis=0
    )
    high = sigma.astype(BF16).astype(F32)
    nb = nb_ref[...] + ((2 * half - 1) - tile) * dims.blocks
    nb = nb.astype(F32)
    base = 4 * dims.vars
    ids = jnp.zeros((LANES - base, dims.columns), F32)
    shape = ids.shape
    for b in range(dims.blocks):
        in_block = within(iota(shape, 1), b * dims.block, dims.block)
        for k in range(dims.others):
            ids = jnp.where(in_block & (iota(shape, 0) == k), nb[b : b + 1, k + 1 : k + 2], ids)
    table = jnp.concatenate([high, sigma - high, ids], axis=0).astype(BF16)
    row, lane = iota((LANES, LANES), 0), iota((LANES, LANES), 1)
    fold = as_bf16(
        (row == lane)
        | ((row < base) & (lane < base) & ((row == lane + base // 2) | (lane == row + base // 2)))
    )
    wide = dims.others * dims.block

    def body(step):
        points = at(step, dims.chunk_points)
        hot = one_hot(column(cols_ref[points, :]), dims.columns)
        plane = dot(dot_nt(hot, table).astype(BF16), fold)
        lanes = iota((dims.chunk, LANES), 1)
        plane = jnp.where(lanes < base, plane * column(wgt_ref[points, :]), plane)
        top = plane.astype(BF16).astype(F32)
        rows = at(step, dims.chunk)
        out_ref[rows, wide:] = jnp.where(
            within(lanes, base // 2, base // 2), plane - top, top
        ).astype(BF16)
        for k in range(0, dims.others, 2):
            pair = range(k, min(k + 2, dims.others))
            root = jnp.concatenate(
                [roots_ref[:, i + 1].reshape(dims.columns, dims.block) for i in pair], axis=1
            )
            out_ref[rows, k * dims.block : (k + len(pair)) * dims.block] = dot(hot, root).astype(BF16)

    repeat_steps(dims.chunks, body)


def own_kernel(
    dims, roots_ref, cols_ref, message_ref, control_ref, obs_ref,
    model_ref, opt_ref, opw_ref, op_ref,
):
    half = lax.rem(lax.axis_index("var"), 2)
    bands = obs_ref.shape[0]
    flat = bands * dims.members
    vars_wide = as_bf16(
        within(iota((dims.lanes, dims.vars), 0) - dims.members * iota((dims.lanes, dims.vars), 1), 0, dims.members)
    )
    bands_wide = as_bf16(
        within(iota((bands, flat), 1) - dims.members * iota((bands, flat), 0), 0, dims.members)
    )
    opw = dot(dot_nt(vars_wide, obs_ref[...]).astype(BF16), bands_wide)
    same = lax.rem(iota(opw.shape, 0), dims.members) == lax.rem(iota(opw.shape, 1), dims.members)
    opw = jnp.where(same, opw, 0.0).astype(BF16)
    opw_ref[...] = opw
    spread, targets_of = scale_spread(dims, half), target_spread(dims)
    root = roots_ref[:, 0].reshape(dims.columns, dims.block)
    shift = ((1 - 2 * half) * dims.blocks).astype(F32)

    def body(step):
        rows = at(step, dims.chunk)
        wide = dims.others * dims.block
        plane = message_ref[rows, wide:]
        cols = column(cols_ref[at(step, dims.chunk_points), :])
        own = jnp.floor(cols * (1.0 / dims.block))
        targets = [jnp.broadcast_to(own, (dims.chunk, dims.block)).astype(BF16)]
        parts = [dot(one_hot(cols, dims.columns), root).astype(BF16)]
        ids = (dot(plane, targets_of) + shift).astype(BF16)
        for k in range(dims.others):
            lanes = slice(k * dims.block, (k + 1) * dims.block)
            targets.append(ids[:, lanes])
            parts.append(message_ref[rows, lanes])
        fill_operator(dims, op_ref, targets, parts)
        model = model_rows(dims, op_ref, plane, spread, control_ref, opw)
        if isinstance(step, int) and step == 0:
            model_ref[...] = model
        else:
            model_ref[...] += model
        opt_ref[:, rows] = op_ref[...].T

    if dims.chunks > 2:
        model_ref[...] = jnp.zeros_like(model_ref)
    repeat_steps(dims.chunks, body)


def side_parts(dims, message_ref, step, targets_of):
    rows = at(step, dims.chunk)
    wide = dims.others * dims.block
    plane = message_ref[rows, wide:]
    ids = dot(plane, targets_of).astype(BF16)
    lanes = [slice(k * dims.block, (k + 1) * dims.block) for k in range(dims.others)]
    return plane, [ids[:, l] for l in lanes], [message_ref[rows, l] for l in lanes]


def sides_kernel(dims, mine_ref, other_ref, own_ref, control_ref, opw_ref, keep_ref, give_ref, op_ref):
    half = lax.rem(lax.axis_index("var"), 2)
    spread, targets_of = scale_spread(dims, half), target_spread(dims)
    opw = opw_ref[...]
    give_ref[dims.slots :, :] = own_ref[...]
    for ref, model_ref in ((mine_ref, keep_ref), (other_ref, give_ref.at[: dims.slots])):

        def body(step):
            plane, targets, parts = side_parts(dims, ref, step, targets_of)
            fill_operator(dims, op_ref, targets, parts)
            model = model_rows(dims, op_ref, plane, spread, control_ref, opw)
            if isinstance(step, int) and step == 0:
                model_ref[...] = model
            else:
                model_ref[...] += model

        if dims.chunks > 2:
            model_ref[...] = jnp.zeros_like(model_ref)
        repeat_steps(dims.chunks, body)


def turn_kernel(dims, mine_ref, other_ref, opt_ref):
    targets_of = target_spread(dims)
    for side, ref in enumerate((mine_ref, other_ref)):

        def body(step):
            _, targets, parts = side_parts(dims, ref, step, targets_of)
            targets = [target.T for target in targets]
            parts = [part.T for part in parts]
            lanes = at(step + side * dims.chunks, dims.chunk)
            for q in range(dims.blocks):
                total = None
                for target, part in zip(targets, parts):
                    term = jnp.where(target == jnp.asarray(q, BF16), part, jnp.zeros((), BF16))
                    total = term if total is None else total + term
                opt_ref[q * dims.block : (q + 1) * dims.block, lanes] = total

        repeat_steps(dims.chunks, body)


def pull_rows(dims, pulled, scale):
    wide = scale.reshape(dims.chunk_points, dims.slots, dims.lanes) * pulled[None]
    return wide.reshape(dims.chunk, dims.lanes).astype(BF16)


def bands_to_vars(misfit, opw):
    high = misfit.astype(BF16)
    rest = misfit - high.astype(F32)
    middle = rest.astype(BF16)
    low = (rest - middle.astype(F32)).astype(BF16)
    return dot_nt(high, opw) + (dot_nt(middle, opw) + dot_nt(low, opw))


def own_adjoint_kernel(dims, misfit_ref, plane_ref, opt_ref, control_ref, opw_ref, out_ref, adj_ref):
    half = lax.rem(lax.axis_index("var"), 2)
    spread = scale_spread(dims, half)
    pulled = bands_to_vars(misfit_ref[...], opw_ref[...])

    def body(step):
        rows = at(step, dims.chunk)
        adj_ref[rows, :] = pull_rows(dims, pulled, dot(plane_ref[rows, :], spread))

    repeat_steps(dims.chunks, body)
    for part in range(dims.columns // 256):
        rows = slice(part * 256, (part + 1) * 256)
        out_ref[rows, :] = control_ref[rows, :].astype(F32) + dot(opt_ref[rows, :], adj_ref[...])


def sides_adjoint_kernel(
    dims, misfit_ref, misfit2_ref, mine_ref, other_ref, opt_ref, own_ref, opw_ref, out_ref, adj_ref
):
    half = lax.rem(lax.axis_index("var"), 2)
    spread = scale_spread(dims, half)
    for side, (values_ref, ref) in enumerate(((misfit_ref, mine_ref), (misfit2_ref, other_ref))):
        pulled = bands_to_vars(values_ref[...], opw_ref[...])

        def body(step):
            scale = dot(ref[at(step, dims.chunk), :], spread)
            adj_ref[at(step + side * dims.chunks, dims.chunk), :] = pull_rows(dims, pulled, scale)

        repeat_steps(dims.chunks, body)
    for part in range(dims.columns // 256):
        rows = slice(part * 256, (part + 1) * 256)
        total = own_ref[rows, :] + dot(opt_ref[rows, :], adj_ref[...])
        out_ref[rows, :] = total.astype(BF16)


class Dims:
    def __init__(self, control, roots, sigma, foot_cols):
        self.blocks, links, self.block = roots.shape[:3]
        self.others = links - 1
        self.columns, self.lanes = control.shape
        self.vars = sigma.shape[0]
        self.members = self.lanes // self.vars
        self.slots, self.points = foot_cols.shape
        self.rows = self.slots * self.points
        self.chunk_points = min(self.points, max(8, 512 // self.slots))
        self.chunk = self.chunk_points * self.slots
        self.chunks = self.rows // self.chunk
        self.width = self.others * self.block + LANES


def whole(array):
    return pl.BlockSpec(array.shape, lambda i, n=len(array.shape): (0,) * n)


def call(kernel, name, out_shape, scratch, flops, in_specs=None):
    specs = {}
    if in_specs is not None:
        specs = {"in_specs": in_specs, "grid": (1,), "out_specs": jax.tree.map(whole, out_shape)}
    return pl.pallas_call(
        kernel,
        out_shape=out_shape,
        scratch_shapes=scratch,
        compiler_params=pltpu.CompilerParams(vmem_limit_bytes=56 * 1024 * 1024),
        cost_estimate=pl.CostEstimate(flops=flops, bytes_accessed=4000000, transcendentals=0),
        name=name,
        **specs,
    )


def shards(
    control,
    roots,
    neighbours,
    sigma,
    obs_op,
    foot_cols,
    foot_wgt,
    obs_value,
    obs_rinv,
    owner_counts,
):
    dims = Dims(control, roots, sigma, foot_cols)
    bands = obs_op.shape[1]
    members = dims.members
    tiles = lax.axis_size("space")
    ranks = lax.axis_size("var")
    outward, inward = [], []
    for t in range(tiles):
        for v in range(ranks):
            to = t + 1 - 2 * (v % 2)
            if 0 <= to < tiles:
                outward.append((t * ranks + v, to * ranks + v))
                inward.append((to * ranks + v, t * ranks + v))
    hop = lambda x, pairs: lax.ppermute(x, ("space", "var"), pairs)
    swap = lambda x, bit: lax.ppermute(x, "var", [(i, i ^ bit) for i in range(ranks)])
    shape = jax.ShapeDtypeStruct
    flat = bands * members
    cols_t, wgt_t = foot_cols.T, foot_wgt.T

    message = call(
        functools.partial(select_kernel, dims),
        "select",
        shape((dims.rows, dims.width), BF16),
        [],
        2000000000,
    )(roots, sigma, swap(sigma, 1), cols_t, wgt_t, neighbours)
    mine = hop(message, outward)

    message, obs_value, obs_rinv = lax.optimization_barrier((message, obs_value, obs_rinv))
    observed = lax.all_to_all(
        jnp.concatenate([obs_value, obs_rinv], axis=1), "space", 0, 0, tiled=True
    )
    capacity = dims.slots // owner_counts.shape[1]
    slot_ids = jnp.arange(dims.slots, dtype=jnp.int32)
    live = slot_ids % capacity < jnp.repeat(owner_counts[0], capacity)
    rinv = jnp.repeat(jnp.where(live[:, None], observed[:, flat:], 0.0), members, axis=1)
    value = observed[:, :flat]

    own_model, own_opt, opw = call(
        functools.partial(own_kernel, dims),
        "own_model",
        (
            shape((dims.slots, flat), F32),
            shape((dims.columns, dims.rows), BF16),
            shape((dims.lanes, flat), BF16),
        ),
        [pltpu.VMEM((dims.chunk, dims.columns), BF16)],
        4000000000,
    )(roots, cols_t, message, control, obs_op.T)

    mine, own_model, own_opt, rinv, value = lax.optimization_barrier(
        (mine, own_model, own_opt, rinv, value)
    )
    other = swap(mine, 1)
    keep, give = call(
        functools.partial(sides_kernel, dims),
        "sides_model",
        (shape((dims.slots, flat), F32), shape((2 * dims.slots, flat), F32)),
        [pltpu.VMEM((dims.chunk, dims.columns), BF16)],
        4000000000,
    )(mine, other, own_model, control, opw)
    got = swap(give, 1)
    arrived = hop(keep + got[: dims.slots], inward)
    sides_opt = call(
        functools.partial(turn_kernel, dims),
        "sides_turn",
        shape((dims.columns, 2 * dims.rows), BF16),
        [],
        4000000000,
    )(mine, other)
    arrived, sides_opt = lax.optimization_barrier((arrived, sides_opt))
    modelled = own_model + got[dims.slots :] + arrived + swap(arrived, 1)
    bit = 2
    while bit < ranks:
        modelled = modelled + swap(modelled, bit)
        bit *= 2
    misfit = rinv * (modelled - value)
    misfit_mine = hop(misfit, outward)

    plane = pl.BlockSpec((dims.rows, LANES), lambda i: (0, dims.others * dims.block // LANES))
    own_total = call(
        functools.partial(own_adjoint_kernel, dims),
        "own_adjoint",
        shape((dims.columns, dims.lanes), F32),
        [pltpu.VMEM((dims.rows, dims.lanes), BF16)],
        2000000000,
        [whole(misfit), plane, whole(own_opt), whole(control), whole(opw)],
    )(misfit, message, own_opt, control, opw)
    misfit_mine, own_total = lax.optimization_barrier((misfit_mine, own_total))
    misfit_other = swap(misfit_mine, 1)
    return call(
        functools.partial(sides_adjoint_kernel, dims),
        "sides_adjoint",
        shape((dims.columns, dims.lanes), BF16),
        [pltpu.VMEM((2 * dims.rows, dims.lanes), BF16)],
        4000000000,
        [whole(misfit)] * 2 + [plane] * 2 + [whole(sides_opt), whole(own_total), whole(opw)],
    )(misfit_mine, misfit_other, mine, other, sides_opt, own_total, opw)


def solution(mesh):
    return jax.shard_map(
        shards,
        mesh=mesh,
        in_specs=(
            P("space", "var"),
            P("space", None, None, None),
            P("space", None),
            P("var", "space"),
            P("var", None),
            P("space", None),
            P("space", None),
            P("space", None),
            P("space", None),
            P("space", None),
        ),
        out_specs=P("space", "var"),
        check_vma=False,
    )
```

time: 74.4 us -> 64.6 us (0.87)
  starting transfers between devices: 27.7 us -> 18.5 us
  waiting for transfers between devices: 6.77 us -> 14.3 us
  local copies, waits for them, and re-layouts: 8.71 us -> 3.81 us
  Pallas kernels: 29.5 us -> 26.4 us
    ppermute x6 -> x3, starting transfers between devices: 19.9 us -> 9.22 us  [shards(): hop = lambda x, pairs: lax.ppermute(x, ('space', 'var'), pairs)]
    ppermute x4 -> x6, waiting for transfers between devices: 0.97 us -> 8.14 us  [shards(): lax.ppermute(x, 'var', [(i, i ^ bit) for i in range(ranks)])]
    all_to_all x1, waiting for transfers between devices: 0.01 us -> 5.4 us  [shards(): lax.all_to_all(jnp.concatenate([obs_value, obs_rinv], axis=1), 'space', 0...]
    ppermute x6 -> x3, waiting for transfers between devices: 5.79 us -> 0.81 us  [shards(): hop = lambda x, pairs: lax.ppermute(x, ('space', 'var'), pairs)]
    unnamed x28 -> x20, local copies, waits for them, and re-layouts: 5.57 us -> 2.12 us
    ppermute x4 -> x6, starting transfers between devices: 1.56 us -> 4.4 us  [shards(): lax.ppermute(x, 'var', [(i, i ^ bit) for i in range(ranks)])]
    mul x1 -> x0, local copies, waits for them, and re-layouts: 2.19 us -> none  [shards(): obs_op[:, None, :, None] * identity_m[None, :, None, :]]
    all_to_all x1, starting transfers between devices: 6.19 us -> 4.84 us  [shards(): lax.all_to_all(jnp.concatenate([obs_value, obs_rinv], axis=1), 'space', 0...]
  transfers between devices with their start and end apart: 11 -> 10, of which waited for: 3 -> 8; matrix products, arithmetic and copies ran while one was open for 4% -> 2% of each run, Pallas kernels for 29% -> 20%
where the time goes in v2:
time: 64.6 us; the launch traced here: 64 us
  Pallas kernels  26.4 us (41%)
  starting transfers between devices  18.5 us (29%)
  waiting for transfers between devices  14.3 us (22%)
  local copies, waits for them, and re-layouts  3.81 us (6%)
  other arithmetic  0.87 us (1%)
    ppermute x3, starting transfers between devices, shards(): hop = lambda x, pairs: lax.ppermute(x, ('space', 'var'), pairs)  9.22 us
    ppermute x6, waiting for transfers between devices, shards(): lax.ppermute(x, 'var', [(i, i ^ bit) for i in range(ranks)])  8.14 us
    all_to_all x1, waiting for transfers between devices, shards(): lax.all_to_all(jnp.concatenate([obs_value, obs_rinv], axis=1), 'space', 0...  5.4 us
    pallas_call x1, Pallas kernels, shards(): call(functools.partial(sides_kernel, dims), 'sides_model', (shape((dims.s...  5.17 us
    pallas_call x1, Pallas kernels, shards(): call(functools.partial(sides_adjoint_kernel, dims), 'sides_adjoint', shap...  4.89 us
    pallas_call x1, Pallas kernels, shards(): call(functools.partial(own_kernel, dims), 'own_model', (shape((dims.slots...  4.87 us
    all_to_all x1, starting transfers between devices, shards(): lax.all_to_all(jnp.concatenate([obs_value, obs_rinv], axis=1), 'space', 0...  4.84 us
    ppermute x6, starting transfers between devices, shards(): lax.ppermute(x, 'var', [(i, i ^ bit) for i in range(ranks)])  4.4 us
  transfers between devices with their start and end apart: 10, of which 8 were waited for; matrix products, arithmetic and copies ran while one was open for 2% of the time, Pallas kernels for 20%

profile of v2, /device:TPU:0, one launch (start us, length us, event | category | flops | bytes accessed | tf_op | source)
XLA Modules:
  0.0 64.0 jit_solution(3106265605732105454)
XLA Ops:
  0.5 0.7 %broadcast_in_dim.19 = s32[8,4]{1,0:T(8,128)S(1)} broadcast(s32[8]{0:T(128)} %bitcast.6), dimensions={0} | broadcast | bytes 160 | tf_op jit(solution)/shard_map/broadcast_in_dim | solution.py:361
  1.6 0.6 copy-done.7
  2.3 3.5 %select.3.message_ref.plane_ref = bf16[512,640]{1,0:T(8,128)(2,1)} custom-call(bf16[8,5,128,128]{3,2,1,0:T(8,128)(2,1)} %roots_ref.3, f32[24,1024]{1,0:T(8,128)} %sigma_ref.1, f32[24,1024]{1,0:T(8,128)} %copy-done.7, s32[16,32]{1,0:T(8,128)} %bitcast.8, f32[16,32]{1,0:T(8,128)} %bitcast.7, s32[8,5]{1,0:T(8,128)} %nb_ref.1), custom_call_target="tpu_custom_call" | custom-call | flops 2000000000 | bytes 4000000 | tf_op jit(solution)/shard_map/select/pallas_call | solution.py:346
  5.8 4.8 %collective-permute-start.1 = (bf16[512,640]{1,0:T(8,128)(2,1)}, bf16[512,640]{1,0:T(8,128)(2,1)S(1)}, u32[]{:S(2)}, u32[]{:S(2)}) collective-permute-start(bf16[512,640]{1,0:T(8,128)(2,1)} %select.3.message_ref.plane_ref), channel_id=1, source_target_pairs={{0,4},{2,6},{4,8},{5,1},{6,10},{7,3},{8,12},{9,5},{10,14},{11,7},{... | collective-permute-start | bytes 1966088 | tf_op jit(solution)/shard_map/ppermute | solution.py:340
  10.7 0.6 all_to_all.8
  11.3 4.8 %all-to-all-start = ((f32[8,4,272]{2,1,0:T(4,128)}), f32[8,4,272]{2,1,0:T(4,128)S(1)}, u32[]{:S(2)}, u32[]{:S(2)}) async-start(f32[8,4,272]{2,1,0:T(4,128)} %all_to_all.8), calls=%async_computation | async-start | bytes 98304 | tf_op jit(solution)/shard_map/all_to_all | solution.py:356
  16.2 4.9 %own_model.1 = (f32[32,256]{1,0:T(8,128)}, bf16[1024,512]{1,0:T(8,128)(2,1)}, bf16[384,256]{1,0:T(8,128)(2,1)}) custom-call(bf16[8,5,128,128]{3,2,1,0:T(8,128)(2,1)} %roots_ref.3, s32[16,32]{1,0:T(8,128)} %bitcast.9, bf16[512,640]{1,0:T(8,128)(2,1)} %select.3.message_ref.plane_ref, bf16[1024,384]{1,0:T(8,128)(2,1)} %control_ref.5, bf16[16,24]{1,0:T(8,128)(2,1)} %bitcast.10), custom_call_target="tpu_custom_call" | custom-call | flops 4000000000 | bytes 4000000 | tf_op jit(solution)/shard_map/own_model/pallas_call | solution.py:365
  21.0 5.4 %all-to-all-done = f32[8,4,272]{2,1,0:T(4,128)S(1)} async-done(((f32[8,4,272]{2,1,0:T(4,128)}), f32[8,4,272]{2,1,0:T(4,128)S(1)}, u32[]{:S(2)}, u32[]{:S(2)}) %all-to-all-start) | async-done | bytes 34848 | tf_op jit(solution)/shard_map/all_to_all | solution.py:356
  26.7 2.1 %collective-permute-done.2.other_ref = bf16[512,640]{1,0:T(8,128)(2,1)S(1)} collective-permute-done((bf16[512,640]{1,0:T(8,128)(2,1)S(1)}, bf16[512,640]{1,0:T(8,128)(2,1)S(1)}, u32[]{:S(2)}, u32[]{:S(2)}) %collective-permute-start.2) | collective-permute-done | bytes 655392 | tf_op jit(solution)/shard_map/ppermute | solution.py:341
  28.8 0.8 %copy-done.6 = bf16[512,640]{1,0:T(8,128)(2,1)} copy-done((bf16[512,640]{1,0:T(8,128)(2,1)}, bf16[512,640]{1,0:T(8,128)(2,1)S(1)}, u32[]{:S(2)}) %copy-start.6) | copy-done | bytes 655384
  29.6 5.2 %sides_model.1 = (f32[32,256]{1,0:T(8,128)}, f32[64,256]{1,0:T(8,128)}) custom-call(bf16[512,640]{1,0:T(8,128)(2,1)} %copy-done.5, bf16[512,640]{1,0:T(8,128)(2,1)} %copy-done.6, f32[32,256]{1,0:T(8,128)} %get-tuple-element.28.own_ref, bf16[1024,384]{1,0:T(8,128)(2,1)} %control_ref.5, bf16[384,256]{1,0:T(8,128)(2,1)} %get-tuple-element.30.opw_ref), custom_call_target="tpu_custom_call" | custom-call | flops 4000000000 | bytes 4000000 | tf_op jit(solution)/shard_map/sides_model/pallas_call | solution.py:381
  35.0 1.3 %collective-permute-done.3 = f32[64,256]{1,0:T(8,128)S(1)} collective-permute-done((f32[64,256]{1,0:T(8,128)}, f32[64,256]{1,0:T(8,128)S(1)}, u32[]{:S(2)}, u32[]{:S(2)}) %collective-permute-start.3) | collective-permute-done | bytes 65568 | tf_op jit(solution)/shard_map/ppermute | solution.py:341
  36.3 0.8 %slice_add_fusion = f32[32,256]{1,0:T(8,128)S(1)} fusion(f32[32,256]{1,0:T(8,128)} %get-tuple-element.32, f32[64,256]{1,0:T(8,128)S(1)} %collective-permute-done.3), kind=kLoop, calls=%fused_computation.1 | loop fusion | flops 8192 | bytes 98304 | tf_op jit(solution)/shard_map/add | solution.py:389
  37.1 1.4 %collective-permute-start.4 = (f32[32,256]{1,0:T(8,128)S(1)}, f32[32,256]{1,0:T(8,128)S(1)}, u32[]{:S(2)}, u32[]{:S(2)}) collective-permute-start(f32[32,256]{1,0:T(8,128)S(1)} %slice_add_fusion), channel_id=1, source_target_pairs={{4,0},{6,2},{8,4},{1,5},{10,6},{3,7},{12,8},{5,9},{14,10},{7,11},{... | collective-permute-start | bytes 98312 | tf_op jit(solution)/shard_map/ppermute | solution.py:340
  38.5 4.1 %sides_turn.1.opt_ref = bf16[1024,1024]{1,0:T(8,128)(2,1)} custom-call(bf16[512,640]{1,0:T(8,128)(2,1)} %copy-done.5, bf16[512,640]{1,0:T(8,128)(2,1)} %copy-done.6), custom_call_target="tpu_custom_call" | custom-call | flops 4000000000 | bytes 4000000 | tf_op jit(solution)/shard_map/sides_turn/pallas_call | solution.py:390
  42.6 0.8 %collective-permute-done.4 = f32[32,256]{1,0:T(8,128)S(1)} collective-permute-done((f32[32,256]{1,0:T(8,128)S(1)}, f32[32,256]{1,0:T(8,128)S(1)}, u32[]{:S(2)}, u32[]{:S(2)}) %collective-permute-start.4) | collective-permute-done | bytes 32800 | tf_op jit(solution)/shard_map/ppermute | solution.py:340
  43.4 2.1 %collective-permute-start.5 = (f32[32,256]{1,0:T(8,128)S(1)}, f32[32,256]{1,0:T(8,128)S(1)}, u32[]{:S(2)}, u32[]{:S(2)}) collective-permute-start(f32[32,256]{1,0:T(8,128)S(1)} %collective-permute-done.4), channel_id=1, source_target_pairs={{0,1},{1,0},{2,3},{3,2},{4,5},{5,4},{6,7},{7,6},{8,9},{9,8},{10,11... | collective-permute-start | bytes 98312 | tf_op jit(solution)/shard_map/ppermute | solution.py:341
  45.6 0.9 %collective-permute-done.5 = f32[32,256]{1,0:T(8,128)S(1)} collective-permute-done((f32[32,256]{1,0:T(8,128)S(1)}, f32[32,256]{1,0:T(8,128)S(1)}, u32[]{:S(2)}, u32[]{:S(2)}) %collective-permute-start.5) | collective-permute-done | bytes 32800 | tf_op jit(solution)/shard_map/ppermute | solution.py:341
  46.4 1.6 %collective-permute-start.6 = (f32[32,256]{1,0:T(8,128)S(1)}, f32[32,256]{1,0:T(8,128)S(1)}, u32[]{:S(2)}, u32[]{:S(2)}) collective-permute-start(f32[32,256]{1,0:T(8,128)S(1)} %fusion.1), channel_id=1, source_target_pairs={{0,2},{1,3},{2,0},{3,1},{4,6},{5,7},{6,4},{7,5},{8,10},{9,11},{10,... | collective-permute-start | bytes 98312 | tf_op jit(solution)/shard_map/ppermute | solution.py:341
  48.1 2.3 %collective-permute-done.6 = f32[32,256]{1,0:T(8,128)S(1)} collective-permute-done((f32[32,256]{1,0:T(8,128)S(1)}, f32[32,256]{1,0:T(8,128)S(1)}, u32[]{:S(2)}, u32[]{:S(2)}) %collective-permute-start.6) | collective-permute-done | bytes 32800 | tf_op jit(solution)/shard_map/ppermute | solution.py:341
  50.4 3.0 %collective-permute-start.7 = (f32[32,256]{1,0:T(8,128)S(1)}, f32[32,256]{1,0:T(8,128)S(1)}, u32[]{:S(2)}, u32[]{:S(2)}) collective-permute-start(f32[32,256]{1,0:T(8,128)S(1)} %subtract_multiply_fusion.misfit_ref), channel_id=1, source_target_pairs={{0,4},{2,6},{4,8},{5,1},{6,10},{7,3},{8,12},{9,5},{10,14},{11,7},{... | collective-permute-start | bytes 98312 | tf_op jit(solution)/shard_map/ppermute | solution.py:340
  53.5 3.8 %own_adjoint.1.own_ref = f32[1024,384]{1,0:T(8,128)} custom-call(f32[32,256]{1,0:T(8,128)} %copy-done.3, bf16[512,640]{1,0:T(8,128)(2,1)} %select.3.message_ref.plane_ref, bf16[1024,512]{1,0:T(8,128)(2,1)} %get-tuple-element.35.opt_ref, bf16[1024,384]{1,0:T(8,128)(2,1)} %control_ref.5, bf16[384,256]{1,0:T(8,128)(2,1)} %get-tuple-element.30.opw_ref), custom_call_target="tpu_custom_call" | custom-call | flops 2000000000 | bytes 4000000 | tf_op jit(solution)/shard_map/own_adjoint/pallas_call | solution.py:407
  57.3 1.2 %collective-permute-done.8.misfit2_ref = f32[32,256]{1,0:T(8,128)S(1)} collective-permute-done((f32[32,256]{1,0:T(8,128)S(1)}, f32[32,256]{1,0:T(8,128)S(1)}, u32[]{:S(2)}, u32[]{:S(2)}) %collective-permute-start.8) | collective-permute-done | bytes 32800 | tf_op jit(solution)/shard_map/ppermute | solution.py:341
  59.1 4.9 %sides_adjoint.1 = bf16[1024,384]{1,0:T(8,128)(2,1)} custom-call(f32[32,256]{1,0:T(8,128)} %copy-done.8, f32[32,256]{1,0:T(8,128)} %copy-done.9, bf16[512,640]{1,0:T(8,128)(2,1)} %copy-done.5, bf16[512,640]{1,0:T(8,128)(2,1)} %copy-done.6, bf16[1024,1024]{1,0:T(8,128)(2,1)} %sides_turn.1.opt_ref, f32[1024,384]{1,0:T(8,128)} %own_adjoint.1.own_ref, ...), custom_call_target="tpu_custom_call" | custom-call | flops 4000000000 | bytes 4000000 | tf_op jit(solution)/shard_map/sides_adjoint/pallas_call | solution.py:417
  (38 shorter events, 2.1 us)
Async XLA Ops:
  0.0 1.6 %collective-permute-start = (f32[24,1024]{1,0:T(8,128)}, f32[24,1024]{1,0:T(8,128)S(1)}, u32[]{:S(2)}, u32[]{:S(2)}) collective-permute-start(f32[24,1024]{1,0:T(8,128)} %sigma_ref.1), channel_id=1, source_target_pairs={{0,1},{1,0},{2,3},{3,2},{4,5},{5,4},{6,7},{7,6},{8,9},{9,8},{10,11... | collective-permute-start | bytes 294920 | tf_op jit(solution)/shard_map/ppermute | solution.py:341
  1.6 0.6 %copy-start.7 = (f32[24,1024]{1,0:T(8,128)}, f32[24,1024]{1,0:T(8,128)S(1)}, u32[]{:S(2)}) copy-start(f32[24,1024]{1,0:T(8,128)S(1)} %collective-permute-done.sigma2_ref) | copy-start | bytes 294916
  2.2 8.3 %copy-start.4 = (f32[32,16]{0,1:T(8,128)S(1)}, f32[32,16]{0,1:T(8,128)}, u32[]{:S(2)}) copy-start(f32[32,16]{0,1:T(8,128)} %param.18) | copy-start | bytes 6148
  2.3 8.4 %copy-start.1 = (f32[32,256]{1,0:T(8,128)S(1)}, f32[32,256]{1,0:T(8,128)}, u32[]{:S(2)}) copy-start(f32[32,256]{1,0:T(8,128)} %param.17) | copy-start | bytes 98308
  5.8 20.8 %collective-permute-start.1 = (bf16[512,640]{1,0:T(8,128)(2,1)}, bf16[512,640]{1,0:T(8,128)(2,1)S(1)}, u32[]{:S(2)}, u32[]{:S(2)}) collective-permute-start(bf16[512,640]{1,0:T(8,128)(2,1)} %select.3.message_ref.plane_ref), channel_id=1, source_target_pairs={{0,4},{2,6},{4,8},{5,1},{6,10},{7,3},{8,12},{9,5},{10,14},{11,7},{... | collective-permute-start | bytes 1966088 | tf_op jit(solution)/shard_map/ppermute | solution.py:340
  11.3 15.1 %all-to-all-start = ((f32[8,4,272]{2,1,0:T(4,128)}), f32[8,4,272]{2,1,0:T(4,128)S(1)}, u32[]{:S(2)}, u32[]{:S(2)}) async-start(f32[8,4,272]{2,1,0:T(4,128)} %all_to_all.8), calls=%async_computation | async-start | bytes 98304 | tf_op jit(solution)/shard_map/all_to_all | solution.py:356
  26.4 8.4 %copy-start = (f32[32,272]{1,0:T(8,128)}, f32[32,272]{1,0:T(8,128)S(1)}, u32[]{:S(2)}) copy-start(f32[32,272]{1,0:T(8,128)S(1)} %all_to_all.10) | copy-start | bytes 104452
  26.6 2.2 %copy-start.5 = (bf16[512,640]{1,0:T(8,128)(2,1)}, bf16[512,640]{1,0:T(8,128)(2,1)S(1)}, u32[]{:S(2)}) copy-start(bf16[512,640]{1,0:T(8,128)(2,1)S(1)} %collective-permute-done.1.mine_ref) | copy-start | bytes 1966084
  26.6 2.2 %collective-permute-start.2 = (bf16[512,640]{1,0:T(8,128)(2,1)S(1)}, bf16[512,640]{1,0:T(8,128)(2,1)S(1)}, u32[]{:S(2)}, u32[]{:S(2)}) collective-permute-start(bf16[512,640]{1,0:T(8,128)(2,1)S(1)} %collective-permute-done.1.mine_ref), channel_id=1, source_target_pairs={{0,1},{1,0},{2,3},{3,2},{4,5},{5,4},{6,7},{7,6},{8,9},{9,8},{10,11... | collective-permute-start | bytes 1966088 | tf_op jit(solution)/shard_map/ppermute | solution.py:341
  28.8 0.9 %copy-start.6 = (bf16[512,640]{1,0:T(8,128)(2,1)}, bf16[512,640]{1,0:T(8,128)(2,1)S(1)}, u32[]{:S(2)}) copy-start(bf16[512,640]{1,0:T(8,128)(2,1)S(1)} %collective-permute-done.2.other_ref) | copy-start | bytes 1966084
  34.8 1.5 %collective-permute-start.3 = (f32[64,256]{1,0:T(8,128)}, f32[64,256]{1,0:T(8,128)S(1)}, u32[]{:S(2)}, u32[]{:S(2)}) collective-permute-start(f32[64,256]{1,0:T(8,128)} %get-tuple-element.31), channel_id=1, source_target_pairs={{0,1},{1,0},{2,3},{3,2},{4,5},{5,4},{6,7},{7,6},{8,9},{9,8},{10,11... | collective-permute-start | bytes 196616 | tf_op jit(solution)/shard_map/ppermute | solution.py:341
  37.0 9.4 %copy-start.2 = (f32[32,256]{1,0:T(8,128)S(1)}, f32[32,256]{1,0:T(8,128)}, u32[]{:S(2)}) copy-start(f32[32,256]{1,0:T(8,128)} %get-tuple-element.28.own_ref) | copy-start | bytes 98308
  37.0 13.4 %slice-start = ((f32[32,272]{1,0:T(8,128)}), f32[32,256]{1,0:T(8,128)S(1)}, s32[]{:S(2)}) async-start(f32[32,272]{1,0:T(8,128)} %copy-done), calls=%async_computation.1 | async-start | bytes 65536 | tf_op jit(solution)/shard_map/slice | solution.py:363
  37.1 6.4 %collective-permute-start.4 = (f32[32,256]{1,0:T(8,128)S(1)}, f32[32,256]{1,0:T(8,128)S(1)}, u32[]{:S(2)}, u32[]{:S(2)}) collective-permute-start(f32[32,256]{1,0:T(8,128)S(1)} %slice_add_fusion), channel_id=1, source_target_pairs={{4,0},{6,2},{8,4},{1,5},{10,6},{3,7},{12,8},{5,9},{14,10},{7,11},{... | collective-permute-start | bytes 98312 | tf_op jit(solution)/shard_map/ppermute | solution.py:340
  43.4 3.0 %collective-permute-start.5 = (f32[32,256]{1,0:T(8,128)S(1)}, f32[32,256]{1,0:T(8,128)S(1)}, u32[]{:S(2)}, u32[]{:S(2)}) collective-permute-start(f32[32,256]{1,0:T(8,128)S(1)} %collective-permute-done.4), channel_id=1, source_target_pairs={{0,1},{1,0},{2,3},{3,2},{4,5},{5,4},{6,7},{7,6},{8,9},{9,8},{10,11... | collective-permute-start | bytes 98312 | tf_op jit(solution)/shard_map/ppermute | solution.py:341
  46.4 4.0 %collective-permute-start.6 = (f32[32,256]{1,0:T(8,128)S(1)}, f32[32,256]{1,0:T(8,128)S(1)}, u32[]{:S(2)}, u32[]{:S(2)}) collective-permute-start(f32[32,256]{1,0:T(8,128)S(1)} %fusion.1), channel_id=1, source_target_pairs={{0,2},{1,3},{2,0},{3,1},{4,6},{5,7},{6,4},{7,5},{8,10},{9,11},{10,... | collective-permute-start | bytes 98312 | tf_op jit(solution)/shard_map/ppermute | solution.py:341
  50.4 3.0 %copy-start.3 = (f32[32,256]{1,0:T(8,128)}, f32[32,256]{1,0:T(8,128)S(1)}, u32[]{:S(2)}) copy-start(f32[32,256]{1,0:T(8,128)S(1)} %subtract_multiply_fusion.misfit_ref) | copy-start | bytes 98308
  50.4 6.9 %collective-permute-start.7 = (f32[32,256]{1,0:T(8,128)S(1)}, f32[32,256]{1,0:T(8,128)S(1)}, u32[]{:S(2)}, u32[]{:S(2)}) collective-permute-start(f32[32,256]{1,0:T(8,128)S(1)} %subtract_multiply_fusion.misfit_ref), channel_id=1, source_target_pairs={{0,4},{2,6},{4,8},{5,1},{6,10},{7,3},{8,12},{9,5},{10,14},{11,7},{... | collective-permute-start | bytes 98312 | tf_op jit(solution)/shard_map/ppermute | solution.py:340
  57.3 1.2 %copy-start.8 = (f32[32,256]{1,0:T(8,128)}, f32[32,256]{1,0:T(8,128)S(1)}, u32[]{:S(2)}) copy-start(f32[32,256]{1,0:T(8,128)S(1)} %collective-permute-done.7.misfit_ref) | copy-start | bytes 98308
  57.3 1.2 %collective-permute-start.8 = (f32[32,256]{1,0:T(8,128)S(1)}, f32[32,256]{1,0:T(8,128)S(1)}, u32[]{:S(2)}, u32[]{:S(2)}) collective-permute-start(f32[32,256]{1,0:T(8,128)S(1)} %collective-permute-done.7.misfit_ref), channel_id=1, source_target_pairs={{0,1},{1,0},{2,3},{3,2},{4,5},{5,4},{6,7},{7,6},{8,9},{9,8},{10,11... | collective-permute-start | bytes 98312 | tf_op jit(solution)/shard_map/ppermute | solution.py:341
  58.5 0.6 copy-start.9

commit v3 on v2

--- a/solution.py
+++ b/solution.py
@@ -252,7 +252,8 @@
 
     def body(step):
         rows = at(step, dims.chunk)
-        adj_ref[rows, :] = pull_rows(dims, pulled, dot(plane_ref[rows, :], spread))
+        plane = plane_ref[rows, dims.others * dims.block :]
+        adj_ref[rows, :] = pull_rows(dims, pulled, dot(plane, spread))
 
     repeat_steps(dims.chunks, body)
     for part in range(dims.columns // 256):
@@ -269,7 +270,7 @@
         pulled = bands_to_vars(values_ref[...], opw_ref[...])
 
         def body(step):
-            scale = dot(ref[at(step, dims.chunk), :], spread)
+            scale = dot(ref[at(step, dims.chunk), dims.others * dims.block :], spread)
             adj_ref[at(step + side * dims.chunks, dims.chunk), :] = pull_rows(dims, pulled, scale)
 
         repeat_steps(dims.chunks, body)
@@ -294,22 +295,15 @@
         self.width = self.others * self.block + LANES
 
 
-def whole(array):
-    return pl.BlockSpec(array.shape, lambda i, n=len(array.shape): (0,) * n)
-
-
-def call(kernel, name, out_shape, scratch, flops, in_specs=None):
-    specs = {}
-    if in_specs is not None:
-        specs = {"in_specs": in_specs, "grid": (1,), "out_specs": jax.tree.map(whole, out_shape)}
+def call(dims, kernel, name, out_shape, scratch, flops, limit=None):
+    limit = (limit or min(56, max(16, dims.rows // 32))) * 1024 * 1024
     return pl.pallas_call(
-        kernel,
+        functools.partial(kernel, dims),
         out_shape=out_shape,
         scratch_shapes=scratch,
-        compiler_params=pltpu.CompilerParams(vmem_limit_bytes=56 * 1024 * 1024),
+        compiler_params=pltpu.CompilerParams(vmem_limit_bytes=limit),
         cost_estimate=pl.CostEstimate(flops=flops, bytes_accessed=4000000, transcendentals=0),
         name=name,
-        **specs,
     )
 
 
@@ -344,11 +338,13 @@
     cols_t, wgt_t = foot_cols.T, foot_wgt.T
 
     message = call(
-        functools.partial(select_kernel, dims),
+        dims,
+        select_kernel,
         "select",
         shape((dims.rows, dims.width), BF16),
         [],
         2000000000,
+        56,
     )(roots, sigma, swap(sigma, 1), cols_t, wgt_t, neighbours)
     mine = hop(message, outward)
 
@@ -363,7 +359,8 @@
     value = observed[:, :flat]
 
     own_model, own_opt, opw = call(
-        functools.partial(own_kernel, dims),
+        dims,
+        own_kernel,
         "own_model",
         (
             shape((dims.slots, flat), F32),
@@ -379,7 +376,8 @@
     )
     other = swap(mine, 1)
     keep, give = call(
-        functools.partial(sides_kernel, dims),
+        dims,
+        sides_kernel,
         "sides_model",
         (shape((dims.slots, flat), F32), shape((2 * dims.slots, flat), F32)),
         [pltpu.VMEM((dims.chunk, dims.columns), BF16)],
@@ -388,7 +386,8 @@
     got = swap(give, 1)
     arrived = hop(keep + got[: dims.slots], inward)
     sides_opt = call(
-        functools.partial(turn_kernel, dims),
+        dims,
+        turn_kernel,
         "sides_turn",
         shape((dims.columns, 2 * dims.rows), BF16),
         [],
@@ -403,24 +402,23 @@
     misfit = rinv * (modelled - value)
     misfit_mine = hop(misfit, outward)
 
-    plane = pl.BlockSpec((dims.rows, LANES), lambda i: (0, dims.others * dims.block // LANES))
     own_total = call(
-        functools.partial(own_adjoint_kernel, dims),
+        dims,
+        own_adjoint_kernel,
         "own_adjoint",
         shape((dims.columns, dims.lanes), F32),
         [pltpu.VMEM((dims.rows, dims.lanes), BF16)],
         2000000000,
-        [whole(misfit), plane, whole(own_opt), whole(control), whole(opw)],
     )(misfit, message, own_opt, control, opw)
     misfit_mine, own_total = lax.optimization_barrier((misfit_mine, own_total))
     misfit_other = swap(misfit_mine, 1)
     return call(
-        functools.partial(sides_adjoint_kernel, dims),
+        dims,
+        sides_adjoint_kernel,
         "sides_adjoint",
         shape((dims.columns, dims.lanes), BF16),
         [pltpu.VMEM((2 * dims.rows, dims.lanes), BF16)],
         4000000000,
-        [whole(misfit)] * 2 + [plane] * 2 + [whole(sides_opt), whole(own_total), whole(opw)],
     )(misfit_mine, misfit_other, mine, other, sides_opt, own_total, opw)
 
 

time: 64.6 us -> 56.3 us (0.87)
  Pallas kernels: 26.4 us -> 14.1 us
  local copies, waits for them, and re-layouts: 3.81 us -> 7 us
  waiting for transfers between devices: 14.3 us -> 15.9 us
  other arithmetic: 0.87 us -> 0.12 us
    pallas_call x6, Pallas kernels: 26.4 us -> 14.1 us  [the longest x1 3.66 us: shards(): call(dims, select_kernel, 'select', shape((dims.rows, dims.width), BF16),...]
    unnamed x20 -> x28, local copies, waits for them, and re-layouts: 2.12 us -> 5.33 us
    ppermute x3, starting transfers between devices: 9.22 us -> 10.5 us  [shards(): hop = lambda x, pairs: lax.ppermute(x, ('space', 'var'), pairs)]
    ppermute x3, waiting for transfers between devices: 0.81 us -> 2.08 us  [shards(): hop = lambda x, pairs: lax.ppermute(x, ('space', 'var'), pairs)]
    ppermute x6, starting transfers between devices: 4.4 us -> 3.21 us  [shards(): lax.ppermute(x, 'var', [(i, i ^ bit) for i in range(ranks)])]
    add x1, other arithmetic: 0.76 us -> 0.01 us  [shards(): arrived = hop(keep + got[:dims.slots], inward)]
  transfers between devices with their start and end apart: 10 -> 10, of which waited for: 8 -> 8; matrix products, arithmetic and copies ran while one was open for 2% -> 2% of each run, Pallas kernels for 20% -> 9%
where the time goes in v3:
time: 56.3 us; the launch traced here: 55.9 us
  starting transfers between devices  18.6 us (33%)
  waiting for transfers between devices  15.9 us (28%)
  Pallas kernels  14.1 us (25%)
  local copies, waits for them, and re-layouts  7 us (12%)
    ppermute x3, starting transfers between devices, shards(): hop = lambda x, pairs: lax.ppermute(x, ('space', 'var'), pairs)  10.5 us
    ppermute x6, waiting for transfers between devices, shards(): lax.ppermute(x, 'var', [(i, i ^ bit) for i in range(ranks)])  7.93 us
    all_to_all x1, waiting for transfers between devices, shards(): lax.all_to_all(jnp.concatenate([obs_value, obs_rinv], axis=1), 'space', 0...  5.89 us
    unnamed x28, local copies, waits for them, and re-layouts  5.33 us
    all_to_all x1, starting transfers between devices, shards(): lax.all_to_all(jnp.concatenate([obs_value, obs_rinv], axis=1), 'space', 0...  4.84 us
    pallas_call x1, Pallas kernels, shards(): call(dims, select_kernel, 'select', shape((dims.rows, dims.width), BF16),...  3.66 us
    ppermute x6, starting transfers between devices, shards(): lax.ppermute(x, 'var', [(i, i ^ bit) for i in range(ranks)])  3.21 us
    pallas_call x1, Pallas kernels, shards(): call(dims, sides_kernel, 'sides_model', (shape((dims.slots, flat), F32),...  2.94 us
  transfers between devices with their start and end apart: 10, of which 8 were waited for; matrix products, arithmetic and copies ran while one was open for 2% of the time, Pallas kernels for 9%

profile of v3, /device:TPU:0, one launch (start us, length us, event | category | flops | bytes accessed | tf_op | source)
XLA Modules:
  0.0 55.9 jit_solution(2065890449545031726)
XLA Ops:
  0.5 0.7 %broadcast_in_dim.19 = s32[8,4]{1,0:T(8,128)S(1)} broadcast(s32[8]{0:T(128)} %bitcast.9), dimensions={0} | broadcast | bytes 160 | tf_op jit(solution)/shard_map/broadcast_in_dim | solution.py:357
  2.3 3.7 %select.3.message_ref.plane_ref = bf16[512,640]{1,0:T(8,128)(2,1)} custom-call(bf16[8,5,128,128]{3,2,1,0:T(8,128)(2,1)} %roots_ref.3, f32[24,1024]{1,0:T(8,128)} %sigma_ref.1, f32[24,1024]{1,0:T(8,128)} %copy-done.13, s32[16,32]{1,0:T(8,128)} %bitcast.5, f32[16,32]{1,0:T(8,128)} %bitcast.10, s32[8,5]{1,0:T(8,128)} %nb_ref.1), custom_call_target="tpu_custom_call" | custom-call | flops 2000000000 | bytes 4000000 | tf_op jit(solution)/shard_map/select/pallas_call | solution.py:340
  6.0 4.8 %collective-permute-start.1 = (bf16[512,640]{1,0:T(8,128)(2,1)}, bf16[512,640]{1,0:T(8,128)(2,1)S(1)}, u32[]{:S(2)}, u32[]{:S(2)}) collective-permute-start(bf16[512,640]{1,0:T(8,128)(2,1)} %select.3.message_ref.plane_ref), channel_id=1, source_target_pairs={{0,4},{2,6},{4,8},{5,1},{6,10},{7,3},{8,12},{9,5},{10,14},{11,7},{... | collective-permute-start | bytes 1966088 | tf_op jit(solution)/shard_map/ppermute | solution.py:334
  11.5 4.8 %all-to-all-start = ((f32[8,4,272]{2,1,0:T(4,128)}), f32[8,4,272]{2,1,0:T(4,128)S(1)}, u32[]{:S(2)}, u32[]{:S(2)}) async-start(f32[8,4,272]{2,1,0:T(4,128)} %all_to_all.8), calls=%async_computation | async-start | bytes 98304 | tf_op jit(solution)/shard_map/all_to_all | solution.py:352
  16.4 1.1 %copy-done.2 = bf16[512,640]{1,0:T(8,128)(2,1)S(1)} copy-done((bf16[512,640]{1,0:T(8,128)(2,1)S(1)}, bf16[512,640]{1,0:T(8,128)(2,1)}, u32[]{:S(2)}) %copy-start.2) | copy-done | bytes 655384
  17.4 2.2 %own_model.1 = (f32[32,256]{1,0:T(8,128)S(1)}, bf16[1024,512]{1,0:T(8,128)(2,1)S(1)}, bf16[384,256]{1,0:T(8,128)(2,1)S(1)}) custom-call(bf16[8,5,128,128]{3,2,1,0:T(8,128)(2,1)S(1)} %copy-done, s32[16,32]{1,0:T(8,128)S(1)} %bitcast.6, bf16[512,640]{1,0:T(8,128)(2,1)S(1)} %copy-done.2, bf16[1024,384]{1,0:T(8,128)(2,1)S(1)} %copy-done.1, ...), custom_call_target="tpu_custom_call" | custom-call | flops 4000000000 | bytes 4000000 | tf_op jit(solution)/shard_map/own_model/pallas_call | solution.py:361
  19.7 1.0 %copy-done.6 = bf16[1024,512]{1,0:T(8,128)(2,1)} copy-done((bf16[1024,512]{1,0:T(8,128)(2,1)}, bf16[1024,512]{1,0:T(8,128)(2,1)S(1)}, u32[]{:S(2)}) %copy-start.6) | copy-done | bytes 1048600
  20.7 5.9 %all-to-all-done = f32[8,4,272]{2,1,0:T(4,128)S(1)} async-done(((f32[8,4,272]{2,1,0:T(4,128)}), f32[8,4,272]{2,1,0:T(4,128)S(1)}, u32[]{:S(2)}, u32[]{:S(2)}) %all-to-all-start) | async-done | bytes 34848 | tf_op jit(solution)/shard_map/all_to_all | solution.py:352
  26.9 2.1 %collective-permute-done.2.other_ref = bf16[512,640]{1,0:T(8,128)(2,1)S(1)} collective-permute-done((bf16[512,640]{1,0:T(8,128)(2,1)S(1)}, bf16[512,640]{1,0:T(8,128)(2,1)S(1)}, u32[]{:S(2)}, u32[]{:S(2)}) %collective-permute-start.2) | collective-permute-done | bytes 655392 | tf_op jit(solution)/shard_map/ppermute | solution.py:335
  28.9 2.9 %sides_model.1 = (f32[32,256]{1,0:T(8,128)S(1)}, f32[64,256]{1,0:T(8,128)S(1)}) custom-call(bf16[512,640]{1,0:T(8,128)(2,1)S(1)} %collective-permute-done.1.mine_ref, bf16[512,640]{1,0:T(8,128)(2,1)S(1)} %collective-permute-done.2.other_ref, f32[32,256]{1,0:T(8,128)S(1)} %get-tuple-element.28.own_ref, bf16[1024,384]{1,0:T(8,128)(2,1)S(1)} %copy-done.1, ...), custom_call_target="tpu_custom_call" | custom-call | flops 4000000000 | bytes 4000000 | tf_op jit(solution)/shard_map/sides_model/pallas_call | solution.py:378
  32.1 1.1 %collective-permute-done.3 = f32[64,256]{1,0:T(8,128)S(1)} collective-permute-done((f32[64,256]{1,0:T(8,128)S(1)}, f32[64,256]{1,0:T(8,128)S(1)}, u32[]{:S(2)}, u32[]{:S(2)}) %collective-permute-start.3) | collective-permute-done | bytes 65568 | tf_op jit(solution)/shard_map/ppermute | solution.py:335
  33.2 1.4 %collective-permute-start.4 = (f32[32,256]{1,0:T(8,128)S(1)}, f32[32,256]{1,0:T(8,128)S(1)}, u32[]{:S(2)}, u32[]{:S(2)}) collective-permute-start(f32[32,256]{1,0:T(8,128)S(1)} %slice_add_fusion), channel_id=1, source_target_pairs={{4,0},{6,2},{8,4},{1,5},{10,6},{3,7},{12,8},{5,9},{14,10},{7,11},{... | collective-permute-start | bytes 98312 | tf_op jit(solution)/shard_map/ppermute | solution.py:334
  34.6 1.5 %sides_turn.1.opt_ref = bf16[1024,1024]{1,0:T(8,128)(2,1)S(1)} custom-call(bf16[512,640]{1,0:T(8,128)(2,1)S(1)} %collective-permute-done.1.mine_ref, bf16[512,640]{1,0:T(8,128)(2,1)S(1)} %collective-permute-done.2.other_ref), custom_call_target="tpu_custom_call" | custom-call | flops 4000000000 | bytes 4000000 | tf_op jit(solution)/shard_map/sides_turn/pallas_call | solution.py:388
  36.2 1.3 %copy-done.8 = bf16[1024,1024]{1,0:T(8,128)(2,1)} copy-done((bf16[1024,1024]{1,0:T(8,128)(2,1)}, bf16[1024,1024]{1,0:T(8,128)(2,1)S(1)}, u32[]{:S(2)}) %copy-start.8) | copy-done | bytes 2097176
  37.5 2.1 %collective-permute-done.4 = f32[32,256]{1,0:T(8,128)S(1)} collective-permute-done((f32[32,256]{1,0:T(8,128)S(1)}, f32[32,256]{1,0:T(8,128)S(1)}, u32[]{:S(2)}, u32[]{:S(2)}) %collective-permute-start.4) | collective-permute-done | bytes 32800 | tf_op jit(solution)/shard_map/ppermute | solution.py:334
  39.6 0.9 %collective-permute-start.5 = (f32[32,256]{1,0:T(8,128)S(1)}, f32[32,256]{1,0:T(8,128)S(1)}, u32[]{:S(2)}, u32[]{:S(2)}) collective-permute-start(f32[32,256]{1,0:T(8,128)S(1)} %collective-permute-done.4), channel_id=1, source_target_pairs={{0,1},{1,0},{2,3},{3,2},{4,5},{5,4},{6,7},{7,6},{8,9},{9,8},{10,11... | collective-permute-start | bytes 98312 | tf_op jit(solution)/shard_map/ppermute | solution.py:335
  40.4 0.9 %collective-permute-done.5 = f32[32,256]{1,0:T(8,128)S(1)} collective-permute-done((f32[32,256]{1,0:T(8,128)S(1)}, f32[32,256]{1,0:T(8,128)S(1)}, u32[]{:S(2)}, u32[]{:S(2)}) %collective-permute-start.5) | collective-permute-done | bytes 32800 | tf_op jit(solution)/shard_map/ppermute | solution.py:335
  41.3 1.6 %collective-permute-start.6 = (f32[32,256]{1,0:T(8,128)S(1)}, f32[32,256]{1,0:T(8,128)S(1)}, u32[]{:S(2)}, u32[]{:S(2)}) collective-permute-start(f32[32,256]{1,0:T(8,128)S(1)} %fusion.1), channel_id=1, source_target_pairs={{0,2},{1,3},{2,0},{3,1},{4,6},{5,7},{6,4},{7,5},{8,10},{9,11},{10,... | collective-permute-start | bytes 98312 | tf_op jit(solution)/shard_map/ppermute | solution.py:335
  43.0 2.3 %collective-permute-done.6 = f32[32,256]{1,0:T(8,128)S(1)} collective-permute-done((f32[32,256]{1,0:T(8,128)S(1)}, f32[32,256]{1,0:T(8,128)S(1)}, u32[]{:S(2)}, u32[]{:S(2)}) %collective-permute-start.6) | collective-permute-done | bytes 32800 | tf_op jit(solution)/shard_map/ppermute | solution.py:335
  45.3 4.3 %collective-permute-start.7 = (f32[32,256]{1,0:T(8,128)S(1)}, f32[32,256]{1,0:T(8,128)S(1)}, u32[]{:S(2)}, u32[]{:S(2)}) collective-permute-start(f32[32,256]{1,0:T(8,128)S(1)} %subtract_multiply_fusion.misfit_ref), channel_id=1, source_target_pairs={{0,4},{2,6},{4,8},{5,1},{6,10},{7,3},{8,12},{9,5},{10,14},{11,7},{... | collective-permute-start | bytes 98312 | tf_op jit(solution)/shard_map/ppermute | solution.py:334
  49.6 1.2 %copy-done.7 = bf16[1024,512]{1,0:T(8,128)(2,1)S(1)} copy-done((bf16[1024,512]{1,0:T(8,128)(2,1)S(1)}, bf16[1024,512]{1,0:T(8,128)(2,1)}, u32[]{:S(2)}) %copy-start.7) | copy-done | bytes 1048600
  50.9 1.1 %own_adjoint.1.own_ref = f32[1024,384]{1,0:T(8,128)S(1)} custom-call(f32[32,256]{1,0:T(8,128)S(1)} %subtract_multiply_fusion.misfit_ref, bf16[512,640]{1,0:T(8,128)(2,1)S(1)} %copy-done.3, bf16[1024,512]{1,0:T(8,128)(2,1)S(1)} %copy-done.7, bf16[1024,384]{1,0:T(8,128)(2,1)S(1)} %copy-done.1, bf16[384,256]{1,0:T(8,128)(2,1)S(1)} %get-tuple-element.30.opw_ref), custom_call_target="tpu_custom_call" | custom-call | flops 2000000000 | bytes 4000000 | tf_op jit(solution)/shard_map/own_adjoint/pallas_call | solution.py:405
  52.1 1.2 %collective-permute-done.8.misfit2_ref = f32[32,256]{1,0:T(8,128)S(1)} collective-permute-done((f32[32,256]{1,0:T(8,128)S(1)}, f32[32,256]{1,0:T(8,128)S(1)}, u32[]{:S(2)}, u32[]{:S(2)}) %collective-permute-start.8) | collective-permute-done | bytes 32800 | tf_op jit(solution)/shard_map/ppermute | solution.py:335
  53.3 2.7 %sides_adjoint.1 = bf16[1024,384]{1,0:T(8,128)(2,1)} custom-call(f32[32,256]{1,0:T(8,128)S(1)} %collective-permute-done.7.misfit_ref, f32[32,256]{1,0:T(8,128)S(1)} %collective-permute-done.8.misfit2_ref, bf16[512,640]{1,0:T(8,128)(2,1)S(1)} %collective-permute-done.1.mine_ref, bf16[512,640]{1,0:T(8,128)(2,1)S(1)} %collective-permute-done.2.other_ref, ...), custom_call_target="tpu_custom_call" | custom-call | flops 4000000000 | bytes 4000000 | tf_op jit(solution)/shard_map/sides_adjoint/pallas_call | solution.py:415
  (46 shorter events, 2.9 us)
Async XLA Ops:
  0.0 1.6 %collective-permute-start = (f32[24,1024]{1,0:T(8,128)}, f32[24,1024]{1,0:T(8,128)S(1)}, u32[]{:S(2)}, u32[]{:S(2)}) collective-permute-start(f32[24,1024]{1,0:T(8,128)} %sigma_ref.1), channel_id=1, source_target_pairs={{0,1},{1,0},{2,3},{3,2},{4,5},{5,4},{6,7},{7,6},{8,9},{9,8},{10,11... | collective-permute-start | bytes 294920 | tf_op jit(solution)/shard_map/ppermute | solution.py:335
  2.3 8.5 %copy-start.12 = (f32[32,16]{0,1:T(8,128)S(1)}, f32[32,16]{0,1:T(8,128)}, u32[]{:S(2)}) copy-start(f32[32,16]{0,1:T(8,128)} %param.18) | copy-start | bytes 6148
  2.3 8.6 %copy-start.11 = (f32[32,256]{1,0:T(8,128)S(1)}, f32[32,256]{1,0:T(8,128)}, u32[]{:S(2)}) copy-start(f32[32,256]{1,0:T(8,128)} %param.17) | copy-start | bytes 98308
  2.3 14.1 %copy-start = (bf16[8,5,128,128]{3,2,1,0:T(8,128)(2,1)S(1)}, bf16[8,5,128,128]{3,2,1,0:T(8,128)(2,1)}, u32[]{:S(2)}) copy-start(bf16[8,5,128,128]{3,2,1,0:T(8,128)(2,1)} %roots_ref.3) | copy-start | bytes 3932164
  2.3 14.1 %copy-start.1 = (bf16[1024,384]{1,0:T(8,128)(2,1)S(1)}, bf16[1024,384]{1,0:T(8,128)(2,1)}, u32[]{:S(2)}) copy-start(bf16[1024,384]{1,0:T(8,128)(2,1)} %control_ref.5) | copy-start | bytes 2359300
  2.3 14.1 %copy-start.4 = (s32[32,16]{0,1:T(8,128)S(1)}, s32[32,16]{0,1:T(8,128)}, u32[]{:S(2)}) copy-start(s32[32,16]{0,1:T(8,128)} %param.15) | copy-start | bytes 6148
  2.3 14.1 %copy-start.5 = (bf16[24,16]{0,1:T(8,128)(2,1)S(1)}, bf16[24,16]{0,1:T(8,128)(2,1)}, u32[]{:S(2)}) copy-start(bf16[24,16]{0,1:T(8,128)(2,1)} %param.14) | copy-start | bytes 2308
  6.0 20.8 %collective-permute-start.1 = (bf16[512,640]{1,0:T(8,128)(2,1)}, bf16[512,640]{1,0:T(8,128)(2,1)S(1)}, u32[]{:S(2)}, u32[]{:S(2)}) collective-permute-start(bf16[512,640]{1,0:T(8,128)(2,1)} %select.3.message_ref.plane_ref), channel_id=1, source_target_pairs={{0,4},{2,6},{4,8},{5,1},{6,10},{7,3},{8,12},{9,5},{10,14},{11,7},{... | collective-permute-start | bytes 1966088 | tf_op jit(solution)/shard_map/ppermute | solution.py:334
  11.5 15.1 %all-to-all-start = ((f32[8,4,272]{2,1,0:T(4,128)}), f32[8,4,272]{2,1,0:T(4,128)S(1)}, u32[]{:S(2)}, u32[]{:S(2)}) async-start(f32[8,4,272]{2,1,0:T(4,128)} %all_to_all.8), calls=%async_computation | async-start | bytes 98304 | tf_op jit(solution)/shard_map/all_to_all | solution.py:352
  16.3 1.1 %copy-start.2 = (bf16[512,640]{1,0:T(8,128)(2,1)S(1)}, bf16[512,640]{1,0:T(8,128)(2,1)}, u32[]{:S(2)}) copy-start(bf16[512,640]{1,0:T(8,128)(2,1)} %select.3.message_ref.plane_ref) | copy-start | bytes 1966084
  19.7 1.0 %copy-start.6 = (bf16[1024,512]{1,0:T(8,128)(2,1)}, bf16[1024,512]{1,0:T(8,128)(2,1)S(1)}, u32[]{:S(2)}) copy-start(bf16[1024,512]{1,0:T(8,128)(2,1)S(1)} %get-tuple-element.35.opt_ref) | copy-start | bytes 3145732
  26.6 5.3 %copy-start.10 = (f32[32,272]{1,0:T(8,128)}, f32[32,272]{1,0:T(8,128)S(1)}, u32[]{:S(2)}) copy-start(f32[32,272]{1,0:T(8,128)S(1)} %all_to_all.10) | copy-start | bytes 104452
  26.8 2.2 %collective-permute-start.2 = (bf16[512,640]{1,0:T(8,128)(2,1)S(1)}, bf16[512,640]{1,0:T(8,128)(2,1)S(1)}, u32[]{:S(2)}, u32[]{:S(2)}) collective-permute-start(bf16[512,640]{1,0:T(8,128)(2,1)S(1)} %collective-permute-done.1.mine_ref), channel_id=1, source_target_pairs={{0,1},{1,0},{2,3},{3,2},{4,5},{5,4},{6,7},{7,6},{8,9},{9,8},{10,11... | collective-permute-start | bytes 1966088 | tf_op jit(solution)/shard_map/ppermute | solution.py:335
  31.9 1.3 %collective-permute-start.3 = (f32[64,256]{1,0:T(8,128)S(1)}, f32[64,256]{1,0:T(8,128)S(1)}, u32[]{:S(2)}, u32[]{:S(2)}) collective-permute-start(f32[64,256]{1,0:T(8,128)S(1)} %get-tuple-element.31), channel_id=1, source_target_pairs={{0,1},{1,0},{2,3},{3,2},{4,5},{5,4},{6,7},{7,6},{8,9},{9,8},{10,11... | collective-permute-start | bytes 196616 | tf_op jit(solution)/shard_map/ppermute | solution.py:335
  33.2 12.1 %slice-start = ((f32[32,272]{1,0:T(8,128)}), f32[32,256]{1,0:T(8,128)S(1)}, s32[]{:S(2)}) async-start(f32[32,272]{1,0:T(8,128)} %copy-done.10), calls=%async_computation.1 | async-start | bytes 65536 | tf_op jit(solution)/shard_map/slice | solution.py:359
  33.2 16.4 %copy-start.3 = (bf16[512,640]{1,0:T(8,128)(2,1)S(1)}, bf16[512,640]{1,0:T(8,128)(2,1)}, u32[]{:S(2)}) copy-start(bf16[512,640]{1,0:T(8,128)(2,1)} %select.3.message_ref.plane_ref) | copy-start | bytes 1966084
  33.2 6.4 %collective-permute-start.4 = (f32[32,256]{1,0:T(8,128)S(1)}, f32[32,256]{1,0:T(8,128)S(1)}, u32[]{:S(2)}, u32[]{:S(2)}) collective-permute-start(f32[32,256]{1,0:T(8,128)S(1)} %slice_add_fusion), channel_id=1, source_target_pairs={{4,0},{6,2},{8,4},{1,5},{10,6},{3,7},{12,8},{5,9},{14,10},{7,11},{... | collective-permute-start | bytes 98312 | tf_op jit(solution)/shard_map/ppermute | solution.py:334
  36.2 1.3 %copy-start.8 = (bf16[1024,1024]{1,0:T(8,128)(2,1)}, bf16[1024,1024]{1,0:T(8,128)(2,1)S(1)}, u32[]{:S(2)}) copy-start(bf16[1024,1024]{1,0:T(8,128)(2,1)S(1)} %sides_turn.1.opt_ref) | copy-start | bytes 6291460
  39.6 1.7 %collective-permute-start.5 = (f32[32,256]{1,0:T(8,128)S(1)}, f32[32,256]{1,0:T(8,128)S(1)}, u32[]{:S(2)}, u32[]{:S(2)}) collective-permute-start(f32[32,256]{1,0:T(8,128)S(1)} %collective-permute-done.4), channel_id=1, source_target_pairs={{0,1},{1,0},{2,3},{3,2},{4,5},{5,4},{6,7},{7,6},{8,9},{9,8},{10,11... | collective-permute-start | bytes 98312 | tf_op jit(solution)/shard_map/ppermute | solution.py:335
  41.3 4.0 %collective-permute-start.6 = (f32[32,256]{1,0:T(8,128)S(1)}, f32[32,256]{1,0:T(8,128)S(1)}, u32[]{:S(2)}, u32[]{:S(2)}) collective-permute-start(f32[32,256]{1,0:T(8,128)S(1)} %fusion.1), channel_id=1, source_target_pairs={{0,2},{1,3},{2,0},{3,1},{4,6},{5,7},{6,4},{7,5},{8,10},{9,11},{10,... | collective-permute-start | bytes 98312 | tf_op jit(solution)/shard_map/ppermute | solution.py:335
  45.3 6.7 %collective-permute-start.7 = (f32[32,256]{1,0:T(8,128)S(1)}, f32[32,256]{1,0:T(8,128)S(1)}, u32[]{:S(2)}, u32[]{:S(2)}) collective-permute-start(f32[32,256]{1,0:T(8,128)S(1)} %subtract_multiply_fusion.misfit_ref), channel_id=1, source_target_pairs={{0,4},{2,6},{4,8},{5,1},{6,10},{7,3},{8,12},{9,5},{10,14},{11,7},{... | collective-permute-start | bytes 98312 | tf_op jit(solution)/shard_map/ppermute | solution.py:334
  49.6 1.2 %copy-start.7 = (bf16[1024,512]{1,0:T(8,128)(2,1)S(1)}, bf16[1024,512]{1,0:T(8,128)(2,1)}, u32[]{:S(2)}) copy-start(bf16[1024,512]{1,0:T(8,128)(2,1)} %copy-done.6) | copy-start | bytes 3145732
  50.9 2.4 %copy-start.9 = (bf16[1024,1024]{1,0:T(8,128)(2,1)S(1)}, bf16[1024,1024]{1,0:T(8,128)(2,1)}, u32[]{:S(2)}) copy-start(bf16[1024,1024]{1,0:T(8,128)(2,1)} %copy-done.8) | copy-start | bytes 6291460
  52.0 1.3 %collective-permute-start.8 = (f32[32,256]{1,0:T(8,128)S(1)}, f32[32,256]{1,0:T(8,128)S(1)}, u32[]{:S(2)}, u32[]{:S(2)}) collective-permute-start(f32[32,256]{1,0:T(8,128)S(1)} %collective-permute-done.7.misfit_ref), channel_id=1, source_target_pairs={{0,1},{1,0},{2,3},{3,2},{4,5},{5,4},{6,7},{7,6},{8,9},{9,8},{10,11... | collective-permute-start | bytes 98312 | tf_op jit(solution)/shard_map/ppermute | solution.py:335
  (1 other events, 0.6 us)

commit v4 on v3

v4 whole, which is shorter than its diff:
```python
import functools

import jax
import jax.numpy as jnp
from jax import lax
from jax.experimental import pallas as pl
from jax.experimental.pallas import tpu as pltpu
from jax.sharding import PartitionSpec as P

F32 = jnp.float32
BF16 = jnp.bfloat16
NT = (((1,), (1,)), ((), ()))


def repeat_steps(count, body):
    if count <= 2:
        for step in range(count):
            body(step)
    else:
        lax.fori_loop(0, count, lambda step, carry: (body(step), carry)[1], 0)


def at(step, size):
    if isinstance(step, int):
        return pl.ds(step * size, size)
    return pl.ds(pl.multiple_of(step * size, size), size)


def dot(a, b):
    return jnp.dot(a, b, preferred_element_type=F32)


def dot_nt(a, b):
    return lax.dot_general(a, b, NT, preferred_element_type=F32)


def iota(shape, axis):
    return lax.broadcasted_iota(jnp.int32, shape, axis)


def spread_rows(values):
    points, slots = values.shape
    wide = jnp.broadcast_to(values.astype(F32)[:, None, :], (points, slots, slots))
    wide = wide.reshape(points * slots, slots)
    hit = iota(wide.shape, 1) == lax.rem(iota(wide.shape, 0), slots)
    return jnp.where(hit, wide, 0.0)


def column(values):
    return jnp.sum(spread_rows(values), axis=1, keepdims=True)


def row_of(values):
    wide = spread_rows(values)
    high = wide.astype(BF16)
    low = (wide - high.astype(F32)).astype(BF16)
    ones = jnp.ones((8, wide.shape[1]), BF16)
    return (dot_nt(ones, high) + dot_nt(ones, low))[:1]


def one_hot(cols, count):
    lane = iota((cols.shape[0], count), 1)
    return jnp.where(lane == cols.astype(jnp.int32), 1.0, 0.0).astype(BF16)


def within(value, low, count):
    return (value >= low) & (value < low + count)


def as_bf16(mask):
    return jnp.where(mask, 1.0, 0.0).astype(BF16)


def scale_spread(dims, half):
    shape = (dims.plane, dims.lanes)
    row = iota(shape, 0) - dims.vars * half
    return as_bf16(within(iota(shape, 1) - dims.members * row, 0, dims.members))


def target_spread(dims):
    shape = (dims.plane, dims.width)
    row = iota(shape, 0) - 2 * dims.vars
    return as_bf16(within(iota(shape, 1) - dims.block * row, 0, dims.block))


def plane_of(dims, message_ref, step):
    pieces = []
    for i in range(dims.chunk // dims.width):
        pieces.append(message_ref[at(step * (dims.chunk // dims.width) + i, dims.plane), :])
    return pieces[0] if len(pieces) == 1 else jnp.concatenate(pieces, axis=1)


def roots_of(dims, message_ref, step):
    rows = pl.ds(dims.head + step * dims.chunk, dims.chunk)
    if not isinstance(step, int):
        rows = pl.ds(pl.multiple_of(dims.head + step * dims.chunk, 64), dims.chunk)
    return [
        message_ref[rows, k * dims.block : (k + 1) * dims.block] for k in range(dims.others)
    ]


def fill_operator(dims, op_ref, targets, parts):
    for q in range(dims.blocks):
        total = None
        for target, part in zip(targets, parts):
            term = jnp.where(target == jnp.asarray(q, target.dtype), part, jnp.zeros((), part.dtype))
            total = term if total is None else total + term
        op_ref[:, q * dims.block : (q + 1) * dims.block] = total


def model_rows(dims, op_ref, scale, control_ref, opw):
    summed = dot(op_ref[...], control_ref[...])
    state = (summed * scale).astype(BF16)
    bands = dot(state, opw)
    return jnp.sum(bands.reshape(dims.chunk_points, dims.slots, bands.shape[1]), axis=0)


def select_kernel(dims, roots_ref, sigma_ref, sigma2_ref, cols_ref, wgt_ref, nb_ref, out_ref):
    tile = lax.axis_index("space")
    half = lax.rem(lax.axis_index("var"), 2)
    sigma, sigma2 = sigma_ref[...], sigma2_ref[...]
    sigma = jnp.concatenate(
        [jnp.where(half == 0, sigma, sigma2), jnp.where(half == 0, sigma2, sigma)], axis=0
    )
    high = sigma.astype(BF16).astype(F32)
    nb = nb_ref[...] + ((2 * half - 1) - tile) * dims.blocks
    nb = nb.astype(F32)
    base = 2 * dims.vars
    ids = jnp.zeros((dims.plane - base, dims.columns), F32)
    shape = ids.shape
    for b in range(dims.blocks):
        in_block = within(iota(shape, 1), b * dims.block, dims.block)
        for k in range(dims.others):
            ids = jnp.where(in_block & (iota(shape, 0) == k), nb[b : b + 1, k + 1 : k + 2], ids)
    rest = jnp.zeros_like(ids)
    table = jnp.concatenate([high, ids, sigma - high, rest], axis=0).astype(BF16)

    def body(step):
        points = at(step, dims.chunk_points)
        hot = one_hot(column(cols_ref[points, :]), dims.columns)
        plane = dot_nt(table, hot)
        scale = (plane[:base] + plane[dims.plane : dims.plane + base]) * row_of(wgt_ref[points, :])
        plane = jnp.concatenate([scale, plane[base : dims.plane]], axis=0).astype(BF16)
        pieces = dims.chunk // dims.width
        for i in range(pieces):
            out_ref[at(step * pieces + i, dims.plane), :] = plane[
                :, i * dims.width : (i + 1) * dims.width
            ]
        rows = pl.ds(dims.head + step * dims.chunk, dims.chunk)
        if not isinstance(step, int):
            rows = pl.ds(pl.multiple_of(dims.head + step * dims.chunk, 64), dims.chunk)
        for k in range(0, dims.others, 2):
            pair = range(k, min(k + 2, dims.others))
            root = jnp.concatenate(
                [roots_ref[:, i + 1].reshape(dims.columns, dims.block) for i in pair], axis=1
            )
            out_ref[rows, k * dims.block : (k + len(pair)) * dims.block] = dot(hot, root).astype(BF16)

    repeat_steps(dims.chunks, body)


def own_kernel(
    dims, roots_ref, cols_ref, message_ref, control_ref, obs_ref,
    model_ref, opt_ref, opw_ref, op_ref,
):
    half = lax.rem(lax.axis_index("var"), 2)
    bands = obs_ref.shape[0]
    flat = bands * dims.members
    vars_wide = as_bf16(
        within(iota((dims.lanes, dims.vars), 0) - dims.members * iota((dims.lanes, dims.vars), 1), 0, dims.members)
    )
    bands_wide = as_bf16(
        within(iota((bands, flat), 1) - dims.members * iota((bands, flat), 0), 0, dims.members)
    )
    opw = dot(dot_nt(vars_wide, obs_ref[...]).astype(BF16), bands_wide)
    same = lax.rem(iota(opw.shape, 0), dims.members) == lax.rem(iota(opw.shape, 1), dims.members)
    opw = jnp.where(same, opw, 0.0).astype(BF16)
    opw_ref[...] = opw
    spread, targets_of = scale_spread(dims, half), target_spread(dims)
    root = roots_ref[:, 0].reshape(dims.columns, dims.block)
    shift = ((1 - 2 * half) * dims.blocks).astype(F32)

    def body(step):
        rows = at(step, dims.chunk)
        plane = plane_of(dims, message_ref, step).T
        cols = column(cols_ref[at(step, dims.chunk_points), :])
        own = jnp.floor(cols * (1.0 / dims.block))
        targets = [jnp.broadcast_to(own, (dims.chunk, dims.block)).astype(BF16)]
        parts = [dot(one_hot(cols, dims.columns), root).astype(BF16)]
        ids = (dot(plane, targets_of) + shift).astype(BF16)
        for k in range(dims.others):
            targets.append(ids[:, k * dims.block : (k + 1) * dims.block])
        parts += roots_of(dims, message_ref, step)
        fill_operator(dims, op_ref, targets, parts)
        model = model_rows(dims, op_ref, dot(plane, spread), control_ref, opw)
        if isinstance(step, int) and step == 0:
            model_ref[...] = model
        else:
            model_ref[...] += model
        opt_ref[:, rows] = op_ref[...].T

    if dims.chunks > 2:
        model_ref[...] = jnp.zeros_like(model_ref)
    repeat_steps(dims.chunks, body)


def side_kernel(dims, message_ref, control_ref, opw_ref, model_ref, op_ref):
    half = lax.rem(lax.axis_index("var"), 2)
    spread, targets_of = scale_spread(dims, half), target_spread(dims)
    opw = opw_ref[...]

    def body(step):
        plane = plane_of(dims, message_ref, step).T
        ids = dot(plane, targets_of).astype(BF16)
        targets = [ids[:, k * dims.block : (k + 1) * dims.block] for k in range(dims.others)]
        fill_operator(dims, op_ref, targets, roots_of(dims, message_ref, step))
        model = model_rows(dims, op_ref, dot(plane, spread), control_ref, opw)
        if isinstance(step, int) and step == 0:
            model_ref[...] = model
        else:
            model_ref[...] += model

    if dims.chunks > 2:
        model_ref[...] = jnp.zeros_like(model_ref)
    repeat_steps(dims.chunks, body)


def give_kernel(dims, message_ref, own_ref, control_ref, opw_ref, give_ref, op_ref):
    give_ref[dims.slots :, :] = own_ref[...]
    side_kernel(dims, message_ref, control_ref, opw_ref, give_ref.at[: dims.slots], op_ref)


def turn_kernel(dims, mine_ref, other_ref, mine_opt_ref, other_opt_ref):
    for ref, opt_ref in ((mine_ref, mine_opt_ref), (other_ref, other_opt_ref)):

        def body(step):
            plane = plane_of(dims, ref, step).astype(F32)
            parts = [part.T for part in roots_of(dims, ref, step)]
            targets = []
            for k in range(dims.others):
                row = plane[2 * dims.vars + k : 2 * dims.vars + k + 1]
                targets.append(jnp.broadcast_to(row, (dims.block, dims.chunk)).astype(BF16))
            for q in range(dims.blocks):
                total = None
                for target, part in zip(targets, parts):
                    term = jnp.where(target == jnp.asarray(q, BF16), part, jnp.zeros((), BF16))
                    total = term if total is None else total + term
                opt_ref[q * dims.block : (q + 1) * dims.block, at(step, dims.chunk)] = total

        repeat_steps(dims.chunks, body)


def adjoint_kernel(dims, misfit_ref, message_ref, opt_ref, base_ref, opw_ref, out_ref, adj_ref):
    half = lax.rem(lax.axis_index("var"), 2)
    spread = scale_spread(dims, half)
    misfit, opw = misfit_ref[...], opw_ref[...]
    high = misfit.astype(BF16)
    rest = misfit - high.astype(F32)
    middle = rest.astype(BF16)
    low = (rest - middle.astype(F32)).astype(BF16)
    pulled = dot_nt(high, opw) + (dot_nt(middle, opw) + dot_nt(low, opw))

    def body(step):
        scale = dot(plane_of(dims, message_ref, step).T, spread)
        wide = scale.reshape(dims.chunk_points, dims.slots, dims.lanes) * pulled[None]
        adj_ref[at(step, dims.chunk), :] = wide.reshape(dims.chunk, dims.lanes).astype(BF16)

    repeat_steps(dims.chunks, body)
    for part in range(dims.columns // 256):
        rows = slice(part * 256, (part + 1) * 256)
        total = base_ref[rows, :].astype(F32) + dot(opt_ref[rows, :], adj_ref[...])
        out_ref[rows, :] = total.astype(out_ref.dtype)


class Dims:
    def __init__(self, control, roots, sigma, foot_cols):
        self.blocks, links, self.block = roots.shape[:3]
        self.others = links - 1
        self.columns, self.lanes = control.shape
        self.vars = sigma.shape[0]
        self.members = self.lanes // self.vars
        self.slots, self.points = foot_cols.shape
        self.rows = self.slots * self.points
        self.chunk_points = min(self.points, max(8, 512 // self.slots))
        self.chunk = self.chunk_points * self.slots
        self.chunks = self.rows // self.chunk
        self.width = self.others * self.block
        self.plane = 64
        self.head = self.plane * (self.rows // self.width)


def call(dims, kernel, name, out_shape, scratch, flops, limit=None):
    limit = (limit or min(56, max(16, dims.rows // 32))) * 1024 * 1024
    return pl.pallas_call(
        functools.partial(kernel, dims),
        out_shape=out_shape,
        scratch_shapes=scratch,
        compiler_params=pltpu.CompilerParams(vmem_limit_bytes=limit),
        cost_estimate=pl.CostEstimate(flops=flops, bytes_accessed=4000000, transcendentals=0),
        name=name,
    )


def shards(
    control,
    roots,
    neighbours,
    sigma,
    obs_op,
    foot_cols,
    foot_wgt,
    obs_value,
    obs_rinv,
    owner_counts,
):
    dims = Dims(control, roots, sigma, foot_cols)
    bands = obs_op.shape[1]
    members = dims.members
    tiles = lax.axis_size("space")
    ranks = lax.axis_size("var")
    outward, inward = [], []
    for t in range(tiles):
        for v in range(ranks):
            to = t + 1 - 2 * (v % 2)
            if 0 <= to < tiles:
                outward.append((t * ranks + v, to * ranks + v))
                inward.append((to * ranks + v, t * ranks + v))
    hop = lambda x, pairs: lax.ppermute(x, ("space", "var"), pairs)
    swap = lambda x, bit: lax.ppermute(x, "var", [(i, i ^ bit) for i in range(ranks)])
    shape = jax.ShapeDtypeStruct
    flat = bands * members
    cols_t, wgt_t = foot_cols.T, foot_wgt.T

    message = call(
        dims,
        select_kernel,
        "select",
        shape((dims.head + dims.rows, dims.width), BF16),
        [],
        2000000000,
        56,
    )(roots, sigma, swap(sigma, 1), cols_t, wgt_t, neighbours)
    mine = hop(message, outward)

    message, obs_value, obs_rinv, owner_counts = lax.optimization_barrier(
        (message, obs_value, obs_rinv, owner_counts)
    )
    observed = lax.all_to_all(
        jnp.concatenate([obs_value, obs_rinv], axis=1), "space", 0, 0, tiled=True
    )
    capacity = dims.slots // owner_counts.shape[1]
    slot_ids = jnp.arange(dims.slots, dtype=jnp.int32)
    live = slot_ids % capacity < jnp.repeat(owner_counts[0], capacity)
    rinv = jnp.repeat(jnp.where(live[:, None], observed[:, flat:], 0.0), members, axis=1)
    value = observed[:, :flat]

    own_model, own_opt, opw = call(
        dims,
        own_kernel,
        "own_model",
        (
            shape((dims.slots, flat), F32),
            shape((dims.columns, dims.rows), BF16),
            shape((dims.lanes, flat), BF16),
        ),
        [pltpu.VMEM((dims.chunk, dims.columns), BF16)],
        4000000000,
    )(roots, cols_t, message, control, obs_op.T)

    mine, own_model, own_opt, rinv, value = lax.optimization_barrier(
        (mine, own_model, own_opt, rinv, value)
    )
    other = swap(mine, 1)
    op_scratch = [pltpu.VMEM((dims.chunk, dims.columns), BF16)]
    keep = call(
        dims, side_kernel, "mine_model", shape((dims.slots, flat), F32), op_scratch, 2000000000
    )(mine, control, opw)
    other, keep = lax.optimization_barrier((other, keep))
    give = call(
        dims, give_kernel, "other_model", shape((2 * dims.slots, flat), F32), op_scratch, 2000000000
    )(other, own_model, control, opw)
    got = swap(give, 1)
    arrived = hop(keep + got[: dims.slots], inward)
    mine_opt, other_opt = call(
        dims,
        turn_kernel,
        "sides_turn",
        (shape((dims.columns, dims.rows), BF16),) * 2,
        [],
        4000000000,
    )(mine, other)
    arrived, mine_opt, other_opt = lax.optimization_barrier((arrived, mine_opt, other_opt))
    modelled = own_model + got[dims.slots :] + arrived + swap(arrived, 1)
    bit = 2
    while bit < ranks:
        modelled = modelled + swap(modelled, bit)
        bit *= 2
    misfit = rinv * (modelled - value)
    misfit_mine = hop(misfit, outward)

    def add_adjoint(name, dtype, *operands):
        return call(
            dims,
            adjoint_kernel,
            name,
            shape((dims.columns, dims.lanes), dtype),
            [pltpu.VMEM((dims.rows, dims.lanes), BF16)],
            2000000000,
        )(*operands, opw)

    total = add_adjoint("own_adjoint", F32, misfit, message, own_opt, control)
    misfit_mine, total = lax.optimization_barrier((misfit_mine, total))
    misfit_other = swap(misfit_mine, 1)
    total = add_adjoint("mine_adjoint", F32, misfit_mine, mine, mine_opt, total)
    misfit_other, total = lax.optimization_barrier((misfit_other, total))
    return add_adjoint("other_adjoint", BF16, misfit_other, other, other_opt, total)


def solution(mesh):
    return jax.shard_map(
        shards,
        mesh=mesh,
        in_specs=(
            P("space", "var"),
            P("space", None, None, None),
            P("space", None),
            P("var", "space"),
            P("var", None),
            P("space", None),
            P("space", None),
            P("space", None),
            P("space", None),
            P("space", None),
        ),
        out_specs=P("space", "var"),
        check_vma=False,
    )
```

time: 56.3 us -> 52.6 us (0.934)
  waiting for transfers between devices: 15.9 us -> 12.7 us
    ppermute x6, waiting for transfers between devices: 7.93 us -> 6.11 us  [shards(): lax.ppermute(x, 'var', [(i, i ^ bit) for i in range(ranks)])]
    all_to_all x1, waiting for transfers between devices: 5.89 us -> 4.39 us  [shards(): lax.all_to_all(jnp.concatenate([obs_value, obs_rinv], axis=1), 'space', 0...]
    broadcast_in_dim x1, local copies, waits for them, and re-layouts: 0.72 us -> 0.07 us  [shards(): live = slot_ids % capacity < jnp.repeat(owner_counts[0], capacity)]
    unnamed x28 -> x34, local copies, waits for them, and re-layouts: 5.33 us -> 5.93 us
    pallas_call x5 -> x7, Pallas kernels: 11.9 us -> 11.4 us  [the longest x3 4.13 us: add_adjoint(): call(dims, adjoint_kernel, name, shape((dims.columns, dims.lanes), dtype)...]
  transfers between devices with their start and end apart: 10 -> 10, of which waited for: 8 -> 8; matrix products, arithmetic and copies ran while one was open for 2% -> 1% of each run, Pallas kernels for 9% -> 13%
where the time goes in v4:
time: 52.6 us; the launch traced here: 52.3 us
  starting transfers between devices  18.7 us (36%)
  Pallas kernels  13.6 us (26%)
  waiting for transfers between devices  12.7 us (24%)
  local copies, waits for them, and re-layouts  6.95 us (13%)
    ppermute x3, starting transfers between devices, shards(): hop = lambda x, pairs: lax.ppermute(x, ('space', 'var'), pairs)  10.7 us
    ppermute x6, waiting for transfers between devices, shards(): lax.ppermute(x, 'var', [(i, i ^ bit) for i in range(ranks)])  6.11 us
    unnamed x34, local copies, waits for them, and re-layouts  5.93 us
    all_to_all x1, starting transfers between devices, shards(): lax.all_to_all(jnp.concatenate([obs_value, obs_rinv], axis=1), 'space', 0...  4.85 us
    all_to_all x1, waiting for transfers between devices, shards(): lax.all_to_all(jnp.concatenate([obs_value, obs_rinv], axis=1), 'space', 0...  4.39 us
    pallas_call x3, Pallas kernels, add_adjoint(): call(dims, adjoint_kernel, name, shape((dims.columns, dims.lanes), dtype)...  4.13 us
    pallas_call x1, Pallas kernels, shards(): call(dims, select_kernel, 'select', shape((dims.head + dims.rows, dims.wi...  3.59 us
    ppermute x6, starting transfers between devices, shards(): lax.ppermute(x, 'var', [(i, i ^ bit) for i in range(ranks)])  3.13 us
  transfers between devices with their start and end apart: 10, of which 8 were waited for; matrix products, arithmetic and copies ran while one was open for 1% of the time, Pallas kernels for 13%

profile of v4, /device:TPU:0, one launch (start us, length us, event | category | flops | bytes accessed | tf_op | source)
XLA Modules:
  0.0 52.3 jit_solution(12645971120082356953)
XLA Ops:
  0.5 1.2 %collective-permute-done.sigma2_ref = f32[24,1024]{1,0:T(8,128)S(1)} collective-permute-done((f32[24,1024]{1,0:T(8,128)}, f32[24,1024]{1,0:T(8,128)S(1)}, u32[]{:S(2)}, u32[]{:S(2)}) %collective-permute-start) | collective-permute-done | bytes 98336 | tf_op jit(solution)/shard_map/ppermute | solution.py:329
  2.3 3.6 %select.3.message_ref = bf16[576,512]{1,0:T(8,128)(2,1)} custom-call(bf16[8,5,128,128]{3,2,1,0:T(8,128)(2,1)} %roots_ref.3, f32[24,1024]{1,0:T(8,128)} %sigma_ref.1, f32[24,1024]{1,0:T(8,128)} %copy-done.16, s32[16,32]{1,0:T(8,128)} %bitcast.5, f32[16,32]{1,0:T(8,128)} %bitcast.10, s32[8,5]{1,0:T(8,128)} %nb_ref.1), custom_call_target="tpu_custom_call" | custom-call | flops 2000000000 | bytes 4000000 | tf_op jit(solution)/shard_map/select/pallas_call | solution.py:334
  5.9 4.8 %collective-permute-start.1 = (bf16[576,512]{1,0:T(8,128)(2,1)}, bf16[576,512]{1,0:T(8,128)(2,1)S(1)}, u32[]{:S(2)}, u32[]{:S(2)}) collective-permute-start(bf16[576,512]{1,0:T(8,128)(2,1)} %select.3.message_ref), channel_id=1, source_target_pairs={{0,4},{2,6},{4,8},{5,1},{6,10},{7,3},{8,12},{9,5},{10,14},{11,7},{... | collective-permute-start | bytes 1769480 | tf_op jit(solution)/shard_map/ppermute | solution.py:328
  11.4 4.8 %all-to-all-start = ((f32[8,4,272]{2,1,0:T(4,128)}), f32[8,4,272]{2,1,0:T(4,128)S(1)}, u32[]{:S(2)}, u32[]{:S(2)}) async-start(f32[8,4,272]{2,1,0:T(4,128)} %all_to_all.8), calls=%async_computation | async-start | bytes 98304 | tf_op jit(solution)/shard_map/all_to_all | solution.py:348
  16.3 1.1 %copy-done.2 = bf16[576,512]{1,0:T(8,128)(2,1)S(1)} copy-done((bf16[576,512]{1,0:T(8,128)(2,1)S(1)}, bf16[576,512]{1,0:T(8,128)(2,1)}, u32[]{:S(2)}) %copy-start.2) | copy-done | bytes 589848
  17.3 2.2 %own_model.1 = (f32[32,256]{1,0:T(8,128)S(1)}, bf16[1024,512]{1,0:T(8,128)(2,1)S(1)}, bf16[384,256]{1,0:T(8,128)(2,1)S(1)}) custom-call(bf16[8,5,128,128]{3,2,1,0:T(8,128)(2,1)S(1)} %copy-done, s32[16,32]{1,0:T(8,128)S(1)} %bitcast.6, bf16[576,512]{1,0:T(8,128)(2,1)S(1)} %copy-done.2, bf16[1024,384]{1,0:T(8,128)(2,1)S(1)} %copy-done.1, ...), custom_call_target="tpu_custom_call" | custom-call | flops 4000000000 | bytes 4000000 | tf_op jit(solution)/shard_map/own_model/pallas_call | solution.py:357
  19.5 1.0 %copy-done.8 = bf16[1024,512]{1,0:T(8,128)(2,1)} copy-done((bf16[1024,512]{1,0:T(8,128)(2,1)}, bf16[1024,512]{1,0:T(8,128)(2,1)S(1)}, u32[]{:S(2)}) %copy-start.8) | copy-done | bytes 1048600
  20.7 4.4 %all-to-all-done = f32[8,4,272]{2,1,0:T(4,128)S(1)} async-done(((f32[8,4,272]{2,1,0:T(4,128)}), f32[8,4,272]{2,1,0:T(4,128)S(1)}, u32[]{:S(2)}, u32[]{:S(2)}) %all-to-all-start) | async-done | bytes 34848 | tf_op jit(solution)/shard_map/all_to_all | solution.py:348
  25.4 1.4 %mine_model.1 = f32[32,256]{1,0:T(8,128)S(1)} custom-call(bf16[576,512]{1,0:T(8,128)(2,1)S(1)} %collective-permute-done.1.message_ref.mine_ref, bf16[1024,384]{1,0:T(8,128)(2,1)S(1)} %copy-done.1, bf16[384,256]{1,0:T(8,128)(2,1)S(1)} %get-tuple-element.37.opw_ref), custom_call_target="tpu_custom_call" | custom-call | flops 2000000000 | bytes 4000000 | tf_op jit(solution)/shard_map/mine_model/pallas_call | solution.py:375
  27.4 1.4 %other_model.1 = f32[64,256]{1,0:T(8,128)S(1)} custom-call(bf16[576,512]{1,0:T(8,128)(2,1)S(1)} %collective-permute-done.2.message_ref.other_ref, f32[32,256]{1,0:T(8,128)S(1)} %get-tuple-element.35.own_ref, bf16[1024,384]{1,0:T(8,128)(2,1)S(1)} %copy-done.1, bf16[384,256]{1,0:T(8,128)(2,1)S(1)} %get-tuple-element.37.opw_ref), custom_call_target="tpu_custom_call" | custom-call | flops 2000000000 | bytes 4000000 | tf_op jit(solution)/shard_map/other_model/pallas_call | solution.py:379
  29.0 1.1 %collective-permute-done.3 = f32[64,256]{1,0:T(8,128)S(1)} collective-permute-done((f32[64,256]{1,0:T(8,128)S(1)}, f32[64,256]{1,0:T(8,128)S(1)}, u32[]{:S(2)}, u32[]{:S(2)}) %collective-permute-start.3) | collective-permute-done | bytes 65568 | tf_op jit(solution)/shard_map/ppermute | solution.py:329
  30.1 1.4 %collective-permute-start.4 = (f32[32,256]{1,0:T(8,128)S(1)}, f32[32,256]{1,0:T(8,128)S(1)}, u32[]{:S(2)}, u32[]{:S(2)}) collective-permute-start(f32[32,256]{1,0:T(8,128)S(1)} %slice_add_fusion), channel_id=1, source_target_pairs={{4,0},{6,2},{8,4},{1,5},{10,6},{3,7},{12,8},{5,9},{14,10},{7,11},{... | collective-permute-start | bytes 98312 | tf_op jit(solution)/shard_map/ppermute | solution.py:328
  31.5 0.8 %sides_turn.1 = (bf16[1024,512]{1,0:T(8,128)(2,1)S(1)}, bf16[1024,512]{1,0:T(8,128)(2,1)S(1)}) custom-call(bf16[576,512]{1,0:T(8,128)(2,1)S(1)} %collective-permute-done.1.message_ref.mine_ref, bf16[576,512]{1,0:T(8,128)(2,1)S(1)} %collective-permute-done.2.message_ref.other_ref), custom_call_target="tpu_custom_call" | custom-call | flops 4000000000 | bytes 4000000 | tf_op jit(solution)/shard_map/sides_turn/pallas_call | solution.py:384
  32.4 1.0 %copy-done.6 = bf16[1024,512]{1,0:T(8,128)(2,1)} copy-done((bf16[1024,512]{1,0:T(8,128)(2,1)}, bf16[1024,512]{1,0:T(8,128)(2,1)S(1)}, u32[]{:S(2)}) %copy-start.6) | copy-done | bytes 1048600
  33.4 1.0 %copy-done.10 = bf16[1024,512]{1,0:T(8,128)(2,1)} copy-done((bf16[1024,512]{1,0:T(8,128)(2,1)}, bf16[1024,512]{1,0:T(8,128)(2,1)S(1)}, u32[]{:S(2)}) %copy-start.10) | copy-done | bytes 1048600
  34.3 2.2 %collective-permute-done.4 = f32[32,256]{1,0:T(8,128)S(1)} collective-permute-done((f32[32,256]{1,0:T(8,128)S(1)}, f32[32,256]{1,0:T(8,128)S(1)}, u32[]{:S(2)}, u32[]{:S(2)}) %collective-permute-start.4) | collective-permute-done | bytes 32800 | tf_op jit(solution)/shard_map/ppermute | solution.py:328
  37.3 0.9 %collective-permute-done.5 = f32[32,256]{1,0:T(8,128)S(1)} collective-permute-done((f32[32,256]{1,0:T(8,128)S(1)}, f32[32,256]{1,0:T(8,128)S(1)}, u32[]{:S(2)}, u32[]{:S(2)}) %collective-permute-start.5) | collective-permute-done | bytes 32800 | tf_op jit(solution)/shard_map/ppermute | solution.py:329
  38.1 1.6 %collective-permute-start.6 = (f32[32,256]{1,0:T(8,128)S(1)}, f32[32,256]{1,0:T(8,128)S(1)}, u32[]{:S(2)}, u32[]{:S(2)}) collective-permute-start(f32[32,256]{1,0:T(8,128)S(1)} %fusion.1), channel_id=1, source_target_pairs={{0,2},{1,3},{2,0},{3,1},{4,6},{5,7},{6,4},{7,5},{8,10},{9,11},{10,... | collective-permute-start | bytes 98312 | tf_op jit(solution)/shard_map/ppermute | solution.py:329
  39.8 2.3 %collective-permute-done.6 = f32[32,256]{1,0:T(8,128)S(1)} collective-permute-done((f32[32,256]{1,0:T(8,128)S(1)}, f32[32,256]{1,0:T(8,128)S(1)}, u32[]{:S(2)}, u32[]{:S(2)}) %collective-permute-start.6) | collective-permute-done | bytes 32800 | tf_op jit(solution)/shard_map/ppermute | solution.py:329
  42.1 4.5 %collective-permute-start.7 = (f32[32,256]{1,0:T(8,128)S(1)}, f32[32,256]{1,0:T(8,128)S(1)}, u32[]{:S(2)}, u32[]{:S(2)}) collective-permute-start(f32[32,256]{1,0:T(8,128)S(1)} %subtract_multiply_fusion.misfit_ref), channel_id=1, source_target_pairs={{0,4},{2,6},{4,8},{5,1},{6,10},{7,3},{8,12},{9,5},{10,14},{11,7},{... | collective-permute-start | bytes 98312 | tf_op jit(solution)/shard_map/ppermute | solution.py:328
  46.7 1.2 %copy-done.9 = bf16[1024,512]{1,0:T(8,128)(2,1)S(1)} copy-done((bf16[1024,512]{1,0:T(8,128)(2,1)S(1)}, bf16[1024,512]{1,0:T(8,128)(2,1)}, u32[]{:S(2)}) %copy-start.9) | copy-done | bytes 1048600
  47.9 1.1 %own_adjoint.1.base_ref = f32[1024,384]{1,0:T(8,128)S(1)} custom-call(f32[32,256]{1,0:T(8,128)S(1)} %subtract_multiply_fusion.misfit_ref, bf16[576,512]{1,0:T(8,128)(2,1)S(1)} %copy-done.3, bf16[1024,512]{1,0:T(8,128)(2,1)S(1)} %copy-done.9, bf16[1024,384]{1,0:T(8,128)(2,1)S(1)} %copy-done.1, bf16[384,256]{1,0:T(8,128)(2,1)S(1)} %get-tuple-element.37.opw_ref), custom_call_target="tpu_custom_call" | custom-call | flops 2000000000 | bytes 4000000 | tf_op jit(solution)/shard_map/own_adjoint/pallas_call | solution.py:402
  49.1 1.1 %mine_adjoint.1.base_ref = f32[1024,384]{1,0:T(8,128)S(1)} custom-call(f32[32,256]{1,0:T(8,128)S(1)} %collective-permute-done.7.misfit_ref, bf16[576,512]{1,0:T(8,128)(2,1)S(1)} %collective-permute-done.1.message_ref.mine_ref, bf16[1024,512]{1,0:T(8,128)(2,1)S(1)} %copy-done.7, f32[1024,384]{1,0:T(8,128)S(1)} %own_adjoint.1.base_ref, ...), custom_call_target="tpu_custom_call" | custom-call | flops 2000000000 | bytes 4000000 | tf_op jit(solution)/shard_map/mine_adjoint/pallas_call | solution.py:402
  50.3 2.0 %other_adjoint.1 = bf16[1024,384]{1,0:T(8,128)(2,1)} custom-call(f32[32,256]{1,0:T(8,128)S(1)} %collective-permute-done.8.misfit_ref, bf16[576,512]{1,0:T(8,128)(2,1)S(1)} %collective-permute-done.2.message_ref.other_ref, bf16[1024,512]{1,0:T(8,128)(2,1)S(1)} %copy-done.11, f32[1024,384]{1,0:T(8,128)S(1)} %mine_adjoint.1.base_ref, ...), custom_call_target="tpu_custom_call" | custom-call | flops 2000000000 | bytes 4000000 | tf_op jit(solution)/shard_map/other_adjoint/pallas_call | solution.py:402
  (54 shorter events, 4.0 us)
Async XLA Ops:
  0.0 1.6 %collective-permute-start = (f32[24,1024]{1,0:T(8,128)}, f32[24,1024]{1,0:T(8,128)S(1)}, u32[]{:S(2)}, u32[]{:S(2)}) collective-permute-start(f32[24,1024]{1,0:T(8,128)} %sigma_ref.1), channel_id=1, source_target_pairs={{0,1},{1,0},{2,3},{3,2},{4,5},{5,4},{6,7},{7,6},{8,9},{9,8},{10,11... | collective-permute-start | bytes 294920 | tf_op jit(solution)/shard_map/ppermute | solution.py:329
  2.2 8.4 %copy-start.14 = (f32[32,16]{0,1:T(8,128)S(1)}, f32[32,16]{0,1:T(8,128)}, u32[]{:S(2)}) copy-start(f32[32,16]{0,1:T(8,128)} %param.18) | copy-start | bytes 6148
  2.2 8.5 %copy-start.13 = (f32[32,256]{1,0:T(8,128)S(1)}, f32[32,256]{1,0:T(8,128)}, u32[]{:S(2)}) copy-start(f32[32,256]{1,0:T(8,128)} %param.17) | copy-start | bytes 98308
  2.3 14.0 %copy-start = (bf16[8,5,128,128]{3,2,1,0:T(8,128)(2,1)S(1)}, bf16[8,5,128,128]{3,2,1,0:T(8,128)(2,1)}, u32[]{:S(2)}) copy-start(bf16[8,5,128,128]{3,2,1,0:T(8,128)(2,1)} %roots_ref.3) | copy-start | bytes 3932164
  2.3 14.0 %copy-start.1 = (bf16[1024,384]{1,0:T(8,128)(2,1)S(1)}, bf16[1024,384]{1,0:T(8,128)(2,1)}, u32[]{:S(2)}) copy-start(bf16[1024,384]{1,0:T(8,128)(2,1)} %base_ref.1) | copy-start | bytes 2359300
  2.3 14.0 %copy-start.4 = (s32[32,16]{0,1:T(8,128)S(1)}, s32[32,16]{0,1:T(8,128)}, u32[]{:S(2)}) copy-start(s32[32,16]{0,1:T(8,128)} %param.15) | copy-start | bytes 6148
  2.3 14.0 %copy-start.5 = (bf16[24,16]{0,1:T(8,128)(2,1)S(1)}, bf16[24,16]{0,1:T(8,128)(2,1)}, u32[]{:S(2)}) copy-start(bf16[24,16]{0,1:T(8,128)(2,1)} %param.14) | copy-start | bytes 2308
  5.9 19.4 %collective-permute-start.1 = (bf16[576,512]{1,0:T(8,128)(2,1)}, bf16[576,512]{1,0:T(8,128)(2,1)S(1)}, u32[]{:S(2)}, u32[]{:S(2)}) collective-permute-start(bf16[576,512]{1,0:T(8,128)(2,1)} %select.3.message_ref), channel_id=1, source_target_pairs={{0,4},{2,6},{4,8},{5,1},{6,10},{7,3},{8,12},{9,5},{10,14},{11,7},{... | collective-permute-start | bytes 1769480 | tf_op jit(solution)/shard_map/ppermute | solution.py:328
  11.4 13.7 %all-to-all-start = ((f32[8,4,272]{2,1,0:T(4,128)}), f32[8,4,272]{2,1,0:T(4,128)S(1)}, u32[]{:S(2)}, u32[]{:S(2)}) async-start(f32[8,4,272]{2,1,0:T(4,128)} %all_to_all.8), calls=%async_computation | async-start | bytes 98304 | tf_op jit(solution)/shard_map/all_to_all | solution.py:348
  16.3 1.1 %copy-start.2 = (bf16[576,512]{1,0:T(8,128)(2,1)S(1)}, bf16[576,512]{1,0:T(8,128)(2,1)}, u32[]{:S(2)}) copy-start(bf16[576,512]{1,0:T(8,128)(2,1)} %select.3.message_ref) | copy-start | bytes 1769476
  17.3 3.2 %copy-start.15 = (s32[1,8]{1,0:T(1,128)S(1)}, s32[1,8]{1,0:T(1,128)}, u32[]{:S(2)}) copy-start(s32[1,8]{1,0:T(1,128)} %param.19) | copy-start | bytes 100
  25.1 1.7 %copy-start.12 = (f32[32,272]{1,0:T(8,128)}, f32[32,272]{1,0:T(8,128)S(1)}, u32[]{:S(2)}) copy-start(f32[32,272]{1,0:T(8,128)S(1)} %all_to_all.10) | copy-start | bytes 104452
  25.3 2.1 %collective-permute-start.2 = (bf16[576,512]{1,0:T(8,128)(2,1)S(1)}, bf16[576,512]{1,0:T(8,128)(2,1)S(1)}, u32[]{:S(2)}, u32[]{:S(2)}) collective-permute-start(bf16[576,512]{1,0:T(8,128)(2,1)S(1)} %collective-permute-done.1.message_ref.mine_ref), channel_id=1, source_target_pairs={{0,1},{1,0},{2,3},{3,2},{4,5},{5,4},{6,7},{7,6},{8,9},{9,8},{10,11... | collective-permute-start | bytes 1769480 | tf_op jit(solution)/shard_map/ppermute | solution.py:329
  28.8 1.3 %collective-permute-start.3 = (f32[64,256]{1,0:T(8,128)S(1)}, f32[64,256]{1,0:T(8,128)S(1)}, u32[]{:S(2)}, u32[]{:S(2)}) collective-permute-start(f32[64,256]{1,0:T(8,128)S(1)} %other_model.1), channel_id=1, source_target_pairs={{0,1},{1,0},{2,3},{3,2},{4,5},{5,4},{6,7},{7,6},{8,9},{9,8},{10,11... | collective-permute-start | bytes 196616 | tf_op jit(solution)/shard_map/ppermute | solution.py:329
  30.1 12.0 %slice-start = ((f32[32,272]{1,0:T(8,128)}), f32[32,256]{1,0:T(8,128)S(1)}, s32[]{:S(2)}) async-start(f32[32,272]{1,0:T(8,128)} %copy-done.12), calls=%async_computation.1 | async-start | bytes 65536 | tf_op jit(solution)/shard_map/slice | solution.py:355
  30.1 16.6 %copy-start.3 = (bf16[576,512]{1,0:T(8,128)(2,1)S(1)}, bf16[576,512]{1,0:T(8,128)(2,1)}, u32[]{:S(2)}) copy-start(bf16[576,512]{1,0:T(8,128)(2,1)} %select.3.message_ref) | copy-start | bytes 1769476
  30.1 6.4 %collective-permute-start.4 = (f32[32,256]{1,0:T(8,128)S(1)}, f32[32,256]{1,0:T(8,128)S(1)}, u32[]{:S(2)}, u32[]{:S(2)}) collective-permute-start(f32[32,256]{1,0:T(8,128)S(1)} %slice_add_fusion), channel_id=1, source_target_pairs={{4,0},{6,2},{8,4},{1,5},{10,6},{3,7},{12,8},{5,9},{14,10},{7,11},{... | collective-permute-start | bytes 98312 | tf_op jit(solution)/shard_map/ppermute | solution.py:328
  36.5 1.6 %collective-permute-start.5 = (f32[32,256]{1,0:T(8,128)S(1)}, f32[32,256]{1,0:T(8,128)S(1)}, u32[]{:S(2)}, u32[]{:S(2)}) collective-permute-start(f32[32,256]{1,0:T(8,128)S(1)} %collective-permute-done.4), channel_id=1, source_target_pairs={{0,1},{1,0},{2,3},{3,2},{4,5},{5,4},{6,7},{7,6},{8,9},{9,8},{10,11... | collective-permute-start | bytes 98312 | tf_op jit(solution)/shard_map/ppermute | solution.py:329
  38.1 4.0 %collective-permute-start.6 = (f32[32,256]{1,0:T(8,128)S(1)}, f32[32,256]{1,0:T(8,128)S(1)}, u32[]{:S(2)}, u32[]{:S(2)}) collective-permute-start(f32[32,256]{1,0:T(8,128)S(1)} %fusion.1), channel_id=1, source_target_pairs={{0,2},{1,3},{2,0},{3,1},{4,6},{5,7},{6,4},{7,5},{8,10},{9,11},{10,... | collective-permute-start | bytes 98312 | tf_op jit(solution)/shard_map/ppermute | solution.py:329
  42.1 7.0 %copy-start.7 = (bf16[1024,512]{1,0:T(8,128)(2,1)S(1)}, bf16[1024,512]{1,0:T(8,128)(2,1)}, u32[]{:S(2)}) copy-start(bf16[1024,512]{1,0:T(8,128)(2,1)} %copy-done.6) | copy-start | bytes 3145732
  42.1 6.9 %collective-permute-start.7 = (f32[32,256]{1,0:T(8,128)S(1)}, f32[32,256]{1,0:T(8,128)S(1)}, u32[]{:S(2)}, u32[]{:S(2)}) collective-permute-start(f32[32,256]{1,0:T(8,128)S(1)} %subtract_multiply_fusion.misfit_ref), channel_id=1, source_target_pairs={{0,4},{2,6},{4,8},{5,1},{6,10},{7,3},{8,12},{9,5},{10,14},{11,7},{... | collective-permute-start | bytes 98312 | tf_op jit(solution)/shard_map/ppermute | solution.py:328
  46.7 1.2 %copy-start.9 = (bf16[1024,512]{1,0:T(8,128)(2,1)S(1)}, bf16[1024,512]{1,0:T(8,128)(2,1)}, u32[]{:S(2)}) copy-start(bf16[1024,512]{1,0:T(8,128)(2,1)} %copy-done.8) | copy-start | bytes 3145732
  49.0 1.3 %copy-start.11 = (bf16[1024,512]{1,0:T(8,128)(2,1)S(1)}, bf16[1024,512]{1,0:T(8,128)(2,1)}, u32[]{:S(2)}) copy-start(bf16[1024,512]{1,0:T(8,128)(2,1)} %copy-done.10) | copy-start | bytes 3145732
  49.0 1.3 %collective-permute-start.8 = (f32[32,256]{1,0:T(8,128)S(1)}, f32[32,256]{1,0:T(8,128)S(1)}, u32[]{:S(2)}, u32[]{:S(2)}) collective-permute-start(f32[32,256]{1,0:T(8,128)S(1)} %collective-permute-done.7.misfit_ref), channel_id=1, source_target_pairs={{0,1},{1,0},{2,3},{3,2},{4,5},{5,4},{6,7},{7,6},{8,9},{9,8},{10,11... | collective-permute-start | bytes 98312 | tf_op jit(solution)/shard_map/ppermute | solution.py:329
  (4 other events, 3.6 us)

commit v5 on v4

v5 whole, which is shorter than its diff:
```python
import functools

import jax
import jax.numpy as jnp
from jax import lax
from jax.experimental import pallas as pl
from jax.experimental.pallas import tpu as pltpu
from jax.sharding import PartitionSpec as P

F32 = jnp.float32
BF16 = jnp.bfloat16
NT = (((1,), (1,)), ((), ()))


def repeat_steps(count, body):
    if count <= 2:
        for step in range(count):
            body(step)
    else:
        lax.fori_loop(0, count, lambda step, carry: (body(step), carry)[1], 0)


def at(step, size):
    if isinstance(step, int):
        return pl.ds(step * size, size)
    return pl.ds(pl.multiple_of(step * size, size), size)


def dot(a, b):
    return jnp.dot(a, b, preferred_element_type=F32)


def dot_nt(a, b):
    return lax.dot_general(a, b, NT, preferred_element_type=F32)


def iota(shape, axis):
    return lax.broadcasted_iota(jnp.int32, shape, axis)


def spread_rows(values):
    points, slots = values.shape
    wide = jnp.broadcast_to(values.astype(F32)[:, None, :], (points, slots, slots))
    wide = wide.reshape(points * slots, slots)
    hit = iota(wide.shape, 1) == lax.rem(iota(wide.shape, 0), slots)
    return jnp.where(hit, wide, 0.0)


def column(values):
    return jnp.sum(spread_rows(values), axis=1, keepdims=True)


def row_of(values):
    wide = spread_rows(values)
    high = wide.astype(BF16)
    low = (wide - high.astype(F32)).astype(BF16)
    ones = jnp.ones((8, wide.shape[1]), BF16)
    return (dot_nt(ones, high) + dot_nt(ones, low))[:1]


def one_hot(cols, count):
    lane = iota((cols.shape[0], count), 1)
    return jnp.where(lane == cols.astype(jnp.int32), 1.0, 0.0).astype(BF16)


def within(value, low, count):
    return (value >= low) & (value < low + count)


def as_bf16(mask):
    return jnp.where(mask, 1.0, 0.0).astype(BF16)


def scale_spread(dims, half):
    shape = (dims.plane, dims.lanes)
    row = iota(shape, 0) - dims.vars * half
    return as_bf16(within(iota(shape, 1) - dims.members * row, 0, dims.members))


def target_spread(dims):
    shape = (dims.plane, dims.width)
    row = iota(shape, 0) - 2 * dims.vars
    return as_bf16(within(iota(shape, 1) - dims.block * row, 0, dims.block))


def roots_of(dims, rows_ref, step):
    rows = at(step, dims.chunk)
    return [rows_ref[rows, k * dims.block : (k + 1) * dims.block] for k in range(dims.others)]


def fill_operator(dims, op_ref, targets, parts):
    for q in range(dims.blocks):
        total = None
        for target, part in zip(targets, parts):
            term = jnp.where(target == jnp.asarray(q, target.dtype), part, jnp.zeros((), part.dtype))
            total = term if total is None else total + term
        op_ref[:, q * dims.block : (q + 1) * dims.block] = total


def model_rows(dims, op_ref, scale, control_ref, opw):
    summed = dot(op_ref[...], control_ref[...])
    state = (summed * scale).astype(BF16)
    bands = dot(state, opw)
    return jnp.sum(bands.reshape(dims.chunk_points, dims.slots, bands.shape[1]), axis=0)


def partner_step(tile, rank):
    return (1 - 2 * lax.rem(tile, 2)) * (1 - 2 * lax.rem(rank, 2))


def select_kernel(dims, roots_ref, cols_ref, out_ref):
    def body(step):
        hot = one_hot(column(cols_ref[at(step, dims.chunk_points), :]), dims.columns)
        for k in range(0, dims.others, 2):
            pair = range(k, min(k + 2, dims.others))
            root = jnp.concatenate(
                [roots_ref[:, i + 1].reshape(dims.columns, dims.block) for i in pair], axis=1
            )
            lanes = slice(k * dims.block, (k + len(pair)) * dims.block)
            out_ref[at(step, dims.chunk), lanes] = dot(hot, root).astype(BF16)

    repeat_steps(dims.chunks, body)


def plane_kernel(
    dims, sigma_ref, sigma2_ref, cols_ref, wgt_ref, nb_ref, obs_ref, plane_ref, opw_ref
):
    tile = lax.axis_index("space")
    half = lax.rem(lax.axis_index("var"), 2)
    bands = obs_ref.shape[0]
    flat = bands * dims.members
    shape = (dims.lanes, dims.vars)
    vars_wide = as_bf16(within(iota(shape, 0) - dims.members * iota(shape, 1), 0, dims.members))
    shape = (bands, flat)
    bands_wide = as_bf16(within(iota(shape, 1) - dims.members * iota(shape, 0), 0, dims.members))
    opw = dot(dot_nt(vars_wide, obs_ref[...]).astype(BF16), bands_wide)
    same = lax.rem(iota(opw.shape, 0), dims.members) == lax.rem(iota(opw.shape, 1), dims.members)
    opw_ref[...] = jnp.where(same, opw, 0.0).astype(BF16)
    sigma, sigma2 = sigma_ref[...], sigma2_ref[...]
    sigma = jnp.concatenate(
        [jnp.where(half == 0, sigma, sigma2), jnp.where(half == 0, sigma2, sigma)], axis=0
    )
    high = sigma.astype(BF16).astype(F32)
    nb = nb_ref[...] - (tile + partner_step(tile, half)) * dims.blocks
    nb = nb.astype(F32)
    base = 2 * dims.vars
    ids = jnp.zeros((dims.plane - base, dims.columns), F32)
    shape = ids.shape
    for b in range(dims.blocks):
        in_block = within(iota(shape, 1), b * dims.block, dims.block)
        for k in range(dims.others):
            ids = jnp.where(in_block & (iota(shape, 0) == k), nb[b : b + 1, k + 1 : k + 2], ids)
    rest = jnp.zeros_like(ids)
    table = jnp.concatenate([high, ids, sigma - high, rest], axis=0).astype(BF16)

    def body(step):
        points = at(step, dims.chunk_points)
        hot = one_hot(column(cols_ref[points, :]), dims.columns)
        plane = dot_nt(table, hot)
        scale = (plane[:base] + plane[dims.plane : dims.plane + base]) * row_of(wgt_ref[points, :])
        plane = jnp.concatenate([scale, plane[base : dims.plane]], axis=0).astype(BF16)
        plane_ref[:, at(step, dims.chunk)] = plane

    repeat_steps(dims.chunks, body)


def own_kernel(
    dims, roots_ref, cols_ref, rows_ref, plane_ref, control_ref, opw_ref, model_ref, opt_ref, op_ref
):
    half = lax.rem(lax.axis_index("var"), 2)
    opw = opw_ref[...]
    spread, targets_of = scale_spread(dims, half), target_spread(dims)
    root = roots_ref[:, 0].reshape(dims.columns, dims.block)
    shift = (partner_step(lax.axis_index("space"), half) * dims.blocks).astype(F32)

    def body(step):
        rows = at(step, dims.chunk)
        plane = plane_ref[:, rows].T
        cols = column(cols_ref[at(step, dims.chunk_points), :])
        own = jnp.floor(cols * (1.0 / dims.block))
        targets = [jnp.broadcast_to(own, (dims.chunk, dims.block)).astype(BF16)]
        parts = [dot(one_hot(cols, dims.columns), root).astype(BF16)]
        ids = (dot(plane, targets_of) + shift).astype(BF16)
        for k in range(dims.others):
            targets.append(ids[:, k * dims.block : (k + 1) * dims.block])
        parts += roots_of(dims, rows_ref, step)
        fill_operator(dims, op_ref, targets, parts)
        model = model_rows(dims, op_ref, dot(plane, spread), control_ref, opw)
        if isinstance(step, int) and step == 0:
            model_ref[...] = model
        else:
            model_ref[...] += model
        opt_ref[:, rows] = op_ref[...].T

    if dims.chunks > 2:
        model_ref[...] = jnp.zeros_like(model_ref)
    repeat_steps(dims.chunks, body)


def side_kernel(dims, rows_ref, plane_ref, control_ref, opw_ref, model_ref, op_ref):
    half = lax.rem(lax.axis_index("var"), 2)
    spread, targets_of = scale_spread(dims, half), target_spread(dims)
    opw = opw_ref[...]

    def body(step):
        plane = plane_ref[:, at(step, dims.chunk)].T
        ids = dot(plane, targets_of).astype(BF16)
        targets = [ids[:, k * dims.block : (k + 1) * dims.block] for k in range(dims.others)]
        fill_operator(dims, op_ref, targets, roots_of(dims, rows_ref, step))
        model = model_rows(dims, op_ref, dot(plane, spread), control_ref, opw)
        if isinstance(step, int) and step == 0:
            model_ref[...] = model
        else:
            model_ref[...] += model

    if dims.chunks > 2:
        model_ref[...] = jnp.zeros_like(model_ref)
    repeat_steps(dims.chunks, body)


def fill_turned(dims, opt_ref, rows_ref, plane_ref):
    def body(step):
        plane = plane_ref[:, at(step, dims.chunk)].astype(F32)
        parts = [part.T for part in roots_of(dims, rows_ref, step)]
        targets = []
        for k in range(dims.others):
            row = plane[2 * dims.vars + k : 2 * dims.vars + k + 1]
            targets.append(jnp.broadcast_to(row, (dims.block, dims.chunk)).astype(BF16))
        for q in range(dims.blocks):
            total = None
            for target, part in zip(targets, parts):
                term = jnp.where(target == jnp.asarray(q, BF16), part, jnp.zeros((), BF16))
                total = term if total is None else total + term
            opt_ref[q * dims.block : (q + 1) * dims.block, at(step, dims.chunk)] = total

    repeat_steps(dims.chunks, body)


def adjoint_kernel(dims, misfit_ref, plane_ref, opt_ref, base_ref, opw_ref, out_ref, adj_ref):
    half = lax.rem(lax.axis_index("var"), 2)
    spread = scale_spread(dims, half)
    misfit, opw = misfit_ref[...], opw_ref[...]
    high = misfit.astype(BF16)
    rest = misfit - high.astype(F32)
    middle = rest.astype(BF16)
    low = (rest - middle.astype(F32)).astype(BF16)
    pulled = dot_nt(high, opw) + (dot_nt(middle, opw) + dot_nt(low, opw))

    def body(step):
        scale = dot(plane_ref[:, at(step, dims.chunk)].T, spread)
        wide = scale.reshape(dims.chunk_points, dims.slots, dims.lanes) * pulled[None]
        adj_ref[at(step, dims.chunk), :] = wide.reshape(dims.chunk, dims.lanes).astype(BF16)

    repeat_steps(dims.chunks, body)
    for part in range(dims.columns // 256):
        rows = slice(part * 256, (part + 1) * 256)
        total = base_ref[rows, :].astype(F32) + dot(opt_ref[rows, :], adj_ref[...])
        out_ref[rows, :] = total.astype(out_ref.dtype)


def side_adjoint_kernel(
    dims, misfit_ref, plane_ref, rows_ref, base_ref, opw_ref, out_ref, adj_ref, opt_ref
):
    fill_turned(dims, opt_ref, rows_ref, plane_ref)
    adjoint_kernel(dims, misfit_ref, plane_ref, opt_ref, base_ref, opw_ref, out_ref, adj_ref)


class Dims:
    def __init__(self, control, roots, sigma, foot_cols):
        self.blocks, links, self.block = roots.shape[:3]
        self.others = links - 1
        self.columns, self.lanes = control.shape
        self.vars = sigma.shape[0]
        self.members = self.lanes // self.vars
        self.slots, self.points = foot_cols.shape
        self.rows = self.slots * self.points
        self.chunk_points = min(self.points, max(8, 512 // self.slots))
        self.chunk = self.chunk_points * self.slots
        self.chunks = self.rows // self.chunk
        self.width = self.others * self.block
        self.plane = 64


def call(dims, kernel, name, out_shape, scratch, flops, limit=None):
    limit = (limit or min(56, max(16, dims.rows // 32))) * 1024 * 1024
    return pl.pallas_call(
        functools.partial(kernel, dims),
        out_shape=out_shape,
        scratch_shapes=scratch,
        compiler_params=pltpu.CompilerParams(vmem_limit_bytes=limit),
        cost_estimate=pl.CostEstimate(flops=flops, bytes_accessed=4000000, transcendentals=0),
        name=name,
    )


def shards(
    control,
    roots,
    neighbours,
    sigma,
    obs_op,
    foot_cols,
    foot_wgt,
    obs_value,
    obs_rinv,
    owner_counts,
):
    dims = Dims(control, roots, sigma, foot_cols)
    bands = obs_op.shape[1]
    members = dims.members
    tiles = lax.axis_size("space")
    ranks = lax.axis_size("var")
    partners = []
    for t in range(tiles):
        for v in range(ranks):
            to = t + (1 - 2 * (t % 2)) * (1 - 2 * (v % 2))
            if 0 <= to < tiles:
                partners.append((t * ranks + v, to * ranks + v))
    hop = lambda x: lax.ppermute(x, ("space", "var"), partners)
    swap = lambda x, bit: lax.ppermute(x, "var", [(i, i ^ bit) for i in range(ranks)])
    shape = jax.ShapeDtypeStruct
    flat = bands * members
    cols_t, wgt_t = foot_cols.T, foot_wgt.T

    sigma2 = swap(sigma, 1)
    picked = call(
        dims, select_kernel, "select", shape((dims.rows, dims.width), BF16), [], 2000000000, 56
    )(roots, cols_t)
    mine = hop(picked)
    picked, sigma2 = lax.optimization_barrier((picked, sigma2))
    plane, opw = call(
        dims,
        plane_kernel,
        "plane",
        (shape((dims.plane, dims.rows), BF16), shape((dims.lanes, flat), BF16)),
        [],
        1000000000,
    )(sigma, sigma2, cols_t, wgt_t, neighbours, obs_op.T)
    mine_plane = hop(plane)
    plane, obs_value, obs_rinv, owner_counts = lax.optimization_barrier(
        (plane, obs_value, obs_rinv, owner_counts)
    )
    observed = lax.all_to_all(
        jnp.concatenate([obs_value, obs_rinv], axis=1), "space", 0, 0, tiled=True
    )
    capacity = dims.slots // owner_counts.shape[1]
    slot_ids = jnp.arange(dims.slots, dtype=jnp.int32)
    live = slot_ids % capacity < jnp.repeat(owner_counts[0], capacity)
    rinv = jnp.repeat(jnp.where(live[:, None], observed[:, flat:], 0.0), members, axis=1)
    value = observed[:, :flat]

    mine, mine_plane, rinv, value = lax.optimization_barrier((mine, mine_plane, rinv, value))
    other, other_plane = swap(mine, 1), swap(mine_plane, 1)
    op_scratch = [pltpu.VMEM((dims.chunk, dims.columns), BF16)]
    keep = call(
        dims, side_kernel, "mine_model", shape((dims.slots, flat), F32), op_scratch, 2000000000
    )(mine, mine_plane, control, opw)
    other, keep = lax.optimization_barrier((other, keep))
    give = call(
        dims, side_kernel, "other_model", shape((dims.slots, flat), F32), op_scratch, 2000000000
    )(other, other_plane, control, opw)
    arrived = hop(keep + swap(give, 1))
    give, own_picked = lax.optimization_barrier((give, picked))
    own_model, own_opt = call(
        dims,
        own_kernel,
        "own_model",
        (shape((dims.slots, flat), F32), shape((dims.columns, dims.rows), BF16)),
        op_scratch,
        4000000000,
    )(roots, cols_t, own_picked, plane, control, opw)
    arrived, own_model, own_opt = lax.optimization_barrier((arrived, own_model, own_opt))
    modelled = arrived + own_model
    bit = 1
    while bit < ranks:
        modelled = modelled + swap(modelled, bit)
        bit *= 2
    misfit = rinv * (modelled - value)
    misfit_mine = hop(misfit)

    def add_adjoint(kernel, name, dtype, scratch, *operands):
        return call(
            dims,
            kernel,
            name,
            shape((dims.columns, dims.lanes), dtype),
            [pltpu.VMEM((dims.rows, dims.lanes), BF16)] + scratch,
            2000000000,
        )(*operands, opw)

    total = add_adjoint(
        adjoint_kernel, "own_adjoint", F32, [], misfit, plane, own_opt, control
    )
    misfit_mine, total = lax.optimization_barrier((misfit_mine, total))
    misfit_other = swap(misfit_mine, 1)
    turned = [pltpu.VMEM((dims.columns, dims.rows), BF16)]
    total = add_adjoint(
        side_adjoint_kernel, "mine_adjoint", F32, turned, misfit_mine, mine_plane, mine, total
    )
    misfit_other, total = lax.optimization_barrier((misfit_other, total))
    return add_adjoint(
        side_adjoint_kernel, "other_adjoint", BF16, turned, misfit_other, other_plane, other, total
    )


def solution(mesh):
    return jax.shard_map(
        shards,
        mesh=mesh,
        in_specs=(
            P("space", "var"),
            P("space", None, None, None),
            P("space", None),
            P("var", "space"),
            P("var", None),
            P("space", None),
            P("space", None),
            P("space", None),
            P("space", None),
            P("space", None),
        ),
        out_specs=P("space", "var"),
        check_vma=False,
    )
```

time: 52.6 us -> 49.9 us (0.949)
  local copies, waits for them, and re-layouts: 6.95 us -> 1.11 us
  waiting for transfers between devices: 12.7 us -> 14.9 us
  starting transfers between devices: 18.7 us -> 20.4 us
  Pallas kernels: 13.6 us -> 12.8 us
    unnamed x34 -> x24, local copies, waits for them, and re-layouts: 5.93 us -> 0.09 us
    all_to_all x1, waiting for transfers between devices: 4.39 us -> 6.79 us  [shards(): lax.all_to_all(jnp.concatenate([obs_value, obs_rinv], axis=1), 'space', 0...]
    all_to_all x1, starting transfers between devices: 4.85 us -> 6.33 us  [shards(): lax.all_to_all(jnp.concatenate([obs_value, obs_rinv], axis=1), 'space', 0...]
    ppermute x6 -> x7, waiting for transfers between devices: 6.11 us -> 4.74 us  [shards(): lax.ppermute(x, 'var', [(i, i ^ bit) for i in range(ranks)])]
    ppermute x3 -> x4, waiting for transfers between devices: 2.16 us -> 3.37 us  [shards(): hop = lambda x: lax.ppermute(x, ('space', 'var'), partners)]
    pallas_call x6, Pallas kernels: 9.98 us -> 9.26 us  [the longest x3 4.14 us: add_adjoint(): call(dims, kernel, name, shape((dims.columns, dims.lanes), dtype), [pltpu...]
    ppermute x3 -> x4, starting transfers between devices: 10.7 us -> 11.3 us  [shards(): hop = lambda x: lax.ppermute(x, ('space', 'var'), partners)]
    ppermute x6 -> x7, starting transfers between devices: 3.13 us -> 2.7 us  [shards(): lax.ppermute(x, 'var', [(i, i ^ bit) for i in range(ranks)])]
  transfers between devices with their start and end apart: 10 -> 12, of which waited for: 8 -> 7; matrix products, arithmetic and copies ran while one was open for 1% -> 1% of each run, Pallas kernels for 13% -> 19%
where the time goes in v5:
time: 49.9 us; the launch traced here: 49.5 us
  starting transfers between devices  20.4 us (41%)
  waiting for transfers between devices  14.9 us (30%)
  Pallas kernels  12.8 us (26%)
  local copies, waits for them, and re-layouts  1.11 us (2%)
    ppermute x4, starting transfers between devices, shards(): hop = lambda x: lax.ppermute(x, ('space', 'var'), partners)  11.3 us
    all_to_all x1, waiting for transfers between devices, shards(): lax.all_to_all(jnp.concatenate([obs_value, obs_rinv], axis=1), 'space', 0...  6.79 us
    all_to_all x1, starting transfers between devices, shards(): lax.all_to_all(jnp.concatenate([obs_value, obs_rinv], axis=1), 'space', 0...  6.33 us
    ppermute x7, waiting for transfers between devices, shards(): lax.ppermute(x, 'var', [(i, i ^ bit) for i in range(ranks)])  4.74 us
    pallas_call x3, Pallas kernels, add_adjoint(): call(dims, kernel, name, shape((dims.columns, dims.lanes), dtype), [pltpu...  4.14 us
    ppermute x4, waiting for transfers between devices, shards(): hop = lambda x: lax.ppermute(x, ('space', 'var'), partners)  3.37 us
    pallas_call x1, Pallas kernels, shards(): call(dims, select_kernel, 'select', shape((dims.rows, dims.width), BF16),...  2.96 us
    ppermute x7, starting transfers between devices, shards(): lax.ppermute(x, 'var', [(i, i ^ bit) for i in range(ranks)])  2.7 us
  transfers between devices with their start and end apart: 12, of which 7 were waited for; matrix products, arithmetic and copies ran while one was open for 1% of the time, Pallas kernels for 19%

profile of v5, /device:TPU:0, one launch (start us, length us, event | category | flops | bytes accessed | tf_op | source)
XLA Modules:
  0.0 49.5 jit_solution(2969916643742098500)
XLA Ops:
  0.0 0.5 collective-permute-start.1
  0.5 3.0 %select.3.rows_ref = bf16[512,512]{1,0:T(8,128)(2,1)} custom-call(bf16[8,5,128,128]{3,2,1,0:T(8,128)(2,1)} %roots_ref.3, s32[16,32]{1,0:T(8,128)} %bitcast.6), custom_call_target="tpu_custom_call" | custom-call | flops 2000000000 | bytes 4000000 | tf_op jit(solution)/shard_map/select/pallas_call | solution.py:326
  3.4 4.4 %collective-permute-start = (bf16[512,512]{1,0:T(8,128)(2,1)}, bf16[512,512]{1,0:T(8,128)(2,1)S(1)}, u32[]{:S(2)}, u32[]{:S(2)}) collective-permute-start(bf16[512,512]{1,0:T(8,128)(2,1)} %select.3.rows_ref), channel_id=1, source_target_pairs={{0,4},{2,6},{4,0},{5,9},{6,2},{7,11},{8,12},{9,5},{10,14},{11,7},{... | collective-permute-start | bytes 1572872 | tf_op jit(solution)/shard_map/ppermute | solution.py:319
  7.9 0.7 %plane.1 = (bf16[64,512]{1,0:T(8,128)(2,1)S(1)}, bf16[384,256]{1,0:T(8,128)(2,1)S(1)}) custom-call(f32[24,1024]{1,0:T(8,128)S(1)} %copy-done.3, f32[24,1024]{1,0:T(8,128)S(1)} %collective-permute-done.1.sigma2_ref, s32[16,32]{1,0:T(8,128)S(1)} %bitcast.7, f32[16,32]{1,0:T(8,128)S(1)} %bitcast.5, s32[8,5]{1,0:T(8,128)S(1)} %copy-done.6, ...), custom_call_target="tpu_custom_call" | custom-call | flops 1000000000 | bytes 4000000 | tf_op jit(solution)/shard_map/plane/pallas_call | solution.py:331
  8.7 1.9 %collective-permute-start.2 = (bf16[64,512]{1,0:T(8,128)(2,1)S(1)}, bf16[64,512]{1,0:T(8,128)(2,1)S(1)}, u32[]{:S(2)}, u32[]{:S(2)}) collective-permute-start(bf16[64,512]{1,0:T(8,128)(2,1)S(1)} %get-tuple-element.42.plane_ref), channel_id=1, source_target_pairs={{0,4},{2,6},{4,0},{5,9},{6,2},{7,11},{8,12},{9,5},{10,14},{11,7},{... | collective-permute-start | bytes 196616 | tf_op jit(solution)/shard_map/ppermute | solution.py:319
  10.8 0.6 %all_to_all.8 = f32[8,4,272]{2,1,0:T(4,128)} reshape(f32[32,272]{1,0:T(8,128)S(1)} %pad_maximum_fusion) | data formatting | bytes 69632 | tf_op jit(solution)/shard_map/all_to_all | solution.py:343
  11.5 6.3 %all-to-all-start = ((f32[8,4,272]{2,1,0:T(4,128)}), f32[8,4,272]{2,1,0:T(4,128)S(1)}, u32[]{:S(2)}, u32[]{:S(2)}) async-start(f32[8,4,272]{2,1,0:T(4,128)} %all_to_all.8), calls=%async_computation | async-start | bytes 98304 | tf_op jit(solution)/shard_map/all_to_all | solution.py:343
  17.8 6.8 %all-to-all-done = f32[8,4,272]{2,1,0:T(4,128)S(1)} async-done(((f32[8,4,272]{2,1,0:T(4,128)}), f32[8,4,272]{2,1,0:T(4,128)S(1)}, u32[]{:S(2)}, u32[]{:S(2)}) %all-to-all-start) | async-done | bytes 34848 | tf_op jit(solution)/shard_map/all_to_all | solution.py:343
  24.9 0.5 %collective-permute-start.4 = (bf16[64,512]{1,0:T(8,128)(2,1)S(1)}, bf16[64,512]{1,0:T(8,128)(2,1)S(1)}, u32[]{:S(2)}, u32[]{:S(2)}) collective-permute-start(bf16[64,512]{1,0:T(8,128)(2,1)S(1)} %collective-permute-done.2.plane_ref), channel_id=1, source_target_pairs={{0,1},{1,0},{2,3},{3,2},{4,5},{5,4},{6,7},{7,6},{8,9},{9,8},{10,11... | collective-permute-start | bytes 196616 | tf_op jit(solution)/shard_map/ppermute | solution.py:320
  25.4 1.4 %mine_model.1 = f32[32,256]{1,0:T(8,128)S(1)} custom-call(bf16[512,512]{1,0:T(8,128)(2,1)S(1)} %collective-permute-done.rows_ref, bf16[64,512]{1,0:T(8,128)(2,1)S(1)} %collective-permute-done.2.plane_ref, bf16[1024,384]{1,0:T(8,128)(2,1)S(1)} %copy-done.1, bf16[384,256]{1,0:T(8,128)(2,1)S(1)} %get-tuple-element.37.opw_ref), custom_call_target="tpu_custom_call" | custom-call | flops 2000000000 | bytes 4000000 | tf_op jit(solution)/shard_map/mine_model/pallas_call | solution.py:355
  26.9 1.4 %other_model.1 = f32[32,256]{1,0:T(8,128)S(1)} custom-call(bf16[512,512]{1,0:T(8,128)(2,1)S(1)} %collective-permute-done.3.rows_ref, bf16[64,512]{1,0:T(8,128)(2,1)S(1)} %collective-permute-done.4.plane_ref, bf16[1024,384]{1,0:T(8,128)(2,1)S(1)} %copy-done.1, bf16[384,256]{1,0:T(8,128)(2,1)S(1)} %get-tuple-element.37.opw_ref), custom_call_target="tpu_custom_call" | custom-call | flops 2000000000 | bytes 4000000 | tf_op jit(solution)/shard_map/other_model/pallas_call | solution.py:359
  28.3 0.2 collective-permute-start.5
  28.5 1.1 %collective-permute-done.5 = f32[32,256]{1,0:T(8,128)S(1)} collective-permute-done((f32[32,256]{1,0:T(8,128)S(1)}, f32[32,256]{1,0:T(8,128)S(1)}, u32[]{:S(2)}, u32[]{:S(2)}) %collective-permute-start.5) | collective-permute-done | bytes 32800 | tf_op jit(solution)/shard_map/ppermute | solution.py:320
  29.6 2.3 %collective-permute-start.6 = (f32[32,256]{1,0:T(8,128)S(1)}, f32[32,256]{1,0:T(8,128)S(1)}, u32[]{:S(2)}, u32[]{:S(2)}) collective-permute-start(f32[32,256]{1,0:T(8,128)S(1)} %add.23), channel_id=1, source_target_pairs={{0,4},{2,6},{4,0},{5,9},{6,2},{7,11},{8,12},{9,5},{10,14},{11,7},{... | collective-permute-start | bytes 98312 | tf_op jit(solution)/shard_map/ppermute | solution.py:319
  32.0 2.1 %own_model.1 = (f32[32,256]{1,0:T(8,128)S(1)}, bf16[1024,512]{1,0:T(8,128)(2,1)S(1)}) custom-call(bf16[8,5,128,128]{3,2,1,0:T(8,128)(2,1)S(1)} %copy-done, s32[16,32]{1,0:T(8,128)S(1)} %bitcast.8, bf16[512,512]{1,0:T(8,128)(2,1)S(1)} %copy-done.2, bf16[64,512]{1,0:T(8,128)(2,1)S(1)} %get-tuple-element.42.plane_ref, bf16[1024,384]{1,0:T(8,128)(2,1)S(1)} %copy-done.1, ...), custom_call_target="tpu_custom_call" | custom-call | flops 4000000000 | bytes 4000000 | tf_op jit(solution)/shard_map/own_model/pallas_call | solution.py:364
  34.1 1.3 %collective-permute-done.6 = f32[32,256]{1,0:T(8,128)S(1)} collective-permute-done((f32[32,256]{1,0:T(8,128)S(1)}, f32[32,256]{1,0:T(8,128)S(1)}, u32[]{:S(2)}, u32[]{:S(2)}) %collective-permute-start.6) | collective-permute-done | bytes 32800 | tf_op jit(solution)/shard_map/ppermute | solution.py:319
  35.4 1.2 %collective-permute-done.7 = f32[32,256]{1,0:T(8,128)S(1)} collective-permute-done((f32[32,256]{1,0:T(8,128)S(1)}, f32[32,256]{1,0:T(8,128)S(1)}, u32[]{:S(2)}, u32[]{:S(2)}) %collective-permute-start.7) | collective-permute-done | bytes 32800 | tf_op jit(solution)/shard_map/ppermute | solution.py:320
  36.6 1.5 %collective-permute-start.8 = (f32[32,256]{1,0:T(8,128)S(1)}, f32[32,256]{1,0:T(8,128)S(1)}, u32[]{:S(2)}, u32[]{:S(2)}) collective-permute-start(f32[32,256]{1,0:T(8,128)S(1)} %add.25), channel_id=1, source_target_pairs={{0,2},{1,3},{2,0},{3,1},{4,6},{5,7},{6,4},{7,5},{8,10},{9,11},{10,... | collective-permute-start | bytes 98312 | tf_op jit(solution)/shard_map/ppermute | solution.py:320
  38.2 2.3 %collective-permute-done.8 = f32[32,256]{1,0:T(8,128)S(1)} collective-permute-done((f32[32,256]{1,0:T(8,128)S(1)}, f32[32,256]{1,0:T(8,128)S(1)}, u32[]{:S(2)}, u32[]{:S(2)}) %collective-permute-start.8) | collective-permute-done | bytes 32800 | tf_op jit(solution)/shard_map/ppermute | solution.py:320
  40.6 2.7 %collective-permute-start.9 = (f32[32,256]{1,0:T(8,128)S(1)}, f32[32,256]{1,0:T(8,128)S(1)}, u32[]{:S(2)}, u32[]{:S(2)}) collective-permute-start(f32[32,256]{1,0:T(8,128)S(1)} %subtract_multiply_fusion.misfit_ref), channel_id=1, source_target_pairs={{0,4},{2,6},{4,0},{5,9},{6,2},{7,11},{8,12},{9,5},{10,14},{11,7},{... | collective-permute-start | bytes 98312 | tf_op jit(solution)/shard_map/ppermute | solution.py:319
  43.3 1.1 %own_adjoint.1.base_ref = f32[1024,384]{1,0:T(8,128)S(1)} custom-call(f32[32,256]{1,0:T(8,128)S(1)} %subtract_multiply_fusion.misfit_ref, bf16[64,512]{1,0:T(8,128)(2,1)S(1)} %get-tuple-element.42.plane_ref, bf16[1024,512]{1,0:T(8,128)(2,1)S(1)} %get-tuple-element.48.opt_ref, bf16[1024,384]{1,0:T(8,128)(2,1)S(1)} %copy-done.1, ...), custom_call_target="tpu_custom_call" | custom-call | flops 2000000000 | bytes 4000000 | tf_op jit(solution)/shard_map/own_adjoint/pallas_call | solution.py:382
  44.3 2.0 %collective-permute-done.9.misfit_ref = f32[32,256]{1,0:T(8,128)S(1)} collective-permute-done((f32[32,256]{1,0:T(8,128)S(1)}, f32[32,256]{1,0:T(8,128)S(1)}, u32[]{:S(2)}, u32[]{:S(2)}) %collective-permute-start.9) | collective-permute-done | bytes 32800 | tf_op jit(solution)/shard_map/ppermute | solution.py:319
  46.4 1.1 %mine_adjoint.1.base_ref = f32[1024,384]{1,0:T(8,128)S(1)} custom-call(f32[32,256]{1,0:T(8,128)S(1)} %collective-permute-done.9.misfit_ref, bf16[64,512]{1,0:T(8,128)(2,1)S(1)} %collective-permute-done.2.plane_ref, bf16[512,512]{1,0:T(8,128)(2,1)S(1)} %collective-permute-done.rows_ref, f32[1024,384]{1,0:T(8,128)S(1)} %own_adjoint.1.base_ref, ...), custom_call_target="tpu_custom_call" | custom-call | flops 2000000000 | bytes 4000000 | tf_op jit(solution)/shard_map/mine_adjoint/pallas_call | solution.py:382
  47.6 2.0 %other_adjoint.1 = bf16[1024,384]{1,0:T(8,128)(2,1)} custom-call(f32[32,256]{1,0:T(8,128)S(1)} %collective-permute-done.10.misfit_ref, bf16[64,512]{1,0:T(8,128)(2,1)S(1)} %collective-permute-done.4.plane_ref, bf16[512,512]{1,0:T(8,128)(2,1)S(1)} %collective-permute-done.3.rows_ref, f32[1024,384]{1,0:T(8,128)S(1)} %mine_adjoint.1.base_ref, ...), custom_call_target="tpu_custom_call" | custom-call | flops 2000000000 | bytes 4000000 | tf_op jit(solution)/shard_map/other_adjoint/pallas_call | solution.py:382
  (49 shorter events, 0.8 us)
Async XLA Ops:
  0.0 7.8 %collective-permute-start.1 = (f32[24,1024]{1,0:T(8,128)}, f32[24,1024]{1,0:T(8,128)S(1)}, u32[]{:S(2)}, u32[]{:S(2)}) collective-permute-start(f32[24,1024]{1,0:T(8,128)} %sigma_ref.1), channel_id=1, source_target_pairs={{0,1},{1,0},{2,3},{3,2},{4,5},{5,4},{6,7},{7,6},{8,9},{9,8},{10,11... | collective-permute-start | bytes 294920 | tf_op jit(solution)/shard_map/ppermute | solution.py:320
  0.5 7.4 %copy-start.3 = (f32[24,1024]{1,0:T(8,128)S(1)}, f32[24,1024]{1,0:T(8,128)}, u32[]{:S(2)}) copy-start(f32[24,1024]{1,0:T(8,128)} %sigma_ref.1) | copy-start | bytes 294916
  0.5 7.4 %copy-start.4 = (f32[32,16]{0,1:T(8,128)S(1)}, f32[32,16]{0,1:T(8,128)}, u32[]{:S(2)}) copy-start(f32[32,16]{0,1:T(8,128)} %param.16) | copy-start | bytes 6148
  0.5 7.4 %copy-start.5 = (s32[32,16]{0,1:T(8,128)S(1)}, s32[32,16]{0,1:T(8,128)}, u32[]{:S(2)}) copy-start(s32[32,16]{0,1:T(8,128)} %param.15) | copy-start | bytes 6148
  0.5 7.4 %copy-start.6 = (s32[8,5]{1,0:T(8,128)S(1)}, s32[8,5]{1,0:T(8,128)}, u32[]{:S(2)}) copy-start(s32[8,5]{1,0:T(8,128)} %nb_ref.1) | copy-start | bytes 484
  0.5 7.4 %copy-start.7 = (bf16[24,16]{0,1:T(8,128)(2,1)S(1)}, bf16[24,16]{0,1:T(8,128)(2,1)}, u32[]{:S(2)}) copy-start(bf16[24,16]{0,1:T(8,128)(2,1)} %param.14) | copy-start | bytes 2308
  3.4 21.3 %collective-permute-start = (bf16[512,512]{1,0:T(8,128)(2,1)}, bf16[512,512]{1,0:T(8,128)(2,1)S(1)}, u32[]{:S(2)}, u32[]{:S(2)}) collective-permute-start(bf16[512,512]{1,0:T(8,128)(2,1)} %select.3.rows_ref), channel_id=1, source_target_pairs={{0,4},{2,6},{4,0},{5,9},{6,2},{7,11},{8,12},{9,5},{10,14},{11,7},{... | collective-permute-start | bytes 1572872 | tf_op jit(solution)/shard_map/ppermute | solution.py:319
  7.9 2.7 %copy-start.11 = (s32[1,8]{1,0:T(1,128)S(1)}, s32[1,8]{1,0:T(1,128)}, u32[]{:S(2)}) copy-start(s32[1,8]{1,0:T(1,128)} %param.19) | copy-start | bytes 100
  7.9 2.8 %copy-start.10 = (f32[32,16]{0,1:T(8,128)S(1)}, f32[32,16]{0,1:T(8,128)}, u32[]{:S(2)}) copy-start(f32[32,16]{0,1:T(8,128)} %param.18) | copy-start | bytes 6148
  7.9 2.9 %copy-start.9 = (f32[32,256]{1,0:T(8,128)S(1)}, f32[32,256]{1,0:T(8,128)}, u32[]{:S(2)}) copy-start(f32[32,256]{1,0:T(8,128)} %param.17) | copy-start | bytes 98308
  7.9 17.5 %copy-start.1 = (bf16[1024,384]{1,0:T(8,128)(2,1)S(1)}, bf16[1024,384]{1,0:T(8,128)(2,1)}, u32[]{:S(2)}) copy-start(bf16[1024,384]{1,0:T(8,128)(2,1)} %base_ref.1) | copy-start | bytes 2359300
  8.7 16.1 %collective-permute-start.2 = (bf16[64,512]{1,0:T(8,128)(2,1)S(1)}, bf16[64,512]{1,0:T(8,128)(2,1)S(1)}, u32[]{:S(2)}, u32[]{:S(2)}) collective-permute-start(bf16[64,512]{1,0:T(8,128)(2,1)S(1)} %get-tuple-element.42.plane_ref), channel_id=1, source_target_pairs={{0,4},{2,6},{4,0},{5,9},{6,2},{7,11},{8,12},{9,5},{10,14},{11,7},{... | collective-permute-start | bytes 196616 | tf_op jit(solution)/shard_map/ppermute | solution.py:319
  11.5 13.1 %all-to-all-start = ((f32[8,4,272]{2,1,0:T(4,128)}), f32[8,4,272]{2,1,0:T(4,128)S(1)}, u32[]{:S(2)}, u32[]{:S(2)}) async-start(f32[8,4,272]{2,1,0:T(4,128)} %all_to_all.8), calls=%async_computation | async-start | bytes 98304 | tf_op jit(solution)/shard_map/all_to_all | solution.py:343
  24.8 2.1 %collective-permute-start.3 = (bf16[512,512]{1,0:T(8,128)(2,1)S(1)}, bf16[512,512]{1,0:T(8,128)(2,1)S(1)}, u32[]{:S(2)}, u32[]{:S(2)}) collective-permute-start(bf16[512,512]{1,0:T(8,128)(2,1)S(1)} %collective-permute-done.rows_ref), channel_id=1, source_target_pairs={{0,1},{1,0},{2,3},{3,2},{4,5},{5,4},{6,7},{7,6},{8,9},{9,8},{10,11... | collective-permute-start | bytes 1572872 | tf_op jit(solution)/shard_map/ppermute | solution.py:320
  24.9 2.0 %collective-permute-start.4 = (bf16[64,512]{1,0:T(8,128)(2,1)S(1)}, bf16[64,512]{1,0:T(8,128)(2,1)S(1)}, u32[]{:S(2)}, u32[]{:S(2)}) collective-permute-start(bf16[64,512]{1,0:T(8,128)(2,1)S(1)} %collective-permute-done.2.plane_ref), channel_id=1, source_target_pairs={{0,1},{1,0},{2,3},{3,2},{4,5},{5,4},{6,7},{7,6},{8,9},{9,8},{10,11... | collective-permute-start | bytes 196616 | tf_op jit(solution)/shard_map/ppermute | solution.py:320
  26.8 5.1 %copy-start = (bf16[8,5,128,128]{3,2,1,0:T(8,128)(2,1)S(1)}, bf16[8,5,128,128]{3,2,1,0:T(8,128)(2,1)}, u32[]{:S(2)}) copy-start(bf16[8,5,128,128]{3,2,1,0:T(8,128)(2,1)} %roots_ref.3) | copy-start | bytes 3932164
  26.9 5.1 %copy-start.2 = (bf16[512,512]{1,0:T(8,128)(2,1)S(1)}, bf16[512,512]{1,0:T(8,128)(2,1)}, u32[]{:S(2)}) copy-start(bf16[512,512]{1,0:T(8,128)(2,1)} %select.3.rows_ref) | copy-start | bytes 1572868
  28.3 1.2 %collective-permute-start.5 = (f32[32,256]{1,0:T(8,128)S(1)}, f32[32,256]{1,0:T(8,128)S(1)}, u32[]{:S(2)}, u32[]{:S(2)}) collective-permute-start(f32[32,256]{1,0:T(8,128)S(1)} %other_model.1), channel_id=1, source_target_pairs={{0,1},{1,0},{2,3},{3,2},{4,5},{5,4},{6,7},{7,6},{8,9},{9,8},{10,11... | collective-permute-start | bytes 98312 | tf_op jit(solution)/shard_map/ppermute | solution.py:320
  29.6 11.0 %slice-start = ((f32[32,272]{1,0:T(8,128)}), f32[32,256]{1,0:T(8,128)S(1)}, s32[]{:S(2)}) async-start(f32[32,272]{1,0:T(8,128)} %copy-done.8), calls=%async_computation.1 | async-start | bytes 65536 | tf_op jit(solution)/shard_map/slice | solution.py:350
  29.6 5.8 %collective-permute-start.6 = (f32[32,256]{1,0:T(8,128)S(1)}, f32[32,256]{1,0:T(8,128)S(1)}, u32[]{:S(2)}, u32[]{:S(2)}) collective-permute-start(f32[32,256]{1,0:T(8,128)S(1)} %add.23), channel_id=1, source_target_pairs={{0,4},{2,6},{4,0},{5,9},{6,2},{7,11},{8,12},{9,5},{10,14},{11,7},{... | collective-permute-start | bytes 98312 | tf_op jit(solution)/shard_map/ppermute | solution.py:319
  35.4 1.2 %collective-permute-start.7 = (f32[32,256]{1,0:T(8,128)S(1)}, f32[32,256]{1,0:T(8,128)S(1)}, u32[]{:S(2)}, u32[]{:S(2)}) collective-permute-start(f32[32,256]{1,0:T(8,128)S(1)} %add.24), channel_id=1, source_target_pairs={{0,1},{1,0},{2,3},{3,2},{4,5},{5,4},{6,7},{7,6},{8,9},{9,8},{10,11... | collective-permute-start | bytes 98312 | tf_op jit(solution)/shard_map/ppermute | solution.py:320
  36.6 3.9 %collective-permute-start.8 = (f32[32,256]{1,0:T(8,128)S(1)}, f32[32,256]{1,0:T(8,128)S(1)}, u32[]{:S(2)}, u32[]{:S(2)}) collective-permute-start(f32[32,256]{1,0:T(8,128)S(1)} %add.25), channel_id=1, source_target_pairs={{0,2},{1,3},{2,0},{3,1},{4,6},{5,7},{6,4},{7,5},{8,10},{9,11},{10,... | collective-permute-start | bytes 98312 | tf_op jit(solution)/shard_map/ppermute | solution.py:320
  40.6 5.8 %collective-permute-start.9 = (f32[32,256]{1,0:T(8,128)S(1)}, f32[32,256]{1,0:T(8,128)S(1)}, u32[]{:S(2)}, u32[]{:S(2)}) collective-permute-start(f32[32,256]{1,0:T(8,128)S(1)} %subtract_multiply_fusion.misfit_ref), channel_id=1, source_target_pairs={{0,4},{2,6},{4,0},{5,9},{6,2},{7,11},{8,12},{9,5},{10,14},{11,7},{... | collective-permute-start | bytes 98312 | tf_op jit(solution)/shard_map/ppermute | solution.py:319
  46.4 1.2 %collective-permute-start.10 = (f32[32,256]{1,0:T(8,128)S(1)}, f32[32,256]{1,0:T(8,128)S(1)}, u32[]{:S(2)}, u32[]{:S(2)}) collective-permute-start(f32[32,256]{1,0:T(8,128)S(1)} %collective-permute-done.9.misfit_ref), channel_id=1, source_target_pairs={{0,1},{1,0},{2,3},{3,2},{4,5},{5,4},{6,7},{7,6},{8,9},{9,8},{10,11... | collective-permute-start | bytes 98312 | tf_op jit(solution)/shard_map/ppermute | solution.py:320
  (1 other events, 2.2 us)

commit v6 on v5

--- a/solution.py
+++ b/solution.py
@@ -236,7 +236,9 @@
     repeat_steps(dims.chunks, body)
 
 
-def adjoint_kernel(dims, misfit_ref, plane_ref, opt_ref, base_ref, opw_ref, out_ref, adj_ref):
+def adjoint_kernel(
+    dims, misfit_ref, plane_ref, opt_ref, base_ref, opw_ref, out_ref, adj_ref, finish=None
+):
     half = lax.rem(lax.axis_index("var"), 2)
     spread = scale_spread(dims, half)
     misfit, opw = misfit_ref[...], opw_ref[...]
@@ -256,6 +258,8 @@
         rows = slice(part * 256, (part + 1) * 256)
         total = base_ref[rows, :].astype(F32) + dot(opt_ref[rows, :], adj_ref[...])
         out_ref[rows, :] = total.astype(out_ref.dtype)
+        if finish is not None:
+            finish(part, rows)
 
 
 def side_adjoint_kernel(
@@ -263,6 +267,23 @@
 ):
     fill_turned(dims, opt_ref, rows_ref, plane_ref)
     adjoint_kernel(dims, misfit_ref, plane_ref, opt_ref, base_ref, opw_ref, out_ref, adj_ref)
+
+
+def last_adjoint_kernel(
+    dims, misfit_ref, plane_ref, rows_ref, base_ref, opw_ref, out_hbm, adj_ref, opt_ref, out_ref, sems
+):
+    copies = []
+
+    def finish(part, rows):
+        copies.append(pltpu.make_async_copy(out_ref.at[rows], out_hbm.at[rows], sems.at[part]))
+        copies[-1].start()
+
+    fill_turned(dims, opt_ref, rows_ref, plane_ref)
+    adjoint_kernel(
+        dims, misfit_ref, plane_ref, opt_ref, base_ref, opw_ref, out_ref, adj_ref, finish
+    )
+    for copy in copies:
+        copy.wait()
 
 
 class Dims:
@@ -281,8 +302,8 @@
         self.plane = 64
 
 
-def call(dims, kernel, name, out_shape, scratch, flops, limit=None):
-    limit = (limit or min(56, max(16, dims.rows // 32))) * 1024 * 1024
+def call(dims, kernel, name, out_shape, scratch, flops, out_specs=None):
+    limit = min(56, max(16, dims.rows // 32)) * 1024 * 1024
     return pl.pallas_call(
         functools.partial(kernel, dims),
         out_shape=out_shape,
@@ -290,6 +311,7 @@
         compiler_params=pltpu.CompilerParams(vmem_limit_bytes=limit),
         cost_estimate=pl.CostEstimate(flops=flops, bytes_accessed=4000000, transcendentals=0),
         name=name,
+        **({} if out_specs is None else {"out_specs": out_specs}),
     )
 
 
@@ -324,7 +346,7 @@
 
     sigma2 = swap(sigma, 1)
     picked = call(
-        dims, select_kernel, "select", shape((dims.rows, dims.width), BF16), [], 2000000000, 56
+        dims, select_kernel, "select", shape((dims.rows, dims.width), BF16), [], 2000000000
     )(roots, cols_t)
     mine = hop(picked)
     picked, sigma2 = lax.optimization_barrier((picked, sigma2))
@@ -378,7 +400,7 @@
     misfit = rinv * (modelled - value)
     misfit_mine = hop(misfit)
 
-    def add_adjoint(kernel, name, dtype, scratch, *operands):
+    def add_adjoint(kernel, name, dtype, scratch, *operands, out_specs=None):
         return call(
             dims,
             kernel,
@@ -386,6 +408,7 @@
             shape((dims.columns, dims.lanes), dtype),
             [pltpu.VMEM((dims.rows, dims.lanes), BF16)] + scratch,
             2000000000,
+            out_specs,
         )(*operands, opw)
 
     total = add_adjoint(
@@ -398,8 +421,13 @@
         side_adjoint_kernel, "mine_adjoint", F32, turned, misfit_mine, mine_plane, mine, total
     )
     misfit_other, total = lax.optimization_barrier((misfit_other, total))
+    sent = [
+        pltpu.VMEM((dims.columns, dims.lanes), BF16),
+        pltpu.SemaphoreType.DMA((dims.columns // 256,)),
+    ]
     return add_adjoint(
-        side_adjoint_kernel, "other_adjoint", BF16, turned, misfit_other, other_plane, other, total
+        last_adjoint_kernel, "other_adjoint", BF16, turned + sent,
+        misfit_other, other_plane, other, total, out_specs=pl.BlockSpec(memory_space=pl.ANY),
     )
 
 

time: 49.9 us -> 49.7 us (level)
  local copies, waits for them, and re-layouts: 1.11 us -> 5.38 us
  waiting for transfers between devices: 14.9 us -> 12.1 us
  Pallas kernels: 12.8 us -> 10.4 us
  starting transfers between devices: 20.4 us -> 20.9 us
    unnamed x24 -> x30, local copies, waits for them, and re-layouts: 0.09 us -> 4.34 us
    ppermute x4, waiting for transfers between devices: 3.37 us -> 0.57 us  [shards(): hop = lambda x: lax.ppermute(x, ('space', 'var'), partners)]
    pallas_call x1, Pallas kernels: 2.96 us -> 0.77 us  [shards(): call(dims, select_kernel, 'select', shape((dims.rows, dims.width), BF16),...]
    ppermute x4, starting transfers between devices: 11.3 us -> 11.9 us  [shards(): hop = lambda x: lax.ppermute(x, ('space', 'var'), partners)]
  transfers between devices with their start and end apart: 12 -> 12, of which waited for: 7 -> 7; matrix products, arithmetic and copies ran while one was open for 1% -> 1% of each run, Pallas kernels for 19% -> 15%
where the time goes in v6:
time: 49.7 us; the launch traced here: 49.2 us
  starting transfers between devices  20.9 us (42%)
  waiting for transfers between devices  12.1 us (24%)
  Pallas kernels  10.4 us (21%)
  local copies, waits for them, and re-layouts  5.38 us (11%)
    ppermute x4, starting transfers between devices, shards(): hop = lambda x: lax.ppermute(x, ('space', 'var'), partners)  11.9 us
    all_to_all x1, waiting for transfers between devices, shards(): lax.all_to_all(jnp.concatenate([obs_value, obs_rinv], axis=1), 'space', 0...  6.79 us
    all_to_all x1, starting transfers between devices, shards(): lax.all_to_all(jnp.concatenate([obs_value, obs_rinv], axis=1), 'space', 0...  6.34 us
    ppermute x7, waiting for transfers between devices, shards(): lax.ppermute(x, 'var', [(i, i ^ bit) for i in range(ranks)])  4.76 us
    unnamed x30, local copies, waits for them, and re-layouts  4.34 us
    pallas_call x3, Pallas kernels, add_adjoint(): call(dims, kernel, name, shape((dims.columns, dims.lanes), dtype), [pltpu...  3.97 us
    ppermute x7, starting transfers between devices, shards(): lax.ppermute(x, 'var', [(i, i ^ bit) for i in range(ranks)])  2.68 us
    pallas_call x1, Pallas kernels, shards(): call(dims, own_kernel, 'own_model', (shape((dims.slots, flat), F32), shap...  2.09 us
  transfers between devices with their start and end apart: 12, of which 7 were waited for; matrix products, arithmetic and copies ran while one was open for 1% of the time, Pallas kernels for 15%

profile of v6, /device:TPU:0, one launch (start us, length us, event | category | flops | bytes accessed | tf_op | source)
XLA Modules:
  0.0 49.2 jit_solution(12711751811399253350)
XLA Ops:
  0.5 1.3 %copy-done = bf16[8,5,128,128]{3,2,1,0:T(8,128)(2,1)S(1)} copy-done((bf16[8,5,128,128]{3,2,1,0:T(8,128)(2,1)S(1)}, bf16[8,5,128,128]{3,2,1,0:T(8,128)(2,1)}, u32[]{:S(2)}) %copy-start) | copy-done | bytes 1310744
  1.8 0.7 %copy-done.5 = s32[32,16]{0,1:T(8,128)S(1)} copy-done((s32[32,16]{0,1:T(8,128)S(1)}, s32[32,16]{0,1:T(8,128)}, u32[]{:S(2)}) %copy-start.5) | copy-done | bytes 2072
  2.5 0.8 %select.3.rows_ref = bf16[512,512]{1,0:T(8,128)(2,1)S(1)} custom-call(bf16[8,5,128,128]{3,2,1,0:T(8,128)(2,1)S(1)} %copy-done, s32[16,32]{1,0:T(8,128)S(1)} %bitcast.6), custom_call_target="tpu_custom_call" | custom-call | flops 2000000000 | bytes 4000000 | tf_op jit(solution)/shard_map/select/pallas_call | solution.py:348
  3.3 4.4 %collective-permute-start = (bf16[512,512]{1,0:T(8,128)(2,1)S(1)}, bf16[512,512]{1,0:T(8,128)(2,1)S(1)}, u32[]{:S(2)}, u32[]{:S(2)}) collective-permute-start(bf16[512,512]{1,0:T(8,128)(2,1)S(1)} %select.3.rows_ref), channel_id=1, source_target_pairs={{0,4},{2,6},{4,0},{5,9},{6,2},{7,11},{8,12},{9,5},{10,14},{11,7},{... | collective-permute-start | bytes 1572872 | tf_op jit(solution)/shard_map/ppermute | solution.py:341
  7.8 0.7 %plane.1 = (bf16[64,512]{1,0:T(8,128)(2,1)S(1)}, bf16[384,256]{1,0:T(8,128)(2,1)S(1)}) custom-call(f32[24,1024]{1,0:T(8,128)S(1)} %copy-done.3, f32[24,1024]{1,0:T(8,128)S(1)} %collective-permute-done.1.sigma2_ref, s32[16,32]{1,0:T(8,128)S(1)} %bitcast.7, f32[16,32]{1,0:T(8,128)S(1)} %bitcast.5, s32[8,5]{1,0:T(8,128)S(1)} %copy-done.7, ...), custom_call_target="tpu_custom_call" | custom-call | flops 1000000000 | bytes 4000000 | tf_op jit(solution)/shard_map/plane/pallas_call | solution.py:353
  8.5 1.9 %collective-permute-start.2 = (bf16[64,512]{1,0:T(8,128)(2,1)S(1)}, bf16[64,512]{1,0:T(8,128)(2,1)S(1)}, u32[]{:S(2)}, u32[]{:S(2)}) collective-permute-start(bf16[64,512]{1,0:T(8,128)(2,1)S(1)} %get-tuple-element.42.plane_ref), channel_id=1, source_target_pairs={{0,4},{2,6},{4,0},{5,9},{6,2},{7,11},{8,12},{9,5},{10,14},{11,7},{... | collective-permute-start | bytes 196616 | tf_op jit(solution)/shard_map/ppermute | solution.py:341
  10.7 0.6 %all_to_all.8 = f32[8,4,272]{2,1,0:T(4,128)} reshape(f32[32,272]{1,0:T(8,128)S(1)} %pad_maximum_fusion) | data formatting | bytes 69632 | tf_op jit(solution)/shard_map/all_to_all | solution.py:365
  11.3 6.3 %all-to-all-start = ((f32[8,4,272]{2,1,0:T(4,128)}), f32[8,4,272]{2,1,0:T(4,128)S(1)}, u32[]{:S(2)}, u32[]{:S(2)}) async-start(f32[8,4,272]{2,1,0:T(4,128)} %all_to_all.8), calls=%async_computation | async-start | bytes 98304 | tf_op jit(solution)/shard_map/all_to_all | solution.py:365
  17.6 6.8 %all-to-all-done = f32[8,4,272]{2,1,0:T(4,128)S(1)} async-done(((f32[8,4,272]{2,1,0:T(4,128)}), f32[8,4,272]{2,1,0:T(4,128)S(1)}, u32[]{:S(2)}, u32[]{:S(2)}) %all-to-all-start) | async-done | bytes 34848 | tf_op jit(solution)/shard_map/all_to_all | solution.py:365
  24.7 0.5 %collective-permute-start.4 = (bf16[64,512]{1,0:T(8,128)(2,1)S(1)}, bf16[64,512]{1,0:T(8,128)(2,1)S(1)}, u32[]{:S(2)}, u32[]{:S(2)}) collective-permute-start(bf16[64,512]{1,0:T(8,128)(2,1)S(1)} %collective-permute-done.2.plane_ref), channel_id=1, source_target_pairs={{0,1},{1,0},{2,3},{3,2},{4,5},{5,4},{6,7},{7,6},{8,9},{9,8},{10,11... | collective-permute-start | bytes 196616 | tf_op jit(solution)/shard_map/ppermute | solution.py:342
  25.2 1.4 %mine_model.1 = f32[32,256]{1,0:T(8,128)S(1)} custom-call(bf16[512,512]{1,0:T(8,128)(2,1)S(1)} %collective-permute-done.rows_ref, bf16[64,512]{1,0:T(8,128)(2,1)S(1)} %collective-permute-done.2.plane_ref, bf16[1024,384]{1,0:T(8,128)(2,1)S(1)} %copy-done.2, bf16[384,256]{1,0:T(8,128)(2,1)S(1)} %get-tuple-element.37.opw_ref), custom_call_target="tpu_custom_call" | custom-call | flops 2000000000 | bytes 4000000 | tf_op jit(solution)/shard_map/mine_model/pallas_call | solution.py:377
  26.7 1.4 %other_model.1 = f32[32,256]{1,0:T(8,128)S(1)} custom-call(bf16[512,512]{1,0:T(8,128)(2,1)S(1)} %collective-permute-done.3.rows_ref, bf16[64,512]{1,0:T(8,128)(2,1)S(1)} %collective-permute-done.4.plane_ref, bf16[1024,384]{1,0:T(8,128)(2,1)S(1)} %copy-done.2, bf16[384,256]{1,0:T(8,128)(2,1)S(1)} %get-tuple-element.37.opw_ref), custom_call_target="tpu_custom_call" | custom-call | flops 2000000000 | bytes 4000000 | tf_op jit(solution)/shard_map/other_model/pallas_call | solution.py:381
  28.3 1.1 %collective-permute-done.5 = f32[32,256]{1,0:T(8,128)S(1)} collective-permute-done((f32[32,256]{1,0:T(8,128)S(1)}, f32[32,256]{1,0:T(8,128)S(1)}, u32[]{:S(2)}, u32[]{:S(2)}) %collective-permute-start.5) | collective-permute-done | bytes 32800 | tf_op jit(solution)/shard_map/ppermute | solution.py:342
  29.4 2.3 %collective-permute-start.6 = (f32[32,256]{1,0:T(8,128)S(1)}, f32[32,256]{1,0:T(8,128)S(1)}, u32[]{:S(2)}, u32[]{:S(2)}) collective-permute-start(f32[32,256]{1,0:T(8,128)S(1)} %add.23), channel_id=1, source_target_pairs={{0,4},{2,6},{4,0},{5,9},{6,2},{7,11},{8,12},{9,5},{10,14},{11,7},{... | collective-permute-start | bytes 98312 | tf_op jit(solution)/shard_map/ppermute | solution.py:341
  31.8 2.1 %own_model.1 = (f32[32,256]{1,0:T(8,128)S(1)}, bf16[1024,512]{1,0:T(8,128)(2,1)S(1)}) custom-call(bf16[8,5,128,128]{3,2,1,0:T(8,128)(2,1)S(1)} %copy-done.1, s32[16,32]{1,0:T(8,128)S(1)} %bitcast.8, bf16[512,512]{1,0:T(8,128)(2,1)S(1)} %select.3.rows_ref, bf16[64,512]{1,0:T(8,128)(2,1)S(1)} %get-tuple-element.42.plane_ref, bf16[1024,384]{1,0:T(8,128)(2,1)S(1)} %copy-done.2, ...), custom_call_target="tpu_custom_call" | custom-call | flops 4000000000 | bytes 4000000 | tf_op jit(solution)/shard_map/own_model/pallas_call | solution.py:386
  33.9 1.0 %copy-done.9 = bf16[1024,512]{1,0:T(8,128)(2,1)} copy-done((bf16[1024,512]{1,0:T(8,128)(2,1)}, bf16[1024,512]{1,0:T(8,128)(2,1)S(1)}, u32[]{:S(2)}) %copy-start.9) | copy-done | bytes 1048600
  35.3 1.2 %collective-permute-done.7 = f32[32,256]{1,0:T(8,128)S(1)} collective-permute-done((f32[32,256]{1,0:T(8,128)S(1)}, f32[32,256]{1,0:T(8,128)S(1)}, u32[]{:S(2)}, u32[]{:S(2)}) %collective-permute-start.7) | collective-permute-done | bytes 32800 | tf_op jit(solution)/shard_map/ppermute | solution.py:342
  36.5 1.5 %collective-permute-start.8 = (f32[32,256]{1,0:T(8,128)S(1)}, f32[32,256]{1,0:T(8,128)S(1)}, u32[]{:S(2)}, u32[]{:S(2)}) collective-permute-start(f32[32,256]{1,0:T(8,128)S(1)} %add.25), channel_id=1, source_target_pairs={{0,2},{1,3},{2,0},{3,1},{4,6},{5,7},{6,4},{7,5},{8,10},{9,11},{10,... | collective-permute-start | bytes 98312 | tf_op jit(solution)/shard_map/ppermute | solution.py:342
  38.0 2.3 %collective-permute-done.8 = f32[32,256]{1,0:T(8,128)S(1)} collective-permute-done((f32[32,256]{1,0:T(8,128)S(1)}, f32[32,256]{1,0:T(8,128)S(1)}, u32[]{:S(2)}, u32[]{:S(2)}) %collective-permute-start.8) | collective-permute-done | bytes 32800 | tf_op jit(solution)/shard_map/ppermute | solution.py:342
  40.4 3.3 %collective-permute-start.9 = (f32[32,256]{1,0:T(8,128)S(1)}, f32[32,256]{1,0:T(8,128)S(1)}, u32[]{:S(2)}, u32[]{:S(2)}) collective-permute-start(f32[32,256]{1,0:T(8,128)S(1)} %subtract_multiply_fusion.misfit_ref), channel_id=1, source_target_pairs={{0,4},{2,6},{4,0},{5,9},{6,2},{7,11},{8,12},{9,5},{10,14},{11,7},{... | collective-permute-start | bytes 98312 | tf_op jit(solution)/shard_map/ppermute | solution.py:341
  43.7 1.2 %copy-done.10 = bf16[1024,512]{1,0:T(8,128)(2,1)S(1)} copy-done((bf16[1024,512]{1,0:T(8,128)(2,1)S(1)}, bf16[1024,512]{1,0:T(8,128)(2,1)}, u32[]{:S(2)}) %copy-start.10) | copy-done | bytes 1048600
  44.9 1.1 %own_adjoint.1.base_ref = f32[1024,384]{1,0:T(8,128)S(1)} custom-call(f32[32,256]{1,0:T(8,128)S(1)} %subtract_multiply_fusion.misfit_ref, bf16[64,512]{1,0:T(8,128)(2,1)S(1)} %get-tuple-element.42.plane_ref, bf16[1024,512]{1,0:T(8,128)(2,1)S(1)} %copy-done.10, bf16[1024,384]{1,0:T(8,128)(2,1)S(1)} %copy-done.2, bf16[384,256]{1,0:T(8,128)(2,1)S(1)} %get-tuple-element.37.opw_ref), custom_call_target="tpu_custom_call" | custom-call | flops 2000000000 | bytes 4000000 | tf_op jit(solution)/shard_map/own_adjoint/pallas_call | solution.py:404
  46.2 1.1 %mine_adjoint.1.base_ref = f32[1024,384]{1,0:T(8,128)S(1)} custom-call(f32[32,256]{1,0:T(8,128)S(1)} %collective-permute-done.9.misfit_ref, bf16[64,512]{1,0:T(8,128)(2,1)S(1)} %collective-permute-done.2.plane_ref, bf16[512,512]{1,0:T(8,128)(2,1)S(1)} %collective-permute-done.rows_ref, f32[1024,384]{1,0:T(8,128)S(1)} %own_adjoint.1.base_ref, ...), custom_call_target="tpu_custom_call" | custom-call | flops 2000000000 | bytes 4000000 | tf_op jit(solution)/shard_map/mine_adjoint/pallas_call | solution.py:404
  47.4 1.8 %other_adjoint.1 = bf16[1024,384]{1,0:T(8,128)(2,1)} custom-call(f32[32,256]{1,0:T(8,128)S(1)} %collective-permute-done.10.misfit_ref, bf16[64,512]{1,0:T(8,128)(2,1)S(1)} %collective-permute-done.4.plane_ref, bf16[512,512]{1,0:T(8,128)(2,1)S(1)} %collective-permute-done.3.rows_ref, f32[1024,384]{1,0:T(8,128)S(1)} %mine_adjoint.1.base_ref, ...), custom_call_target="tpu_custom_call" | custom-call | flops 2000000000 | bytes 4000000 | tf_op jit(solution)/shard_map/other_adjoint/pallas_call | solution.py:404
  (55 shorter events, 2.0 us)
Async XLA Ops:
  0.0 7.7 %collective-permute-start.1 = (f32[24,1024]{1,0:T(8,128)}, f32[24,1024]{1,0:T(8,128)S(1)}, u32[]{:S(2)}, u32[]{:S(2)}) collective-permute-start(f32[24,1024]{1,0:T(8,128)} %sigma_ref.1), channel_id=1, source_target_pairs={{0,1},{1,0},{2,3},{3,2},{4,5},{5,4},{6,7},{7,6},{8,9},{9,8},{10,11... | collective-permute-start | bytes 294920 | tf_op jit(solution)/shard_map/ppermute | solution.py:342
  2.5 5.2 %copy-start.3 = (f32[24,1024]{1,0:T(8,128)S(1)}, f32[24,1024]{1,0:T(8,128)}, u32[]{:S(2)}) copy-start(f32[24,1024]{1,0:T(8,128)} %sigma_ref.1) | copy-start | bytes 294916
  2.5 5.2 %copy-start.4 = (f32[32,16]{0,1:T(8,128)S(1)}, f32[32,16]{0,1:T(8,128)}, u32[]{:S(2)}) copy-start(f32[32,16]{0,1:T(8,128)} %param.16) | copy-start | bytes 6148
  2.5 5.2 %copy-start.7 = (s32[8,5]{1,0:T(8,128)S(1)}, s32[8,5]{1,0:T(8,128)}, u32[]{:S(2)}) copy-start(s32[8,5]{1,0:T(8,128)} %nb_ref.1) | copy-start | bytes 484
  2.5 5.2 %copy-start.8 = (bf16[24,16]{0,1:T(8,128)(2,1)S(1)}, bf16[24,16]{0,1:T(8,128)(2,1)}, u32[]{:S(2)}) copy-start(bf16[24,16]{0,1:T(8,128)(2,1)} %param.14) | copy-start | bytes 2308
  3.3 21.4 %collective-permute-start = (bf16[512,512]{1,0:T(8,128)(2,1)S(1)}, bf16[512,512]{1,0:T(8,128)(2,1)S(1)}, u32[]{:S(2)}, u32[]{:S(2)}) collective-permute-start(bf16[512,512]{1,0:T(8,128)(2,1)S(1)} %select.3.rows_ref), channel_id=1, source_target_pairs={{0,4},{2,6},{4,0},{5,9},{6,2},{7,11},{8,12},{9,5},{10,14},{11,7},{... | collective-permute-start | bytes 1572872 | tf_op jit(solution)/shard_map/ppermute | solution.py:341
  7.7 2.7 %copy-start.14 = (s32[1,8]{1,0:T(1,128)S(1)}, s32[1,8]{1,0:T(1,128)}, u32[]{:S(2)}) copy-start(s32[1,8]{1,0:T(1,128)} %param.19) | copy-start | bytes 100
  7.7 2.8 %copy-start.13 = (f32[32,16]{0,1:T(8,128)S(1)}, f32[32,16]{0,1:T(8,128)}, u32[]{:S(2)}) copy-start(f32[32,16]{0,1:T(8,128)} %param.18) | copy-start | bytes 6148
  7.7 2.9 %copy-start.12 = (f32[32,256]{1,0:T(8,128)S(1)}, f32[32,256]{1,0:T(8,128)}, u32[]{:S(2)}) copy-start(f32[32,256]{1,0:T(8,128)} %param.17) | copy-start | bytes 98308
  7.7 17.5 %copy-start.2 = (bf16[1024,384]{1,0:T(8,128)(2,1)S(1)}, bf16[1024,384]{1,0:T(8,128)(2,1)}, u32[]{:S(2)}) copy-start(bf16[1024,384]{1,0:T(8,128)(2,1)} %base_ref.1) | copy-start | bytes 2359300
  8.5 16.1 %collective-permute-start.2 = (bf16[64,512]{1,0:T(8,128)(2,1)S(1)}, bf16[64,512]{1,0:T(8,128)(2,1)S(1)}, u32[]{:S(2)}, u32[]{:S(2)}) collective-permute-start(bf16[64,512]{1,0:T(8,128)(2,1)S(1)} %get-tuple-element.42.plane_ref), channel_id=1, source_target_pairs={{0,4},{2,6},{4,0},{5,9},{6,2},{7,11},{8,12},{9,5},{10,14},{11,7},{... | collective-permute-start | bytes 196616 | tf_op jit(solution)/shard_map/ppermute | solution.py:341
  11.3 13.1 %all-to-all-start = ((f32[8,4,272]{2,1,0:T(4,128)}), f32[8,4,272]{2,1,0:T(4,128)S(1)}, u32[]{:S(2)}, u32[]{:S(2)}) async-start(f32[8,4,272]{2,1,0:T(4,128)} %all_to_all.8), calls=%async_computation | async-start | bytes 98304 | tf_op jit(solution)/shard_map/all_to_all | solution.py:365
  24.5 2.2 %copy-start.11 = (f32[32,272]{1,0:T(8,128)}, f32[32,272]{1,0:T(8,128)S(1)}, u32[]{:S(2)}) copy-start(f32[32,272]{1,0:T(8,128)S(1)} %all_to_all.10) | copy-start | bytes 104452
  24.6 2.1 %collective-permute-start.3 = (bf16[512,512]{1,0:T(8,128)(2,1)S(1)}, bf16[512,512]{1,0:T(8,128)(2,1)S(1)}, u32[]{:S(2)}, u32[]{:S(2)}) collective-permute-start(bf16[512,512]{1,0:T(8,128)(2,1)S(1)} %collective-permute-done.rows_ref), channel_id=1, source_target_pairs={{0,1},{1,0},{2,3},{3,2},{4,5},{5,4},{6,7},{7,6},{8,9},{9,8},{10,11... | collective-permute-start | bytes 1572872 | tf_op jit(solution)/shard_map/ppermute | solution.py:342
  24.7 2.0 %collective-permute-start.4 = (bf16[64,512]{1,0:T(8,128)(2,1)S(1)}, bf16[64,512]{1,0:T(8,128)(2,1)S(1)}, u32[]{:S(2)}, u32[]{:S(2)}) collective-permute-start(bf16[64,512]{1,0:T(8,128)(2,1)S(1)} %collective-permute-done.2.plane_ref), channel_id=1, source_target_pairs={{0,1},{1,0},{2,3},{3,2},{4,5},{5,4},{6,7},{7,6},{8,9},{9,8},{10,11... | collective-permute-start | bytes 196616 | tf_op jit(solution)/shard_map/ppermute | solution.py:342
  26.7 5.1 %copy-start.1 = (bf16[8,5,128,128]{3,2,1,0:T(8,128)(2,1)S(1)}, bf16[8,5,128,128]{3,2,1,0:T(8,128)(2,1)}, u32[]{:S(2)}) copy-start(bf16[8,5,128,128]{3,2,1,0:T(8,128)(2,1)} %roots_ref.3) | copy-start | bytes 3932164
  26.7 5.1 %copy-start.6 = (s32[32,16]{0,1:T(8,128)S(1)}, s32[32,16]{0,1:T(8,128)}, u32[]{:S(2)}) copy-start(s32[32,16]{0,1:T(8,128)} %param.15) | copy-start | bytes 6148
  28.2 1.2 %collective-permute-start.5 = (f32[32,256]{1,0:T(8,128)S(1)}, f32[32,256]{1,0:T(8,128)S(1)}, u32[]{:S(2)}, u32[]{:S(2)}) collective-permute-start(f32[32,256]{1,0:T(8,128)S(1)} %other_model.1), channel_id=1, source_target_pairs={{0,1},{1,0},{2,3},{3,2},{4,5},{5,4},{6,7},{7,6},{8,9},{9,8},{10,11... | collective-permute-start | bytes 98312 | tf_op jit(solution)/shard_map/ppermute | solution.py:342
  29.4 11.0 %slice-start = ((f32[32,272]{1,0:T(8,128)}), f32[32,256]{1,0:T(8,128)S(1)}, s32[]{:S(2)}) async-start(f32[32,272]{1,0:T(8,128)} %copy-done.11), calls=%async_computation.1 | async-start | bytes 65536 | tf_op jit(solution)/shard_map/slice | solution.py:372
  29.4 5.8 %collective-permute-start.6 = (f32[32,256]{1,0:T(8,128)S(1)}, f32[32,256]{1,0:T(8,128)S(1)}, u32[]{:S(2)}, u32[]{:S(2)}) collective-permute-start(f32[32,256]{1,0:T(8,128)S(1)} %add.23), channel_id=1, source_target_pairs={{0,4},{2,6},{4,0},{5,9},{6,2},{7,11},{8,12},{9,5},{10,14},{11,7},{... | collective-permute-start | bytes 98312 | tf_op jit(solution)/shard_map/ppermute | solution.py:341
  35.2 1.2 %collective-permute-start.7 = (f32[32,256]{1,0:T(8,128)S(1)}, f32[32,256]{1,0:T(8,128)S(1)}, u32[]{:S(2)}, u32[]{:S(2)}) collective-permute-start(f32[32,256]{1,0:T(8,128)S(1)} %add.24), channel_id=1, source_target_pairs={{0,1},{1,0},{2,3},{3,2},{4,5},{5,4},{6,7},{7,6},{8,9},{9,8},{10,11... | collective-permute-start | bytes 98312 | tf_op jit(solution)/shard_map/ppermute | solution.py:342
  36.5 3.9 %collective-permute-start.8 = (f32[32,256]{1,0:T(8,128)S(1)}, f32[32,256]{1,0:T(8,128)S(1)}, u32[]{:S(2)}, u32[]{:S(2)}) collective-permute-start(f32[32,256]{1,0:T(8,128)S(1)} %add.25), channel_id=1, source_target_pairs={{0,2},{1,3},{2,0},{3,1},{4,6},{5,7},{6,4},{7,5},{8,10},{9,11},{10,... | collective-permute-start | bytes 98312 | tf_op jit(solution)/shard_map/ppermute | solution.py:342
  40.4 5.8 %collective-permute-start.9 = (f32[32,256]{1,0:T(8,128)S(1)}, f32[32,256]{1,0:T(8,128)S(1)}, u32[]{:S(2)}, u32[]{:S(2)}) collective-permute-start(f32[32,256]{1,0:T(8,128)S(1)} %subtract_multiply_fusion.misfit_ref), channel_id=1, source_target_pairs={{0,4},{2,6},{4,0},{5,9},{6,2},{7,11},{8,12},{9,5},{10,14},{11,7},{... | collective-permute-start | bytes 98312 | tf_op jit(solution)/shard_map/ppermute | solution.py:341
  46.2 1.2 %collective-permute-start.10 = (f32[32,256]{1,0:T(8,128)S(1)}, f32[32,256]{1,0:T(8,128)S(1)}, u32[]{:S(2)}, u32[]{:S(2)}) collective-permute-start(f32[32,256]{1,0:T(8,128)S(1)} %collective-permute-done.9.misfit_ref), channel_id=1, source_target_pairs={{0,1},{1,0},{2,3},{3,2},{4,5},{5,4},{6,7},{7,6},{8,9},{9,8},{10,11... | collective-permute-start | bytes 98312 | tf_op jit(solution)/shard_map/ppermute | solution.py:342
  (4 other events, 4.3 us)

commit v7 on v6

--- a/solution.py
+++ b/solution.py
@@ -348,8 +348,8 @@
     picked = call(
         dims, select_kernel, "select", shape((dims.rows, dims.width), BF16), [], 2000000000
     )(roots, cols_t)
+    picked, sigma2 = lax.optimization_barrier((picked, sigma2))
     mine = hop(picked)
-    picked, sigma2 = lax.optimization_barrier((picked, sigma2))
     plane, opw = call(
         dims,
         plane_kernel,
@@ -371,13 +371,12 @@
     rinv = jnp.repeat(jnp.where(live[:, None], observed[:, flat:], 0.0), members, axis=1)
     value = observed[:, :flat]
 
-    mine, mine_plane, rinv, value = lax.optimization_barrier((mine, mine_plane, rinv, value))
     other, other_plane = swap(mine, 1), swap(mine_plane, 1)
     op_scratch = [pltpu.VMEM((dims.chunk, dims.columns), BF16)]
     keep = call(
         dims, side_kernel, "mine_model", shape((dims.slots, flat), F32), op_scratch, 2000000000
     )(mine, mine_plane, control, opw)
-    other, keep = lax.optimization_barrier((other, keep))
+    other, keep, rinv, value = lax.optimization_barrier((other, keep, rinv, value))
     give = call(
         dims, side_kernel, "other_model", shape((dims.slots, flat), F32), op_scratch, 2000000000
     )(other, other_plane, control, opw)

time: 49.7 us -> 49.4 us (level)
    all_to_all x1, waiting for transfers between devices: 6.79 us -> 3.46 us  [shards(): lax.all_to_all(jnp.concatenate([obs_value, obs_rinv], axis=1), 'space', 0...]
    ppermute x4, waiting for transfers between devices: 0.57 us -> 3.89 us  [shards(): hop = lambda x: lax.ppermute(x, ('space', 'var'), partners)]
  transfers between devices with their start and end apart: 12 -> 12, of which waited for: 7 -> 8; matrix products, arithmetic and copies ran while one was open for 1% -> 1% of each run, Pallas kernels for 15% -> 15%
where the time goes in v7:
time: 49.4 us; the launch traced here: 48.9 us
  starting transfers between devices  20.9 us (42%)
  waiting for transfers between devices  11.9 us (24%)
  Pallas kernels  10.4 us (21%)
  local copies, waits for them, and re-layouts  5.34 us (11%)
    ppermute x4, starting transfers between devices, shards(): hop = lambda x: lax.ppermute(x, ('space', 'var'), partners)  12 us
    all_to_all x1, starting transfers between devices, shards(): lax.all_to_all(jnp.concatenate([obs_value, obs_rinv], axis=1), 'space', 0...  6.34 us
    ppermute x7, waiting for transfers between devices, shards(): lax.ppermute(x, 'var', [(i, i ^ bit) for i in range(ranks)])  4.56 us
    unnamed x30, local copies, waits for them, and re-layouts  4.32 us
    pallas_call x3, Pallas kernels, add_adjoint(): call(dims, kernel, name, shape((dims.columns, dims.lanes), dtype), [pltpu...  3.97 us
    ppermute x4, waiting for transfers between devices, shards(): hop = lambda x: lax.ppermute(x, ('space', 'var'), partners)  3.89 us
    all_to_all x1, waiting for transfers between devices, shards(): lax.all_to_all(jnp.concatenate([obs_value, obs_rinv], axis=1), 'space', 0...  3.46 us
    ppermute x7, starting transfers between devices, shards(): lax.ppermute(x, 'var', [(i, i ^ bit) for i in range(ranks)])  2.51 us
  transfers between devices with their start and end apart: 12, of which 8 were waited for; matrix products, arithmetic and copies ran while one was open for 1% of the time, Pallas kernels for 15%

profile of v7, /device:TPU:0, one launch (start us, length us, event | category | flops | bytes accessed | tf_op | source)
XLA Modules:
  0.0 48.9 jit_solution(9383418587457750636)
XLA Ops:
  0.5 1.3 %copy-done = bf16[8,5,128,128]{3,2,1,0:T(8,128)(2,1)S(1)} copy-done((bf16[8,5,128,128]{3,2,1,0:T(8,128)(2,1)S(1)}, bf16[8,5,128,128]{3,2,1,0:T(8,128)(2,1)}, u32[]{:S(2)}) %copy-start) | copy-done | bytes 1310744
  1.8 0.7 %copy-done.5 = s32[32,16]{0,1:T(8,128)S(1)} copy-done((s32[32,16]{0,1:T(8,128)S(1)}, s32[32,16]{0,1:T(8,128)}, u32[]{:S(2)}) %copy-start.5) | copy-done | bytes 2072
  2.5 0.8 %select.3.rows_ref = bf16[512,512]{1,0:T(8,128)(2,1)S(1)} custom-call(bf16[8,5,128,128]{3,2,1,0:T(8,128)(2,1)S(1)} %copy-done, s32[16,32]{1,0:T(8,128)S(1)} %bitcast.6), custom_call_target="tpu_custom_call" | custom-call | flops 2000000000 | bytes 4000000 | tf_op jit(solution)/shard_map/select/pallas_call | solution.py:348
  3.3 4.4 %collective-permute-start.1 = (bf16[512,512]{1,0:T(8,128)(2,1)S(1)}, bf16[512,512]{1,0:T(8,128)(2,1)S(1)}, u32[]{:S(2)}, u32[]{:S(2)}) collective-permute-start(bf16[512,512]{1,0:T(8,128)(2,1)S(1)} %select.3.rows_ref), channel_id=1, source_target_pairs={{0,4},{2,6},{4,0},{5,9},{6,2},{7,11},{8,12},{9,5},{10,14},{11,7},{... | collective-permute-start | bytes 1572872 | tf_op jit(solution)/shard_map/ppermute | solution.py:341
  7.8 0.7 %plane.1 = (bf16[64,512]{1,0:T(8,128)(2,1)S(1)}, bf16[384,256]{1,0:T(8,128)(2,1)S(1)}) custom-call(f32[24,1024]{1,0:T(8,128)S(1)} %copy-done.3, f32[24,1024]{1,0:T(8,128)S(1)} %collective-permute-done.sigma2_ref, s32[16,32]{1,0:T(8,128)S(1)} %bitcast.7, f32[16,32]{1,0:T(8,128)S(1)} %bitcast.5, s32[8,5]{1,0:T(8,128)S(1)} %copy-done.7, bf16[16,24]{1,0:T(8,128)(2,1)S(1)} %bitcast.9), custom_call_target="tpu_custom_call" | custom-call | flops 1000000000 | bytes 4000000 | tf_op jit(solution)/shard_map/plane/pallas_call | solution.py:353
  8.5 1.9 %collective-permute-start.3 = (bf16[64,512]{1,0:T(8,128)(2,1)S(1)}, bf16[64,512]{1,0:T(8,128)(2,1)S(1)}, u32[]{:S(2)}, u32[]{:S(2)}) collective-permute-start(bf16[64,512]{1,0:T(8,128)(2,1)S(1)} %get-tuple-element.38.plane_ref), channel_id=1, source_target_pairs={{0,4},{2,6},{4,0},{5,9},{6,2},{7,11},{8,12},{9,5},{10,14},{11,7},{... | collective-permute-start | bytes 196616 | tf_op jit(solution)/shard_map/ppermute | solution.py:341
  10.7 0.6 %all_to_all.8 = f32[8,4,272]{2,1,0:T(4,128)} reshape(f32[32,272]{1,0:T(8,128)S(1)} %pad_maximum_fusion) | data formatting | bytes 69632 | tf_op jit(solution)/shard_map/all_to_all | solution.py:365
  11.3 6.3 %all-to-all-start = ((f32[8,4,272]{2,1,0:T(4,128)}), f32[8,4,272]{2,1,0:T(4,128)S(1)}, u32[]{:S(2)}, u32[]{:S(2)}) async-start(f32[8,4,272]{2,1,0:T(4,128)} %all_to_all.8), calls=%async_computation | async-start | bytes 98304 | tf_op jit(solution)/shard_map/all_to_all | solution.py:365
  17.6 3.3 %collective-permute-done.1.rows_ref = bf16[512,512]{1,0:T(8,128)(2,1)S(1)} collective-permute-done((bf16[512,512]{1,0:T(8,128)(2,1)S(1)}, bf16[512,512]{1,0:T(8,128)(2,1)S(1)}, u32[]{:S(2)}, u32[]{:S(2)}) %collective-permute-start.1) | collective-permute-done | bytes 524320 | tf_op jit(solution)/shard_map/ppermute | solution.py:341
  21.0 3.5 %all-to-all-done = f32[8,4,272]{2,1,0:T(4,128)S(1)} async-done(((f32[8,4,272]{2,1,0:T(4,128)}), f32[8,4,272]{2,1,0:T(4,128)S(1)}, u32[]{:S(2)}, u32[]{:S(2)}) %all-to-all-start) | async-done | bytes 34848 | tf_op jit(solution)/shard_map/all_to_all | solution.py:365
  24.7 1.4 %mine_model.1 = f32[32,256]{1,0:T(8,128)S(1)} custom-call(bf16[512,512]{1,0:T(8,128)(2,1)S(1)} %collective-permute-done.1.rows_ref, bf16[64,512]{1,0:T(8,128)(2,1)S(1)} %collective-permute-done.3.plane_ref, bf16[1024,384]{1,0:T(8,128)(2,1)S(1)} %copy-done.2, bf16[384,256]{1,0:T(8,128)(2,1)S(1)} %get-tuple-element.30.opw_ref), custom_call_target="tpu_custom_call" | custom-call | flops 2000000000 | bytes 4000000 | tf_op jit(solution)/shard_map/mine_model/pallas_call | solution.py:376
  26.2 1.4 %other_model.1 = f32[32,256]{1,0:T(8,128)S(1)} custom-call(bf16[512,512]{1,0:T(8,128)(2,1)S(1)} %collective-permute-done.2.rows_ref, bf16[64,512]{1,0:T(8,128)(2,1)S(1)} %collective-permute-done.4.plane_ref, bf16[1024,384]{1,0:T(8,128)(2,1)S(1)} %copy-done.2, bf16[384,256]{1,0:T(8,128)(2,1)S(1)} %get-tuple-element.30.opw_ref), custom_call_target="tpu_custom_call" | custom-call | flops 2000000000 | bytes 4000000 | tf_op jit(solution)/shard_map/other_model/pallas_call | solution.py:380
  28.2 0.9 %collective-permute-done.5 = f32[32,256]{1,0:T(8,128)S(1)} collective-permute-done((f32[32,256]{1,0:T(8,128)S(1)}, f32[32,256]{1,0:T(8,128)S(1)}, u32[]{:S(2)}, u32[]{:S(2)}) %collective-permute-start.5) | collective-permute-done | bytes 32800 | tf_op jit(solution)/shard_map/ppermute | solution.py:342
  29.0 2.5 %collective-permute-start.6 = (f32[32,256]{1,0:T(8,128)S(1)}, f32[32,256]{1,0:T(8,128)S(1)}, u32[]{:S(2)}, u32[]{:S(2)}) collective-permute-start(f32[32,256]{1,0:T(8,128)S(1)} %add.23), channel_id=1, source_target_pairs={{0,4},{2,6},{4,0},{5,9},{6,2},{7,11},{8,12},{9,5},{10,14},{11,7},{... | collective-permute-start | bytes 98312 | tf_op jit(solution)/shard_map/ppermute | solution.py:341
  31.5 2.1 %own_model.1 = (f32[32,256]{1,0:T(8,128)S(1)}, bf16[1024,512]{1,0:T(8,128)(2,1)S(1)}) custom-call(bf16[8,5,128,128]{3,2,1,0:T(8,128)(2,1)S(1)} %copy-done.1, s32[16,32]{1,0:T(8,128)S(1)} %bitcast.8, bf16[512,512]{1,0:T(8,128)(2,1)S(1)} %select.3.rows_ref, bf16[64,512]{1,0:T(8,128)(2,1)S(1)} %get-tuple-element.38.plane_ref, bf16[1024,384]{1,0:T(8,128)(2,1)S(1)} %copy-done.2, ...), custom_call_target="tpu_custom_call" | custom-call | flops 4000000000 | bytes 4000000 | tf_op jit(solution)/shard_map/own_model/pallas_call | solution.py:385
  33.6 1.0 %copy-done.9 = bf16[1024,512]{1,0:T(8,128)(2,1)} copy-done((bf16[1024,512]{1,0:T(8,128)(2,1)}, bf16[1024,512]{1,0:T(8,128)(2,1)S(1)}, u32[]{:S(2)}) %copy-start.9) | copy-done | bytes 1048600
  35.0 1.2 %collective-permute-done.7 = f32[32,256]{1,0:T(8,128)S(1)} collective-permute-done((f32[32,256]{1,0:T(8,128)S(1)}, f32[32,256]{1,0:T(8,128)S(1)}, u32[]{:S(2)}, u32[]{:S(2)}) %collective-permute-start.7) | collective-permute-done | bytes 32800 | tf_op jit(solution)/shard_map/ppermute | solution.py:342
  36.2 1.5 %collective-permute-start.8 = (f32[32,256]{1,0:T(8,128)S(1)}, f32[32,256]{1,0:T(8,128)S(1)}, u32[]{:S(2)}, u32[]{:S(2)}) collective-permute-start(f32[32,256]{1,0:T(8,128)S(1)} %add.25), channel_id=1, source_target_pairs={{0,2},{1,3},{2,0},{3,1},{4,6},{5,7},{6,4},{7,5},{8,10},{9,11},{10,... | collective-permute-start | bytes 98312 | tf_op jit(solution)/shard_map/ppermute | solution.py:342
  37.7 2.3 %collective-permute-done.8 = f32[32,256]{1,0:T(8,128)S(1)} collective-permute-done((f32[32,256]{1,0:T(8,128)S(1)}, f32[32,256]{1,0:T(8,128)S(1)}, u32[]{:S(2)}, u32[]{:S(2)}) %collective-permute-start.8) | collective-permute-done | bytes 32800 | tf_op jit(solution)/shard_map/ppermute | solution.py:342
  40.1 3.3 %collective-permute-start.9 = (f32[32,256]{1,0:T(8,128)S(1)}, f32[32,256]{1,0:T(8,128)S(1)}, u32[]{:S(2)}, u32[]{:S(2)}) collective-permute-start(f32[32,256]{1,0:T(8,128)S(1)} %subtract_multiply_fusion.misfit_ref), channel_id=1, source_target_pairs={{0,4},{2,6},{4,0},{5,9},{6,2},{7,11},{8,12},{9,5},{10,14},{11,7},{... | collective-permute-start | bytes 98312 | tf_op jit(solution)/shard_map/ppermute | solution.py:341
  43.4 1.2 %copy-done.10 = bf16[1024,512]{1,0:T(8,128)(2,1)S(1)} copy-done((bf16[1024,512]{1,0:T(8,128)(2,1)S(1)}, bf16[1024,512]{1,0:T(8,128)(2,1)}, u32[]{:S(2)}) %copy-start.10) | copy-done | bytes 1048600
  44.6 1.1 %own_adjoint.1.base_ref = f32[1024,384]{1,0:T(8,128)S(1)} custom-call(f32[32,256]{1,0:T(8,128)S(1)} %subtract_multiply_fusion.misfit_ref, bf16[64,512]{1,0:T(8,128)(2,1)S(1)} %get-tuple-element.38.plane_ref, bf16[1024,512]{1,0:T(8,128)(2,1)S(1)} %copy-done.10, bf16[1024,384]{1,0:T(8,128)(2,1)S(1)} %copy-done.2, bf16[384,256]{1,0:T(8,128)(2,1)S(1)} %get-tuple-element.30.opw_ref), custom_call_target="tpu_custom_call" | custom-call | flops 2000000000 | bytes 4000000 | tf_op jit(solution)/shard_map/own_adjoint/pallas_call | solution.py:403
  45.9 1.1 %mine_adjoint.1.base_ref = f32[1024,384]{1,0:T(8,128)S(1)} custom-call(f32[32,256]{1,0:T(8,128)S(1)} %collective-permute-done.9.misfit_ref, bf16[64,512]{1,0:T(8,128)(2,1)S(1)} %collective-permute-done.3.plane_ref, bf16[512,512]{1,0:T(8,128)(2,1)S(1)} %collective-permute-done.1.rows_ref, f32[1024,384]{1,0:T(8,128)S(1)} %own_adjoint.1.base_ref, ...), custom_call_target="tpu_custom_call" | custom-call | flops 2000000000 | bytes 4000000 | tf_op jit(solution)/shard_map/mine_adjoint/pallas_call | solution.py:403
  47.1 1.8 %other_adjoint.1 = bf16[1024,384]{1,0:T(8,128)(2,1)} custom-call(f32[32,256]{1,0:T(8,128)S(1)} %collective-permute-done.10.misfit_ref, bf16[64,512]{1,0:T(8,128)(2,1)S(1)} %collective-permute-done.4.plane_ref, bf16[512,512]{1,0:T(8,128)(2,1)S(1)} %collective-permute-done.2.rows_ref, f32[1024,384]{1,0:T(8,128)S(1)} %mine_adjoint.1.base_ref, ...), custom_call_target="tpu_custom_call" | custom-call | flops 2000000000 | bytes 4000000 | tf_op jit(solution)/shard_map/other_adjoint/pallas_call | solution.py:403
  (55 shorter events, 2.3 us)
Async XLA Ops:
  0.0 3.3 %collective-permute-start = (f32[24,1024]{1,0:T(8,128)}, f32[24,1024]{1,0:T(8,128)S(1)}, u32[]{:S(2)}, u32[]{:S(2)}) collective-permute-start(f32[24,1024]{1,0:T(8,128)} %sigma_ref.1), channel_id=1, source_target_pairs={{0,1},{1,0},{2,3},{3,2},{4,5},{5,4},{6,7},{7,6},{8,9},{9,8},{10,11... | collective-permute-start | bytes 294920 | tf_op jit(solution)/shard_map/ppermute | solution.py:342
  2.5 5.2 %copy-start.3 = (f32[24,1024]{1,0:T(8,128)S(1)}, f32[24,1024]{1,0:T(8,128)}, u32[]{:S(2)}) copy-start(f32[24,1024]{1,0:T(8,128)} %sigma_ref.1) | copy-start | bytes 294916
  2.5 5.2 %copy-start.4 = (f32[32,16]{0,1:T(8,128)S(1)}, f32[32,16]{0,1:T(8,128)}, u32[]{:S(2)}) copy-start(f32[32,16]{0,1:T(8,128)} %param.16) | copy-start | bytes 6148
  2.5 5.2 %copy-start.7 = (s32[8,5]{1,0:T(8,128)S(1)}, s32[8,5]{1,0:T(8,128)}, u32[]{:S(2)}) copy-start(s32[8,5]{1,0:T(8,128)} %nb_ref.1) | copy-start | bytes 484
  2.5 5.2 %copy-start.8 = (bf16[24,16]{0,1:T(8,128)(2,1)S(1)}, bf16[24,16]{0,1:T(8,128)(2,1)}, u32[]{:S(2)}) copy-start(bf16[24,16]{0,1:T(8,128)(2,1)} %param.14) | copy-start | bytes 2308
  3.3 17.7 %collective-permute-start.1 = (bf16[512,512]{1,0:T(8,128)(2,1)S(1)}, bf16[512,512]{1,0:T(8,128)(2,1)S(1)}, u32[]{:S(2)}, u32[]{:S(2)}) collective-permute-start(bf16[512,512]{1,0:T(8,128)(2,1)S(1)} %select.3.rows_ref), channel_id=1, source_target_pairs={{0,4},{2,6},{4,0},{5,9},{6,2},{7,11},{8,12},{9,5},{10,14},{11,7},{... | collective-permute-start | bytes 1572872 | tf_op jit(solution)/shard_map/ppermute | solution.py:341
  7.7 2.7 %copy-start.14 = (s32[1,8]{1,0:T(1,128)S(1)}, s32[1,8]{1,0:T(1,128)}, u32[]{:S(2)}) copy-start(s32[1,8]{1,0:T(1,128)} %param.19) | copy-start | bytes 100
  7.7 2.8 %copy-start.13 = (f32[32,16]{0,1:T(8,128)S(1)}, f32[32,16]{0,1:T(8,128)}, u32[]{:S(2)}) copy-start(f32[32,16]{0,1:T(8,128)} %param.18) | copy-start | bytes 6148
  7.7 2.9 %copy-start.12 = (f32[32,256]{1,0:T(8,128)S(1)}, f32[32,256]{1,0:T(8,128)}, u32[]{:S(2)}) copy-start(f32[32,256]{1,0:T(8,128)} %param.17) | copy-start | bytes 98308
  7.7 16.9 %copy-start.2 = (bf16[1024,384]{1,0:T(8,128)(2,1)S(1)}, bf16[1024,384]{1,0:T(8,128)(2,1)}, u32[]{:S(2)}) copy-start(bf16[1024,384]{1,0:T(8,128)(2,1)} %base_ref.1) | copy-start | bytes 2359300
  8.5 16.1 %collective-permute-start.3 = (bf16[64,512]{1,0:T(8,128)(2,1)S(1)}, bf16[64,512]{1,0:T(8,128)(2,1)S(1)}, u32[]{:S(2)}, u32[]{:S(2)}) collective-permute-start(bf16[64,512]{1,0:T(8,128)(2,1)S(1)} %get-tuple-element.38.plane_ref), channel_id=1, source_target_pairs={{0,4},{2,6},{4,0},{5,9},{6,2},{7,11},{8,12},{9,5},{10,14},{11,7},{... | collective-permute-start | bytes 196616 | tf_op jit(solution)/shard_map/ppermute | solution.py:341
  11.3 13.1 %all-to-all-start = ((f32[8,4,272]{2,1,0:T(4,128)}), f32[8,4,272]{2,1,0:T(4,128)S(1)}, u32[]{:S(2)}, u32[]{:S(2)}) async-start(f32[8,4,272]{2,1,0:T(4,128)} %all_to_all.8), calls=%async_computation | async-start | bytes 98304 | tf_op jit(solution)/shard_map/all_to_all | solution.py:365
  21.0 5.2 %collective-permute-start.2 = (bf16[512,512]{1,0:T(8,128)(2,1)S(1)}, bf16[512,512]{1,0:T(8,128)(2,1)S(1)}, u32[]{:S(2)}, u32[]{:S(2)}) collective-permute-start(bf16[512,512]{1,0:T(8,128)(2,1)S(1)} %collective-permute-done.1.rows_ref), channel_id=1, source_target_pairs={{0,1},{1,0},{2,3},{3,2},{4,5},{5,4},{6,7},{7,6},{8,9},{9,8},{10,11... | collective-permute-start | bytes 1572872 | tf_op jit(solution)/shard_map/ppermute | solution.py:342
  24.5 1.6 %copy-start.11 = (f32[32,272]{1,0:T(8,128)}, f32[32,272]{1,0:T(8,128)S(1)}, u32[]{:S(2)}) copy-start(f32[32,272]{1,0:T(8,128)S(1)} %all_to_all.10) | copy-start | bytes 104452
  24.6 1.6 %collective-permute-start.4 = (bf16[64,512]{1,0:T(8,128)(2,1)S(1)}, bf16[64,512]{1,0:T(8,128)(2,1)S(1)}, u32[]{:S(2)}, u32[]{:S(2)}) collective-permute-start(bf16[64,512]{1,0:T(8,128)(2,1)S(1)} %collective-permute-done.3.plane_ref), channel_id=1, source_target_pairs={{0,1},{1,0},{2,3},{3,2},{4,5},{5,4},{6,7},{7,6},{8,9},{9,8},{10,11... | collective-permute-start | bytes 196616 | tf_op jit(solution)/shard_map/ppermute | solution.py:342
  26.2 5.3 %copy-start.1 = (bf16[8,5,128,128]{3,2,1,0:T(8,128)(2,1)S(1)}, bf16[8,5,128,128]{3,2,1,0:T(8,128)(2,1)}, u32[]{:S(2)}) copy-start(bf16[8,5,128,128]{3,2,1,0:T(8,128)(2,1)} %roots_ref.3) | copy-start | bytes 3932164
  26.2 5.3 %copy-start.6 = (s32[32,16]{0,1:T(8,128)S(1)}, s32[32,16]{0,1:T(8,128)}, u32[]{:S(2)}) copy-start(s32[32,16]{0,1:T(8,128)} %param.15) | copy-start | bytes 6148
  27.6 1.4 %collective-permute-start.5 = (f32[32,256]{1,0:T(8,128)S(1)}, f32[32,256]{1,0:T(8,128)S(1)}, u32[]{:S(2)}, u32[]{:S(2)}) collective-permute-start(f32[32,256]{1,0:T(8,128)S(1)} %other_model.1), channel_id=1, source_target_pairs={{0,1},{1,0},{2,3},{3,2},{4,5},{5,4},{6,7},{7,6},{8,9},{9,8},{10,11... | collective-permute-start | bytes 98312 | tf_op jit(solution)/shard_map/ppermute | solution.py:342
  29.0 11.1 %slice-start = ((f32[32,272]{1,0:T(8,128)}), f32[32,256]{1,0:T(8,128)S(1)}, s32[]{:S(2)}) async-start(f32[32,272]{1,0:T(8,128)} %copy-done.11), calls=%async_computation.1 | async-start | bytes 65536 | tf_op jit(solution)/shard_map/slice | solution.py:372
  29.0 5.9 %collective-permute-start.6 = (f32[32,256]{1,0:T(8,128)S(1)}, f32[32,256]{1,0:T(8,128)S(1)}, u32[]{:S(2)}, u32[]{:S(2)}) collective-permute-start(f32[32,256]{1,0:T(8,128)S(1)} %add.23), channel_id=1, source_target_pairs={{0,4},{2,6},{4,0},{5,9},{6,2},{7,11},{8,12},{9,5},{10,14},{11,7},{... | collective-permute-start | bytes 98312 | tf_op jit(solution)/shard_map/ppermute | solution.py:341
  35.0 1.2 %collective-permute-start.7 = (f32[32,256]{1,0:T(8,128)S(1)}, f32[32,256]{1,0:T(8,128)S(1)}, u32[]{:S(2)}, u32[]{:S(2)}) collective-permute-start(f32[32,256]{1,0:T(8,128)S(1)} %add.24), channel_id=1, source_target_pairs={{0,1},{1,0},{2,3},{3,2},{4,5},{5,4},{6,7},{7,6},{8,9},{9,8},{10,11... | collective-permute-start | bytes 98312 | tf_op jit(solution)/shard_map/ppermute | solution.py:342
  36.2 3.9 %collective-permute-start.8 = (f32[32,256]{1,0:T(8,128)S(1)}, f32[32,256]{1,0:T(8,128)S(1)}, u32[]{:S(2)}, u32[]{:S(2)}) collective-permute-start(f32[32,256]{1,0:T(8,128)S(1)} %add.25), channel_id=1, source_target_pairs={{0,2},{1,3},{2,0},{3,1},{4,6},{5,7},{6,4},{7,5},{8,10},{9,11},{10,... | collective-permute-start | bytes 98312 | tf_op jit(solution)/shard_map/ppermute | solution.py:342
  40.1 5.8 %collective-permute-start.9 = (f32[32,256]{1,0:T(8,128)S(1)}, f32[32,256]{1,0:T(8,128)S(1)}, u32[]{:S(2)}, u32[]{:S(2)}) collective-permute-start(f32[32,256]{1,0:T(8,128)S(1)} %subtract_multiply_fusion.misfit_ref), channel_id=1, source_target_pairs={{0,4},{2,6},{4,0},{5,9},{6,2},{7,11},{8,12},{9,5},{10,14},{11,7},{... | collective-permute-start | bytes 98312 | tf_op jit(solution)/shard_map/ppermute | solution.py:341
  45.9 1.2 %collective-permute-start.10 = (f32[32,256]{1,0:T(8,128)S(1)}, f32[32,256]{1,0:T(8,128)S(1)}, u32[]{:S(2)}, u32[]{:S(2)}) collective-permute-start(f32[32,256]{1,0:T(8,128)S(1)} %collective-permute-done.9.misfit_ref), channel_id=1, source_target_pairs={{0,1},{1,0},{2,3},{3,2},{4,5},{5,4},{6,7},{7,6},{8,9},{9,8},{10,11... | collective-permute-start | bytes 98312 | tf_op jit(solution)/shard_map/ppermute | solution.py:342
  (4 other events, 4.3 us)
